TPU v7x, 128 devices: a whole 4x4x4 slice. The times are simulated.
128 devices in a mesh: dp: 8 (over z, y_lo), space: 16 (over y_hi, x, core).
Axes of the slice: x: 4, y: 4 (y_hi: 2, y_lo: 2; y = y_hi * 2 + y_lo), z: 4, core: 2. Of those that a mesh axis runs over, the one named last changes fastest.
Arguments:
- activation: bfloat16 [8, 16, 64, 128, 128], P('dp', None, 'space'), may hold values from -6 to 6
- cotangent: bfloat16 [8, 16, 64, 128, 128], P('dp', None, 'space'), may hold values from -6 to 6
- volume: bfloat16 [8, 1, 64, 128, 128], P('dp', None, 'space'), may hold values from -6 to 6
- dec_weight: bfloat16 [27, 16, 16], replicated, may hold values from -0.3125 to 0.3125
- enc_grad: float32 [8, 16, 7376], P('dp', 'space'), may hold values from -6 to 6
- params: float32 [14288], P('dp'), may hold values from -0.6 to 0.6
- moment: float32 [14288], P('dp'), may hold values from -0.3 to 0.3
- second: float32 [14288], P('dp'), may hold values from 0.001 to 0.004
Outputs:
- grad_input: bfloat16 [8, 16, 64, 128, 128], P('dp', None, 'space')
- new_params: float32 [14288], P('dp')
- new_moment: float32 [14288], P('dp')
- new_second: float32 [14288], P('dp')
- working: bfloat16 [14288], replicated
- encoded: bfloat16 [8, 16, 64, 128, 128], P('dp', None, 'space')
All inputs are finite; a program needn't handle non-finite values.
Results may differ from a plain program's by a relative error of at most 0.0073.
Values may be sent and summed in bfloat16 or wider, within the bound.
No kernel may reach another device: no remote copies, remote signals or barrier semaphores. Data moves between devices by JAX's collectives and lax.ppermute only.
A program may use at most 256 MiB of HBM per device.

v0:
```python
import math

import jax
import jax.numpy as jnp
from jax import lax
from jax.sharding import PartitionSpec as P


def padded_2(cells, sides, width):
    for axis, dim in sides:
        count = lax.axis_size(axis)
        ends = count - 1
        head = lax.slice_in_dim(cells, 0, width, axis=dim)
        tail = lax.slice_in_dim(cells, cells.shape[dim] - width, cells.shape[dim], axis=dim)
        cells = jnp.concatenate(
            [
                lax.ppermute(tail, axis, [(i, (i + 1) % count) for i in range(ends)]),
                cells,
                lax.ppermute(head, axis, [((i + 1) % count, i) for i in range(ends)]),
            ],
            axis=dim,
        )
    return cells


def lateral_stack(padded_in):
    height = padded_in.shape[2]
    columns = padded_in.shape[3]
    spread = jnp.pad(padded_in, ((0, 0), (0, 0), (1, 1), (1, 1)))
    return jnp.concatenate(
        [
            spread[:, :, row_off : row_off + height, col_off : col_off + columns]
            for row_off in range(3)
            for col_off in range(3)
        ],
        axis=0,
    )


def convolve(padded_in, weight):
    stacked = lateral_stack(padded_in)
    planes = padded_in.shape[1] - 2
    kernels = weight.reshape(3, 9 * weight.shape[1], weight.shape[2])
    summed = jnp.zeros(
        (weight.shape[2], planes, padded_in.shape[2], padded_in.shape[3]), jnp.float32
    )
    for depth_off in range(3):
        summed = summed + jnp.einsum(
            "ko,kdhw->odhw",
            kernels[depth_off],
            stacked[:, depth_off : depth_off + planes],
            preferred_element_type=jnp.float32,
        )
    return summed


def correlate(padded_in, cotan):
    stacked = lateral_stack(padded_in)
    planes = padded_in.shape[1] - 2
    pieces = [
        jnp.einsum(
            "kdhw,odhw->ko",
            stacked[:, depth_off : depth_off + planes],
            cotan,
            preferred_element_type=jnp.float32,
        )
        for depth_off in range(3)
    ]
    return jnp.stack(pieces).reshape(27, padded_in.shape[0], cotan.shape[0])


def local(activation, cotangent, volume, dec_weight, enc_grad, params, moment, second):
    channels = activation.shape[1]
    planes = activation.shape[2]
    joined = jnp.concatenate([activation[0], cotangent[0]], axis=0)
    padded = padded_2(joined, (("space", 1),), 1)
    input_rim = padded[:channels]
    cotan_padded = padded[channels:]
    weight_grad = correlate(input_rim, cotangent[0])
    flipped = dec_weight[::-1].transpose(0, 2, 1)
    grad_input = convolve(cotan_padded, flipped).astype(jnp.bfloat16)[None]
    devices = lax.axis_size("dp") * lax.axis_size("space")
    voxels = devices * planes * activation.shape[3] * activation.shape[4]
    partial_grad = jnp.concatenate(
        [weight_grad.reshape(-1) / math.sqrt(voxels), enc_grad[0, 0] / math.sqrt(devices)]
    )
    summed_all = lax.psum(partial_grad, "space")
    gradient = lax.psum_scatter(summed_all, "dp", scatter_dimension=0, tiled=True)
    new_moment = 0.9 * moment + 0.1 * gradient
    new_second = 0.999 * second + 0.001 * gradient * gradient
    new_params = params - 0.01 * new_moment / (jnp.sqrt(new_second) + 1e-08)
    working = lax.all_gather(new_params.astype(jnp.bfloat16), "dp", axis=0, tiled=True)
    offset = 27 * channels * channels
    weight_one = working[offset : offset + 27 * channels].reshape(27, 1, channels)
    offset = offset + 27 * channels
    bias_one = working[offset : offset + channels].astype(jnp.float32)[:, None, None, None]
    offset = offset + channels
    weight_two = working[offset : offset + 27 * channels * channels].reshape(27, channels, channels)
    offset = offset + 27 * channels * channels
    bias_two = working[offset : offset + channels].astype(jnp.float32)[:, None, None, None]
    volume_pad = padded_2(volume[0], (("space", 1),), 1)
    first = jax.nn.relu(convolve(volume_pad, weight_one) + bias_one).astype(jnp.bfloat16)
    first_rim = padded_2(first, (("space", 1),), 1)
    encoded = jax.nn.relu(convolve(first_rim, weight_two) + bias_two).astype(jnp.bfloat16)[None]
    return (grad_input, new_params, new_moment, new_second, working, encoded)


def solution(mesh):
    in_specs = (
        P("dp", None, "space", None, None),
        P("dp", None, "space", None, None),
        P("dp", None, "space", None, None),
        P(),
        P("dp", "space", None),
        P("dp"),
        P("dp"),
        P("dp"),
    )
    out_specs = (
        P("dp", None, "space", None, None),
        P("dp"),
        P("dp"),
        P("dp"),
        P(),
        P("dp", None, "space", None, None),
    )
    return jax.shard_map(local, mesh=mesh, in_specs=in_specs, out_specs=out_specs, check_vma=False)
```

profile of v0, /device:TPU:16, one launch (start us, length us, event | category | flops | bytes accessed | tf_op | source)
XLA Modules:
  0.0 336.0 jit_solution(17022091541136885667)
XLA Ops:
  0.7 5.0 %copy_bitcast_fusion = (bf16[16,4,128,128]{3,0,2,1:T(8,128)(2,1)S(1)}, bf16[16,4,128,128]{3,0,2,1:T(8,128)(2,1)S(1)}) fusion(bf16[1,16,4,128,128]{4,3,2,1,0:T(8,128)(2,1)} %param.9, bf16[1,16,4,128,128]{4,3,2,1,0:T(8,128)(2,1)} %param.8), kind=kLoop, calls=%fused_computation.66 | loop fusion | bytes 8388608 | tf_op jit(solution)/shard_map/squeeze | solution.py:75
  10.6 7.3 %collective-permute-start.1 = (bf16[32,1,128,128]{3,0,2,1:T(8,128)(2,1)}, bf16[32,1,128,128]{3,0,2,1:T(8,128)(2,1)}, u32[]{:S(2)}, u32[]{:S(2)}) collective-permute-start(bf16[32,1,128,128]{3,0,2,1:T(8,128)(2,1)} %get-tuple-element.33), channel_id=1, source_target_pairs={{1,0},{2,1},{3,2},{4,3},{5,4},{6,5},{7,6},{8,7},{9,8},{10,9},{11,1... | collective-permute-start | bytes 3145736 | tf_op jit(solution)/shard_map/ppermute | solution.py:19
  19.9 7.3 %collective-permute-start.3 = (bf16[1,1,128,128]{3,0,2,1:T(2,128)(2,1)S(1)}, bf16[1,1,128,128]{3,0,2,1:T(2,128)(2,1)S(1)}, u32[]{:S(2)}, u32[]{:S(2)}) collective-permute-start(bf16[1,1,128,128]{3,0,2,1:T(2,128)(2,1)S(1)} %copy.89), channel_id=1, source_target_pairs={{1,0},{2,1},{3,2},{4,3},{5,4},{6,5},{7,6},{8,7},{9,8},{10,9},{11,1... | collective-permute-start | bytes 98312 | tf_op jit(solution)/shard_map/ppermute | solution.py:19
  31.2 4.7 %pad_slice_fusion.24 = (bf16[1,6,128,128]{3,0,2,1:T(2,128)(2,1)S(1)}, bf16[1,6,128,128]{3,0,2,1:T(2,128)(2,1)S(1)}, bf16[1,6,128,128]{3,0,2,1:T(2,128)(2,1)}, bf...) fusion(bf16[1,6,128,128]{3,0,2,1:T(2,128)(2,1)S(1)} %constant_d, ...), kind=kLoop, calls=%fused_computation.95 | loop fusion | bytes 1769472 | tf_op jit(solution)/shard_map/slice | solution.py:32
  35.9 13.2 %concatenate.33 = bf16[9,6,128,128]{3,0,2,1:T(8,128)(2,1)} concatenate(bf16[1,6,128,128]{3,0,2,1:T(2,128)(2,1)} %get-tuple-element.43, bf16[1,6,128,128]{3,0,2,1:T(2,128)(2,1)S(1)} %get-tuple-element.37, bf16[1,6,128,128]{3,0,2,1:T(2,128)(2,1)} %get-tuple-element.38, bf16[1,6,128,128]{3,0,2,1:T(2,128)(2,1)} %get-tuple-element.39, ...), dimensions={0} | concatenate | bytes 3538944 | tf_op jit(solution)/shard_map/concatenate | solution.py:30
  49.1 4.0 %pad_maximum_fusion = bf16[32,6,128,128]{3,0,2,1:T(8,128)(2,1)S(1)} fusion(bf16[32,1,128,128]{3,0,2,1:T(8,128)(2,1)} %collective-permute-done.1, bf16[16,4,128,128]{3,0,2,1:T(8,128)(2,1)S(1)} %get-tuple-element.59, bf16[16,4,128,128]{3,0,2,1:T(8,128)(2,1)} %copy-done.4, bf16[32,1,128,128]{3,0,2,1:T(8,128)(2,1)} %collective-permute-done), kind=kLoop, calls=%fused_computation.30 | loop fusion | flops 25165824 | bytes 12582912 | tf_op jit(solution)/shard_map/concatenate | solution.py:15
  59.5 2.8 fusion.8
  62.3 2.8 fusion.9
  72.8 2.8 fusion.17
  75.6 4.3 %constant_dynamic-update-slice_fusion.1 = (bf16[144,6,128,128]{3,0,2,1:T(8,128)(2,1)}, bf16[144,6,128,128]{3,0,2,1:T(8,128)(2,1)}) fusion(bf16[144,6,128,128]{3,0,2,1:T(8,128)(2,1)} %fusion.17, bf16[32,6,128,128]{3,0,2,1:T(8,128)(2,1)S(1)} %pad_maximum_fusion, bf16[144,6,128,128]{3,0,2,1:T(8,128)(2,1)} %fusion.9), kind=kLoop, calls=%fused_computation.75 | loop fusion | bytes 12582912
  87.7 2.9 fusion.21
  90.6 8.9 %convolution_bitcast_fusion = f32[1,144,16]{1,2,0:T(8,128)S(1)} fusion(bf16[144,6,128,128]{3,0,2,1:T(8,128)(2,1)} %fusion.21, bf16[1,16,4,128,128]{4,3,2,1,0:T(8,128)(2,1)S(1)} %copy-done), kind=kOutput, calls=%fused_computation.69 | convolution fusion | flops 301989888 | bytes 30417920 | tf_op jit(solution)/shard_map/kdhw,odhw->ko/dot_general | solution.py:61
  99.5 8.9 %convolution_bitcast_fusion.1 = f32[1,144,16]{1,2,0:T(8,128)S(1)} fusion(bf16[144,6,128,128]{3,0,2,1:T(8,128)(2,1)} %fusion.21, bf16[1,16,4,128,128]{4,3,2,1,0:T(8,128)(2,1)S(1)} %copy-done), kind=kOutput, calls=%fused_computation.70 | convolution fusion | flops 301989888 | bytes 30417920 | tf_op jit(solution)/shard_map/kdhw,odhw->ko/dot_general | solution.py:61
  108.4 8.9 %convolution_bitcast_fusion.2 = f32[1,144,16]{1,2,0:T(8,128)S(1)} fusion(bf16[144,6,128,128]{3,0,2,1:T(8,128)(2,1)} %fusion.21, bf16[1,16,4,128,128]{4,3,2,1,0:T(8,128)(2,1)S(1)} %copy-done), kind=kOutput, calls=%fused_computation.71 | convolution fusion | flops 301989888 | bytes 30417920 | tf_op jit(solution)/shard_map/kdhw,odhw->ko/dot_general | solution.py:61
  118.4 36.1 %all-reduce.5 = f32[14288]{0:T(1024)S(1)} all-reduce(f32[14288]{0:T(1024)S(1)} %pad_maximum_fusion.4), channel_id=2, replica_groups=mesh['dp'=8,'space'=16] {'dp'}, use_global_device_ids=true, to_apply=%region_1.2.clone | all-reduce | flops 14288 | bytes 114304
  154.6 33.7 %psum.8 = f32[1786]{0:T(1024)S(1)} all-reduce(f32[1786]{0:T(1024)S(1)} %dynamic-slice.2), channel_id=1, replica_groups=mesh['dp'=8,'space'=16] {'space'}, use_global_device_ids=true, to_apply=%region_0.1 | all-reduce | flops 1786 | bytes 14288 | tf_op jit(solution)/shard_map/psum | solution.py:87
  189.1 30.9 %all-reduce.4 = bf16[14288]{0:T(1024)(128)(2,1)S(1)} all-reduce(bf16[14288]{0:T(1024)(128)(2,1)S(1)} %dynamic-update-slice), channel_id=1, replica_groups=mesh['dp'=8,'space'=16] {'dp'}, use_global_device_ids=true, to_apply=%add.4 | all-reduce | flops 14288 | bytes 57152
  220.3 4.5 %fusion.35 = f32[16,4,128,128]{3,0,2,1:T(8,128)} fusion(bf16[9,6,128,128]{3,0,2,1:T(8,128)(2,1)} %concatenate.33, bf16[9,16]{1,0:T(8,128)(2,1)S(1)} %slice.321), kind=kOutput, calls=%fused_computation.62 | convolution fusion | flops 18874368 | bytes 6291744 | tf_op jit(solution)/shard_map/ko,kdhw->odhw/dot_general | solution.py:48
  227.6 5.0 %maximum_convert_fusion.1 = bf16[16,4,128,128]{3,0,2,1:T(8,128)(2,1)S(1)} fusion(f32[16,4,128,128]{3,0,2,1:T(8,128)} %fusion.37, f32[16,4,128,128]{3,0,2,1:T(8,128)} %fusion.35, bf16[9,6,128,128]{3,0,2,1:T(8,128)(2,1)} %concatenate.33, f32[16]{0:T(128)S(1)} %get-tuple-element.53, bf16[9,16]{1,0:T(8,128)(2,1)S(1)} %slice.324), kind=kOutput, calls=%fused_computation.32 | convolution fusion | flops 24117248 | bytes 12583264 | tf_op jit(solution)/shard_map/ko,kdhw->odhw/dot_general | solution.py:48
  235.8 7.3 %collective-permute-start.5 = (bf16[16,1,128,128]{3,0,2,1:T(8,128)(2,1)}, bf16[16,1,128,128]{3,0,2,1:T(8,128)(2,1)}, u32[]{:S(2)}, u32[]{:S(2)}) collective-permute-start(bf16[16,1,128,128]{3,0,2,1:T(8,128)(2,1)} %get-tuple-element.35), channel_id=1, source_target_pairs={{1,0},{2,1},{3,2},{4,3},{5,4},{6,5},{7,6},{8,7},{9,8},{10,9},{11,1... | collective-permute-start | bytes 1572872 | tf_op jit(solution)/shard_map/ppermute | solution.py:19
  250.7 2.8 fusion.13
  253.5 7.8 %fusion.58 = f32[4,128,128,16]{2,3,1,0:T(8,128)S(1)} fusion(bf16[144,6,128,128]{3,0,2,1:T(8,128)(2,1)} %fusion.13, bf16[144,16,1,1]{1,0,3,2:T(8,128)(2,1)S(1)} %bitcast.74), kind=kOutput, calls=%fused_computation.111 | convolution fusion | flops 301989888 | bytes 32510464 | tf_op jit(solution)/shard_map/ko,kdhw->odhw/dot_general | solution.py:48
  261.3 8.0 %fusion.59 = f32[4,128,128,16]{2,3,1,0:T(8,128)S(1)} fusion(bf16[144,6,128,128]{3,0,2,1:T(8,128)(2,1)} %fusion.13, bf16[144,16,1,1]{1,0,3,2:T(8,128)(2,1)S(1)} %bitcast.75), kind=kOutput, calls=%fused_computation.112 | convolution fusion | flops 301989888 | bytes 32510464 | tf_op jit(solution)/shard_map/ko,kdhw->odhw/dot_general | solution.py:48
  269.3 10.8 %fusion.41 = bf16[1,16,4,128,128]{4,1,3,2,0:T(8,128)(2,1)} fusion(bf16[144,6,128,128]{3,0,2,1:T(8,128)(2,1)} %fusion.13, bf16[144,16,1,1]{1,0,3,2:T(8,128)(2,1)S(1)} %bitcast.76, f32[4,128,128,16]{2,3,1,0:T(8,128)S(1)} %fusion.58, f32[4,128,128,16]{2,3,1,0:T(8,128)S(1)} %fusion.59), kind=kOutput, calls=%fused_computation.68 | convolution fusion | flops 305135616 | bytes 38801920 | tf_op jit(solution)/shard_map/ko,kdhw->odhw/dot_general | solution.py:48
  280.5 3.5 %copy.59 = bf16[1,16,4,128,128]{4,3,2,1,0:T(8,128)(2,1)} copy(bf16[1,16,4,128,128]{4,1,3,2,0:T(8,128)(2,1)} %fusion.41) | data formatting | bytes 4194304
  290.6 2.8 fusion.24
  293.3 2.8 fusion.25
  296.1 3.6 %constant_dynamic-update-slice_fusion.5 = bf16[144,6,128,128]{3,0,2,1:T(8,128)(2,1)} fusion(bf16[144,6,128,128]{3,0,2,1:T(8,128)(2,1)} %fusion.25, bf16[16,1,128,128]{3,0,2,1:T(8,128)(2,1)} %collective-permute-done.5, bf16[16,4,128,128]{3,0,2,1:T(8,128)(2,1)S(1)} %copy-done.3, bf16[16,1,128,128]{3,0,2,1:T(8,128)(2,1)} %collective-permute-done.4), kind=kLoop, calls=%fused_computation.79 | loop fusion | flops 9437184 | bytes 6291456
  307.4 2.8 fusion.29
  310.2 7.7 %fusion.2 = f32[16,4,128,128]{3,0,2,1:T(8,128)S(1)} fusion(bf16[144,6,128,128]{3,0,2,1:T(8,128)(2,1)} %fusion.29, bf16[144,16]{1,0:T(8,128)(2,1)S(1)} %slice.339), kind=kOutput, calls=%fused_computation.2 | convolution fusion | flops 301989888 | bytes 23073280 | tf_op jit(solution)/shard_map/ko,kdhw->odhw/dot_general | solution.py:48
  317.9 8.0 %fusion.4 = f32[16,4,128,128]{3,0,2,1:T(8,128)S(1)} fusion(bf16[144,6,128,128]{3,0,2,1:T(8,128)(2,1)} %fusion.29, bf16[144,16]{1,0:T(8,128)(2,1)S(1)} %slice.306), kind=kOutput, calls=%fused_computation.4 | convolution fusion | flops 301989888 | bytes 23073280 | tf_op jit(solution)/shard_map/ko,kdhw->odhw/dot_general | solution.py:48
  326.0 7.8 %fusion.30 = bf16[1,16,4,128,128]{4,1,3,2,0:T(8,128)(2,1)S(1)} fusion(f32[16,4,128,128]{3,0,2,1:T(8,128)S(1)} %fusion.4, f32[16,4,128,128]{3,0,2,1:T(8,128)S(1)} %fusion.2, f32[16]{0:T(128)S(1)} %get-tuple-element.52, bf16[144,6,128,128]{3,0,2,1:T(8,128)(2,1)} %fusion.29, bf16[144,16]{1,0:T(8,128)(2,1)S(1)} %slice.342), kind=kOutput, calls=%fused_computation.59 | convolution fusion | flops 307232768 | bytes 29364800 | tf_op jit(solution)/shard_map/ko,kdhw->odhw/dot_general | solution.py:48
  (87 shorter events, 64.1 us)
Async XLA Ops:
  0.6 28.1 %copy-start.12 = (u32[128]{0:T(128)S(1)}, u32[128]{0:T(128)}, u32[]{:S(2)}) copy-start(u32[128]{0:T(128)} %constant.42) | copy-start | bytes 1540
  0.6 17.2 %copy-start.5 = (bf16[1,1,4,128,128]{4,3,2,1,0:T(8,128)(2,1)S(1)}, bf16[1,1,4,128,128]{4,3,2,1,0:T(8,128)(2,1)}, u32[]{:S(2)}) copy-start(bf16[1,1,4,128,128]{4,3,2,1,0:T(8,128)(2,1)} %param.10) | copy-start | bytes 393220
  0.7 26.6 %copy-start.7 = (bf16[27,16,16]{0,2,1:T(8,128)(2,1)S(1)}, bf16[27,16,16]{0,2,1:T(8,128)(2,1)}, u32[]{:S(2)}) copy-start(bf16[27,16,16]{0,2,1:T(8,128)(2,1)} %param.11) | copy-start | bytes 41476
  0.7 26.8 %copy-start.8 = (f32[1,1,7376]{2,1,0:T(1,128)S(1)}, f32[1,1,7376]{2,1,0:T(1,128)}, u32[]{:S(2)}) copy-start(f32[1,1,7376]{2,1,0:T(1,128)} %param.12) | copy-start | bytes 88516
  5.7 1.3 copy-start.4
  8.7 40.4 %collective-permute-start = (bf16[32,1,128,128]{3,0,2,1:T(8,128)(2,1)}, bf16[32,1,128,128]{3,0,2,1:T(8,128)(2,1)}, u32[]{:S(2)}, u32[]{:S(2)}) collective-permute-start(bf16[32,1,128,128]{3,0,2,1:T(8,128)(2,1)} %get-tuple-element.32), channel_id=1, source_target_pairs={{0,1},{1,2},{2,3},{3,4},{4,5},{5,6},{6,7},{7,8},{8,9},{9,10},{10,1... | collective-permute-start | bytes 3145736 | tf_op jit(solution)/shard_map/ppermute | solution.py:17
  10.6 38.5 %collective-permute-start.1 = (bf16[32,1,128,128]{3,0,2,1:T(8,128)(2,1)}, bf16[32,1,128,128]{3,0,2,1:T(8,128)(2,1)}, u32[]{:S(2)}, u32[]{:S(2)}) collective-permute-start(bf16[32,1,128,128]{3,0,2,1:T(8,128)(2,1)} %get-tuple-element.33), channel_id=1, source_target_pairs={{1,0},{2,1},{3,2},{4,3},{5,4},{6,5},{7,6},{8,7},{9,8},{10,9},{11,1... | collective-permute-start | bytes 3145736 | tf_op jit(solution)/shard_map/ppermute | solution.py:19
  18.0 12.7 %collective-permute-start.2 = (bf16[1,1,128,128]{3,0,2,1:T(2,128)(2,1)S(1)}, bf16[1,1,128,128]{3,0,2,1:T(2,128)(2,1)S(1)}, u32[]{:S(2)}, u32[]{:S(2)}) collective-permute-start(bf16[1,1,128,128]{3,0,2,1:T(2,128)(2,1)S(1)} %copy.88), channel_id=1, source_target_pairs={{0,1},{1,2},{2,3},{3,4},{4,5},{5,6},{6,7},{7,8},{8,9},{9,10},{10,1... | collective-permute-start | bytes 98312 | tf_op jit(solution)/shard_map/ppermute | solution.py:17
  19.9 11.1 %collective-permute-start.3 = (bf16[1,1,128,128]{3,0,2,1:T(2,128)(2,1)S(1)}, bf16[1,1,128,128]{3,0,2,1:T(2,128)(2,1)S(1)}, u32[]{:S(2)}, u32[]{:S(2)}) collective-permute-start(bf16[1,1,128,128]{3,0,2,1:T(2,128)(2,1)S(1)} %copy.89), channel_id=1, source_target_pairs={{1,0},{2,1},{3,2},{4,3},{5,4},{6,5},{7,6},{8,7},{9,8},{10,9},{11,1... | collective-permute-start | bytes 98312 | tf_op jit(solution)/shard_map/ppermute | solution.py:19
  85.3 5.3 %copy-start = (bf16[1,16,4,128,128]{4,3,2,1,0:T(8,128)(2,1)S(1)}, bf16[1,16,4,128,128]{4,3,2,1,0:T(8,128)(2,1)}, u32[]{:S(2)}) copy-start(bf16[1,16,4,128,128]{4,3,2,1,0:T(8,128)(2,1)} %param.9) | copy-start | bytes 6291460
  108.4 79.8 %copy-start.9 = (f32[1786]{0:T(1024)S(1)}, f32[1786]{0:T(1024)}, u32[]{:S(2)}) copy-start(f32[1786]{0:T(1024)} %param.13) | copy-start | bytes 21436
  108.4 79.8 %copy-start.10 = (f32[1786]{0:T(1024)S(1)}, f32[1786]{0:T(1024)}, u32[]{:S(2)}) copy-start(f32[1786]{0:T(1024)} %param.14) | copy-start | bytes 21436
  108.4 79.8 %copy-start.11 = (f32[1786]{0:T(1024)S(1)}, f32[1786]{0:T(1024)}, u32[]{:S(2)}) copy-start(f32[1786]{0:T(1024)} %param.15) | copy-start | bytes 21436
  220.0 60.1 %copy-start.6 = (bf16[14288]{0:T(1024)(128)(2,1)}, bf16[14288]{0:T(1024)(128)(2,1)S(1)}, u32[]{:S(2)}) copy-start(bf16[14288]{0:T(1024)(128)(2,1)S(1)} %all-reduce.4) | copy-start | bytes 85732
  220.3 4.5 %copy-start.1 = (bf16[9,6,128,128]{3,0,2,1:T(8,128)(2,1)S(1)}, bf16[9,6,128,128]{3,0,2,1:T(8,128)(2,1)}, u32[]{:S(2)}) copy-start(bf16[9,6,128,128]{3,0,2,1:T(8,128)(2,1)} %concatenate.33) | copy-start | bytes 5308420
  232.6 15.9 %copy-start.2 = (bf16[16,4,128,128]{3,0,2,1:T(8,128)(2,1)}, bf16[16,4,128,128]{3,0,2,1:T(8,128)(2,1)S(1)}, u32[]{:S(2)}) copy-start(bf16[16,4,128,128]{3,0,2,1:T(8,128)(2,1)S(1)} %maximum_convert_fusion.1) | copy-start | bytes 6291460
  233.9 50.1 %collective-permute-start.4 = (bf16[16,1,128,128]{3,0,2,1:T(8,128)(2,1)}, bf16[16,1,128,128]{3,0,2,1:T(8,128)(2,1)}, u32[]{:S(2)}, u32[]{:S(2)}) collective-permute-start(bf16[16,1,128,128]{3,0,2,1:T(8,128)(2,1)} %get-tuple-element.34), channel_id=1, source_target_pairs={{0,1},{1,2},{2,3},{3,4},{4,5},{5,6},{6,7},{7,8},{8,9},{9,10},{10,1... | collective-permute-start | bytes 1572872 | tf_op jit(solution)/shard_map/ppermute | solution.py:17
  235.8 48.1 %collective-permute-start.5 = (bf16[16,1,128,128]{3,0,2,1:T(8,128)(2,1)}, bf16[16,1,128,128]{3,0,2,1:T(8,128)(2,1)}, u32[]{:S(2)}, u32[]{:S(2)}) collective-permute-start(bf16[16,1,128,128]{3,0,2,1:T(8,128)(2,1)} %get-tuple-element.35), channel_id=1, source_target_pairs={{1,0},{2,1},{3,2},{4,3},{5,4},{6,5},{7,6},{8,7},{9,8},{10,9},{11,1... | collective-permute-start | bytes 1572872 | tf_op jit(solution)/shard_map/ppermute | solution.py:19
  269.3 14.7 %copy-start.3 = (bf16[16,4,128,128]{3,0,2,1:T(8,128)(2,1)S(1)}, bf16[16,4,128,128]{3,0,2,1:T(8,128)(2,1)}, u32[]{:S(2)}) copy-start(bf16[16,4,128,128]{3,0,2,1:T(8,128)(2,1)} %copy-done.2) | copy-start | bytes 6291460
where the time goes:
time: 343 us; the launch traced here: 336 us
  local copies, waits for them, and re-layouts  103 us (30%)
  blocking collectives  101 us (29%)
  matrix products  88.9 us (26%)
  starting transfers between devices  27.5 us (8%)
  other arithmetic  13 us (4%)
    unnamed x58, local copies, waits for them, and re-layouts  67.1 us
    unnamed x2, blocking collectives  66.9 us
    dot_general x9, matrix products, convolve(): jnp.einsum('ko,kdhw->odhw', kernels[depth_off], stacked[:, depth_off:dept...  62.2 us
    psum x1, blocking collectives, local(): summed_all = lax.psum(partial_grad, 'space')  33.7 us
    dot_general x3, matrix products, correlate(): jnp.einsum('kdhw,odhw->ko', stacked[:, depth_off:depth_off + planes], cot...  26.7 us
    ppermute x3, starting transfers between devices, padded_2(): lax.ppermute(head, axis, [((i + 1) % count, i) for i in range(ends)])  21.8 us
    concatenate x4, local copies, waits for them, and re-layouts, lateral_stack(): jnp.concatenate([spread[:, :, row_off:row_off + height, col_off:col_off +...  21.7 us
  transfers between devices with their start and end apart: 6, of which 1 were waited for; matrix products, arithmetic and copies ran while one was open for 18% of the time, Pallas kernels for 0%

commit v1 on v0

v1 whole, which is shorter than its diff:
```python
import math

import jax
import jax.numpy as jnp
import numpy as np
from jax import lax
from jax.experimental import pallas as pl
from jax.experimental.pallas import tpu as pltpu
from jax.sharding import PartitionSpec as P

BF = jnp.bfloat16
F32 = jnp.float32
VMEM = pltpu.VMEM
LIMIT = 48 * 1024 * 1024


def exchange_matrix():
    rows = lax.broadcasted_iota(jnp.int32, (256, 256), 0)
    cols = lax.broadcasted_iota(jnp.int32, (256, 256), 1)
    return jnp.where(cols == (rows % 16) * 16 + rows // 16, 1.0, 0.0).astype(BF)


def mm(left, right):
    return lax.dot_general(left, right, (((1,), (0,)), ((), ())), preferred_element_type=F32)


def mm_lanes(left, right):
    return lax.dot_general(left, right, (((1,), (1,)), ((), ())), preferred_element_type=F32)


def lane_masks(rows):
    lanes = lax.broadcasted_iota(jnp.int32, (rows, 128), 1)
    return lanes != 0, lanes != 127


def from_left(value, keep):
    return jnp.where(keep, pltpu.roll(value, 1, 1), 0.0)


def from_right(value, keep):
    return jnp.where(keep, pltpu.roll(value, 127, 1), 0.0)


def rows_first(act_ref, cot_ref, act_out, cot_out):
    step = pl.program_id(0)
    swap = exchange_matrix()
    not_first, not_last = lane_masks(256)

    @pl.when(step == 0)
    def _():
        edge = jnp.zeros((4, 1, 16, 128), BF)
        cot_out[:, 0:1] = edge
        cot_out[:, 129:130] = edge

    for pair in range(2):
        cells = jnp.concatenate(
            [cot_ref[:, 2 * pair + z].reshape(256, 128) for z in range(2)], axis=1
        )
        moved = mm(swap, cells)
        for z in range(2):
            part = moved[:, z * 128 : (z + 1) * 128].astype(BF).reshape(16, 16, 128)
            cot_out[2 * pair + z, pl.ds(step * 16 + 1, 16)] = part
        cells = jnp.concatenate(
            [act_ref[:, 2 * pair + z].reshape(256, 128) for z in range(2)], axis=1
        )
        moved = mm(swap, cells)
        for z in range(2):
            part = moved[:, z * 128 : (z + 1) * 128]
            shifted = (from_left(part, not_first), part, from_right(part, not_last))
            for dx in range(3):
                act_out[dx, 2 * pair + z] = shifted[dx].astype(BF).reshape(16, 16, 128)


def call_rows_first(act, cot):
    block = pl.BlockSpec((16, 4, 16, 128), lambda j: (0, 0, j, 0))
    return pl.pallas_call(
        rows_first,
        grid=(8,),
        in_specs=[block, block],
        out_specs=[
            pl.BlockSpec((3, 4, 16, 16, 128), lambda j: (0, 0, j, 0, 0)),
            pl.BlockSpec((4, 130, 16, 128), lambda j: (0, 0, 0, 0)),
        ],
        out_shape=[
            jax.ShapeDtypeStruct((3, 4, 128, 16, 128), BF),
            jax.ShapeDtypeStruct((4, 130, 16, 128), BF),
        ],
        compiler_params=pltpu.CompilerParams(vmem_limit_bytes=LIMIT),
        name="rows_first",
    )(act, cot)


def window(planes, base):
    return jnp.concatenate(
        [ref[z, pl.ds(base, 4)].reshape(64, 128) for ref, z in planes], axis=0
    )


def weight_sum(odd_ref, near_ref, far_ref, act_ref, cot_ref, grad_ref, rim_ref, total):
    step = pl.program_id(0)
    odd = odd_ref[0]
    swap = exchange_matrix()

    @pl.when(step == 0)
    def _():
        total[...] = jnp.zeros_like(total)
        edge = jnp.zeros((2, 1, 16, 128), BF)
        rim_ref[:, 0:1] = edge
        rim_ref[:, 129:130] = edge

        def body(j, carry):
            rows = pl.ds(pl.multiple_of(j * 16, 16), 16)
            cells = jnp.concatenate(
                [ref[0:16, rows].reshape(256, 128) for ref in (near_ref, far_ref)], axis=1
            )
            moved = mm(swap, cells).astype(BF)
            here = pl.ds(j * 16 + 1, 16)
            rim_ref[1 - odd, here] = moved[:, :128].reshape(16, 16, 128)
            rim_ref[odd, here] = moved[:, 128:].reshape(16, 16, 128)
            return carry

        lax.fori_loop(0, 8, body, 0)

    planes = [(rim_ref, 0)] + [(cot_ref, z) for z in range(4)] + [(rim_ref, 1)]
    left, right = [], []
    for q in range(8):
        base = step * 16 + 2 * q
        for zt in range(2):
            left.append(
                jnp.concatenate(
                    [
                        act_ref[dx, 2 * zt + z, 2 * q : 2 * q + 2].reshape(32, 128)
                        for dx in range(3)
                        for z in range(2)
                    ],
                    axis=0,
                )
            )
            right.append(window(planes[2 * zt : 2 * zt + 4], base))
    total[...] += mm_lanes(jnp.concatenate(left, axis=1), jnp.concatenate(right, axis=1))

    @pl.when(step == 7)
    def _():
        for dx in range(3):
            summed = None
            for z in range(2):
                for r in range(2):
                    start = ((dx * 2 + z) * 2 + r) * 16
                    part = total[start : start + 16]
                    shift = (z * 4 + r) * 16
                    if shift:
                        part = pltpu.roll(part, 256 - shift, 1)
                    summed = part if summed is None else summed + part
            grad_ref[dx * 16 : (dx + 1) * 16] = summed


def call_weight_sum(odd, near, far, act_rows, cot_rows):
    whole = lambda shape: pl.BlockSpec(shape, lambda j: (0,) * len(shape))
    return pl.pallas_call(
        weight_sum,
        grid=(8,),
        in_specs=[
            pl.BlockSpec(memory_space=pltpu.SMEM),
            whole((18, 128, 128)),
            whole((18, 128, 128)),
            pl.BlockSpec((3, 4, 16, 16, 128), lambda j: (0, 0, j, 0, 0)),
            whole((4, 130, 16, 128)),
        ],
        out_specs=[whole((48, 256)), whole((2, 130, 16, 128))],
        out_shape=[
            jax.ShapeDtypeStruct((48, 256), F32),
            jax.ShapeDtypeStruct((2, 130, 16, 128), BF),
        ],
        scratch_shapes=[pltpu.VMEM((192, 256), F32)],
        compiler_params=pltpu.CompilerParams(vmem_limit_bytes=LIMIT),
        name="weight_sum",
    )(odd, near, far, act_rows, cot_rows)


def conv_block(step, planes, kernel, out_ref, held, finish):
    swap = exchange_matrix()
    not_first, not_last = lane_masks(64)
    for q in range(8):
        base = step * 16 + 2 * q
        cells = jnp.concatenate(
            [window(planes[2 * zt : 2 * zt + 4], base) for zt in range(2)], axis=1
        )
        product = mm(kernel, cells)
        for zt in range(2):
            part = product[:, zt * 128 : (zt + 1) * 128]
            summed = (
                part[64:128]
                + from_left(part[0:64], not_first)
                + from_right(part[128:192], not_last)
            )
            rounded = finish(summed).astype(BF).reshape(2, 2, 16, 128)
            for z in range(2):
                held[2 * zt + z, 2 * q : 2 * q + 2] = rounded[z]
    for zt in range(2):
        cells = jnp.concatenate(
            [held[2 * zt + z].reshape(256, 128) for z in range(2)], axis=1
        )
        moved = mm(swap, cells).astype(BF)
        for z in range(2):
            out_ref[:, 2 * zt + z] = moved[:, z * 128 : (z + 1) * 128].reshape(16, 16, 128)


def shifted_kernels(bases):
    return jnp.concatenate(
        [
            pltpu.roll(base, (z * 4 + r) * 16, 1) if z + r else base
            for base in bases
            for z in range(2)
            for r in range(2)
        ],
        axis=0,
    ).astype(BF)


def input_grad(weight_ref, cot_ref, rim_ref, out_ref, kernel, held):
    step = pl.program_id(0)

    @pl.when(step == 0)
    def _():
        bases = []
        for dx in range(3):
            base = jnp.zeros((16, 256), F32)
            for dz in range(3):
                for dy in range(3):
                    tap = weight_ref[26 - (9 * dz + 3 * dy + dx)].astype(F32)
                    tap = jnp.concatenate([tap, jnp.zeros((16, 240), F32)], axis=1)
                    place = (dz * 4 + dy) * 16
                    base = base + (pltpu.roll(tap, place, 1) if place else tap)
            bases.append(base)
        kernel[...] = shifted_kernels(bases)

    planes = [(rim_ref, 0)] + [(cot_ref, z) for z in range(4)] + [(rim_ref, 1)]
    conv_block(step, planes, kernel[...], out_ref, held, lambda value: value)


def call_input_grad(weight, cot_rows, rim_rows):
    whole = lambda shape: pl.BlockSpec(shape, lambda j: (0,) * len(shape))
    return pl.pallas_call(
        input_grad,
        grid=(8,),
        in_specs=[whole((27, 16, 16)), whole((4, 130, 16, 128)), whole((2, 130, 16, 128))],
        out_specs=pl.BlockSpec((16, 4, 16, 128), lambda j: (0, 0, j, 0)),
        out_shape=jax.ShapeDtypeStruct((16, 4, 128, 128), BF),
        scratch_shapes=[pltpu.VMEM((192, 256), BF), pltpu.VMEM((4, 16, 16, 128), BF)],
        compiler_params=pltpu.CompilerParams(vmem_limit_bytes=LIMIT),
        name="input_grad",
    )(weight, cot_rows, rim_rows)


def placement():
    table = np.zeros((8, 64, 1408), np.float32)

    def put(group, column):
        table[group % 8, group // 8, column] = 1.0

    for dz in range(3):
        for dy in range(3):
            for dx in range(3):
                k = 9 * dz + 3 * dy + dx
                for i in range(16):
                    put(28 + k * 16 + i, dx * 256 + (dz * 4 + dy) * 16 + i)
                put(k, 896 + dx * 64 + dz * 16 + 3 + dy)
    for lane in range(128):
        put(28 + 27 * 16, 768 + lane)
    put(27, 1152 + 192)
    return table.astype(BF)


def adam(params, moment, second, gradient):
    new_moment = 0.9 * moment + 0.1 * gradient
    new_second = 0.999 * second + 0.001 * gradient * gradient
    new_params = params - 0.01 * new_moment / (jnp.sqrt(new_second) + 1e-08)
    return new_params, new_moment, new_second


def update_encoder(scale, grad_ref, state_ref, table_ref, new_ref, two_ref, one_ref, bias_ref):
    gradient = grad_ref[...] * scale
    new = adam(state_ref[0], state_ref[1], state_ref[2], gradient)
    for n in range(3):
        new_ref[n] = new[n]
    rows = lax.broadcasted_iota(jnp.int32, (64, 128), 0)
    lanes = lax.broadcasted_iota(jnp.int32, (64, 128), 1)
    clean = jnp.where(rows * 128 + lanes < 7376, new[0], 0.0)
    turned = jnp.transpose(clean).astype(BF)
    found = jnp.zeros((16, 1408), F32)
    for group in range(8):
        found = found + mm(turned[group * 16 : (group + 1) * 16], table_ref[group])
    two_ref[...] = shifted_kernels([found[:, dx * 256 : (dx + 1) * 256] for dx in range(3)])
    bias_ref[...] = found[:, 768:896]
    base, bias = found[:, 896:1152], found[:, 1152:1408]
    one_ref[...] = jnp.concatenate(
        [
            (pltpu.roll(base, z * 16 + r, 1) if z + r else base) + bias
            for z in range(2)
            for r in range(8)
        ],
        axis=0,
    ).astype(BF)


def call_update_encoder(scale, grad, state, table):
    return pl.pallas_call(
        lambda *refs: update_encoder(scale, *refs),
        out_shape=[
            jax.ShapeDtypeStruct((3, 64, 128), F32),
            jax.ShapeDtypeStruct((192, 256), BF),
            jax.ShapeDtypeStruct((256, 256), BF),
            jax.ShapeDtypeStruct((16, 128), F32),
        ],
        compiler_params=pltpu.CompilerParams(vmem_limit_bytes=LIMIT),
        name="update_encoder",
    )(grad, state, table)


def volume_windows(odd_ref, near_ref, far_ref, volume_ref, out_ref):
    odd = odd_ref[0]
    not_first, not_last = lane_masks(128)
    for plane in range(8):
        if plane < 2 or plane > 5:
            z = plane if plane < 2 else plane - 6
            low = plane < 2
            near = near_ref[16 + z].astype(F32)
            far = far_ref[16 + z].astype(F32)
            use_near = odd == (1 if low else 0)
            cells = jnp.where(use_near, near, far)
        else:
            cells = volume_ref[plane - 2].astype(F32)
        lateral = (from_left(cells, not_first), cells, from_right(cells, not_last))
        pad = jnp.zeros((4, 128), F32)
        for dx in range(3):
            value = lateral[dx]
            down = jnp.concatenate([pad, value[:124]], axis=0)
            up = jnp.concatenate([value[4:], pad], axis=0)
            out_ref[0, dx, plane] = down.astype(BF).reshape(8, 16, 128)
            out_ref[1, dx, plane] = up.astype(BF).reshape(8, 16, 128)


def call_volume_windows(odd, near, far, volume):
    vmem = pl.BlockSpec(memory_space=pltpu.VMEM)
    return pl.pallas_call(
        volume_windows,
        in_specs=[pl.BlockSpec(memory_space=pltpu.SMEM), vmem, vmem, vmem],
        out_shape=jax.ShapeDtypeStruct((2, 3, 8, 8, 16, 128), BF),
        compiler_params=pltpu.CompilerParams(vmem_limit_bytes=LIMIT),
        name="volume_windows",
    )(odd, near, far, volume)


def encode(inside_ref, one_ref, two_ref, bias_ref, cells_ref, out_ref, first, held):
    step = pl.program_id(0)

    @pl.when(step == 0)
    def _():
        edge = jnp.zeros((6, 1, 16, 128), BF)
        first[:, 0:1] = edge
        first[:, 129:130] = edge
        rows = lax.broadcasted_iota(jnp.int32, (64, 256), 0)
        ones = jnp.where(rows == 0, 1.0, 0.0).astype(BF)
        kernel = one_ref[...]

        def body(j, carry):
            for zp in range(3):
                cells = jnp.concatenate(
                    [
                        jnp.concatenate(
                            [cells_ref[s, dx, 2 * zp + z, j] for s in range(2)], axis=1
                        )
                        for dx in range(3)
                        for z in range(4)
                    ]
                    + [ones],
                    axis=0,
                )
                product = jnp.maximum(mm(kernel, cells), 0.0)
                for s in range(2):
                    part = product[:, s * 128 : (s + 1) * 128].reshape(2, 128, 128)
                    for z in range(2):
                        plane = 2 * zp + z
                        value = part[z]
                        if plane == 0:
                            value = jnp.where(inside_ref[0] == 1, value, 0.0)
                        if plane == 5:
                            value = jnp.where(inside_ref[1] == 1, value, 0.0)
                        first[plane, pl.ds(j * 16 + s * 8 + 1, 8)] = value.astype(BF).reshape(
                            8, 16, 128
                        )
            return carry

        lax.fori_loop(0, 8, body, 0)

    bias = jnp.concatenate([bias_ref[...]] * 4, axis=0)
    planes = [(first, z) for z in range(6)]
    conv_block(
        step, planes, two_ref[...], out_ref, held, lambda value: jnp.maximum(value + bias, 0.0)
    )


def call_encode(inside, one, two, bias, cells):
    whole = lambda shape: pl.BlockSpec(shape, lambda j: (0,) * len(shape))
    return pl.pallas_call(
        encode,
        grid=(8,),
        in_specs=[
            pl.BlockSpec(memory_space=pltpu.SMEM),
            whole((256, 256)),
            whole((192, 256)),
            whole((16, 128)),
            whole((2, 3, 8, 8, 16, 128)),
        ],
        out_specs=pl.BlockSpec((16, 4, 16, 128), lambda j: (0, 0, j, 0)),
        out_shape=jax.ShapeDtypeStruct((16, 4, 128, 128), BF),
        scratch_shapes=[pltpu.VMEM((6, 130, 16, 128), BF), pltpu.VMEM((4, 16, 16, 128), BF)],
        compiler_params=pltpu.CompilerParams(vmem_limit_bytes=LIMIT),
        name="encode",
    )(inside, one, two, bias, cells)


def partner(value, axis, bit):
    count = lax.axis_size(axis)
    return lax.ppermute(value, axis, [(i, i ^ bit) for i in range(count)])


def local(activation, cotangent, volume, dec_weight, enc_grad, params, moment, second):
    act, cot, vol = activation[0], cotangent[0], volume[0, 0]
    space = lax.axis_index("space")
    count = lax.axis_size("space")
    n_dp = lax.axis_size("dp")
    data = lax.axis_index("dp")
    odd = lax.rem(space, 2)
    odd_arg = odd.reshape(1).astype(jnp.int32)

    def boundary(side):
        cot_plane = lax.dynamic_index_in_dim(cot, 3 * side, 1, keepdims=False)
        vol_planes = lax.dynamic_slice_in_dim(vol, 2 * side, 2, 0)
        return jnp.concatenate([cot_plane, vol_planes], axis=0)

    near = lax.ppermute(boundary(1 - odd), "space", [(i, i ^ 1) for i in range(count)])
    pairs = [(i, i + 1) for i in range(1, count - 1, 2)]
    far = lax.ppermute(boundary(odd), "space", pairs + [(b, a) for a, b in pairs])

    enc = jnp.pad(enc_grad[0, 0], (0, 8192 - 7376)).reshape(64, 128)
    pad = lambda value: jnp.pad(value, (0, 2048 - 1786)).reshape(16, 128)
    state = jnp.concatenate([pad(params), pad(moment), pad(second)], axis=0)[None]
    for bit in (1, 2, 4):
        sent = jnp.concatenate([enc, state.reshape(-1, 128)], axis=0)
        got = partner(sent, "dp", bit)
        enc = enc + got[:64]
        state = jnp.concatenate([state, got[64:].reshape(state.shape)], axis=0)
    state = state.reshape(2, 2, 2, 3, 2048)
    for axis, bit in ((0, 4), (1, 2), (2, 1)):
        state = jnp.where((data & bit) != 0, jnp.flip(state, axis), state)
    state = state.reshape(8, 3, 2048)[:, :, :1786].transpose(1, 0, 2).reshape(3, 14288)
    enc_state = jnp.pad(state[:, 6912:], ((0, 0), (0, 8192 - 7376))).reshape(3, 64, 128)

    act_rows, cot_rows = call_rows_first(act, cot)
    dec, rim_rows = call_weight_sum(odd_arg, near, far, act_rows, cot_rows)
    for axis, bit in (("space", 8), ("space", 4)):
        enc = enc + partner(enc, axis, bit)
    both = jnp.concatenate([enc, dec.reshape(96, 128)], axis=0)
    for axis, bit in (("space", 2), ("space", 1)):
        both = both + partner(both, axis, bit)
    enc, dec = both[:64], both[64:]
    grad_input = call_input_grad(dec_weight, cot_rows, rim_rows)[None]

    devices = n_dp * count
    table = jnp.asarray(placement())
    new_enc, two, one, bias = call_update_encoder(1.0 / math.sqrt(devices), enc, enc_state, table)
    cells = call_volume_windows(odd_arg, near, far, vol)
    inside = jnp.stack([space > 0, space < count - 1]).astype(jnp.int32)
    encoded = call_encode(inside, one, two, bias, cells)[None]

    for axis, bit in (("space", 8), ("space", 4), ("dp", 1), ("dp", 2), ("dp", 4)):
        dec = dec + partner(dec, axis, bit)
    voxels = devices * act.shape[1] * act.shape[2] * act.shape[3]
    dec = dec.reshape(3, 16, 4, 4, 16)[:, :, 2::-1, 2::-1]
    dec = dec.transpose(2, 3, 0, 1, 4).reshape(6912) / math.sqrt(voxels)
    new_dec = adam(state[0, :6912], state[1, :6912], state[2, :6912], dec)
    new = [
        jnp.concatenate([new_dec[n], new_enc[n].reshape(8192)[:7376]]) for n in range(3)
    ]
    working = new[0].astype(BF)
    own = [lax.dynamic_slice_in_dim(value, data * 1786, 1786, 0) for value in new]
    return (grad_input, own[0], own[1], own[2], working, encoded)


def solution(mesh):
    in_specs = (
        P("dp", None, "space", None, None),
        P("dp", None, "space", None, None),
        P("dp", None, "space", None, None),
        P(),
        P("dp", "space", None),
        P("dp"),
        P("dp"),
        P("dp"),
    )
    out_specs = (
        P("dp", None, "space", None, None),
        P("dp"),
        P("dp"),
        P("dp"),
        P(),
        P("dp", None, "space", None, None),
    )
    return jax.shard_map(local, mesh=mesh, in_specs=in_specs, out_specs=out_specs, check_vma=False)
```

time: 343 us -> 104 us (0.30)
  the two profiles are of different devices: /device:TPU:16 before, /device:TPU:0 now
where the time goes in v1:
time: 104 us
  Pallas kernels  33.4 us (32%)
  waiting for transfers between devices  24.1 us (23%)
  starting transfers between devices  21.6 us (21%)
  local copies, waits for them, and re-layouts  14.9 us (14%)
  other arithmetic  8.4 us (8%)
  between operations  1.12 us (1%)
    ppermute x12, waiting for transfers between devices, partner(): return lax.ppermute(value, axis, [(i, i ^ bit) for i in range(count)])  24.1 us
    ppermute x12, starting transfers between devices, partner(): return lax.ppermute(value, axis, [(i, i ^ bit) for i in range(count)])  21 us
    pallas_call x1, Pallas kernels, call_encode(): pl.pallas_call(encode, grid=(8,), in_specs=[pl.BlockSpec(memory_space=plt...  9.49 us
    pallas_call x1, Pallas kernels, call_weight_sum(): pl.pallas_call(weight_sum, grid=(8,), in_specs=[pl.BlockSpec(memory_space...  9.21 us
    unnamed x32, local copies, waits for them, and re-layouts  7.61 us
    pallas_call x1, Pallas kernels, call_input_grad(): pl.pallas_call(input_grad, grid=(8,), in_specs=[whole((27, 16, 16)), whol...  7.04 us
    pallas_call x1, Pallas kernels, call_rows_first(): pl.pallas_call(rows_first, grid=(8,), in_specs=[block, block], out_specs=...  6.86 us
  transfers between devices with their start and end apart: 14, of which 9 were waited for; matrix products, arithmetic and copies ran while one was open for 10% of the time, Pallas kernels for 23%

profile of v1, /device:TPU:0, one launch (start us, length us, event | category | flops | bytes accessed | tf_op | source)
XLA Modules:
  0.0 103.6 jit_solution(9512303018535016085)
XLA Ops:
  0.7 0.9 dynamic-slice_bitcast_fusion.2
  1.6 1.3 %dynamic-slice_bitcast_fusion = (bf16[16,128,128]{2,1,0:T(8,128)(2,1)S(1)}, bf16[16,128,128]{2,1,0:T(8,128)(2,1)S(1)}) fusion(bf16[1,16,4,128,128]{4,3,2,1,0:T(8,128)(2,1)} %param.10, s32[]{:T(128)S(6)} %select_n.40, s32[]{:T(128)S(6)} %select_n.38), kind=kLoop, calls=%fused_computation.2 | loop fusion | bytes 2097160 | tf_op jit(solution)/shard_map/jit(dynamic_index_in_dim)/squeeze | solution.py:438
  2.9 0.9 pad_maximum_fusion
  3.9 1.7 %collective-permute-start.2 = (f32[112,128]{1,0:T(8,128)S(1)}, f32[112,128]{1,0:T(8,128)S(1)}, u32[]{:S(2)}, u32[]{:S(2)}) collective-permute-start(f32[112,128]{1,0:T(8,128)S(1)} %pad_maximum_fusion.8), channel_id=1, source_target_pairs={{0,16},{16,0},{32,48},{48,32},{64,80},{80,64},{96,112},{112,96},{1... | collective-permute-start | bytes 172040 | tf_op jit(solution)/shard_map/ppermute | solution.py:425
  5.7 2.7 %collective-permute-done.2 = f32[112,128]{1,0:T(8,128)S(1)} collective-permute-done((f32[112,128]{1,0:T(8,128)S(1)}, f32[112,128]{1,0:T(8,128)S(1)}, u32[]{:S(2)}, u32[]{:S(2)}) %collective-permute-start.2) | collective-permute-done | bytes 57376 | tf_op jit(solution)/shard_map/ppermute | solution.py:425
  8.4 2.1 %collective-permute-start.3 = (f32[160,128]{1,0:T(8,128)S(1)}, f32[160,128]{1,0:T(8,128)S(1)}, u32[]{:S(2)}, u32[]{:S(2)}) collective-permute-start(f32[160,128]{1,0:T(8,128)S(1)} %pad_maximum_fusion.5), channel_id=1, source_target_pairs={{0,32},{16,48},{32,0},{48,16},{64,96},{80,112},{96,64},{112,80},{1... | collective-permute-start | bytes 245768 | tf_op jit(solution)/shard_map/ppermute | solution.py:425
  12.0 0.9 collective-permute-done.3
  13.6 4.0 %collective-permute-start.4 = (f32[256,128]{1,0:T(8,128)}, f32[256,128]{1,0:T(8,128)}, u32[]{:S(2)}, u32[]{:S(2)}) collective-permute-start(f32[256,128]{1,0:T(8,128)} %pad_maximum_fusion.3), channel_id=1, source_target_pairs={{0,64},{16,80},{32,96},{48,112},{64,0},{80,16},{96,32},{112,48},{1... | collective-permute-start | bytes 393224 | tf_op jit(solution)/shard_map/ppermute | solution.py:425
  17.6 3.8 %collective-permute-done.4 = f32[256,128]{1,0:T(8,128)} collective-permute-done((f32[256,128]{1,0:T(8,128)}, f32[256,128]{1,0:T(8,128)}, u32[]{:S(2)}, u32[]{:S(2)}) %collective-permute-start.4) | collective-permute-done | bytes 131104 | tf_op jit(solution)/shard_map/ppermute | solution.py:425
  22.1 5.0 %collective-permute-start.5 = (f32[64,128]{1,0:T(8,128)S(1)}, f32[64,128]{1,0:T(8,128)S(1)}, u32[]{:S(2)}, u32[]{:S(2)}) collective-permute-start(f32[64,128]{1,0:T(8,128)S(1)} %slice_add_fusion), channel_id=1, source_target_pairs={{0,8},{1,9},{2,10},{3,11},{4,12},{5,13},{6,14},{7,15},{8,0},{9,1},... | collective-permute-start | bytes 98312 | tf_op jit(solution)/shard_map/ppermute | solution.py:425
  27.2 1.0 copy.17.weight_ref
  28.2 1.6 %copy-done.3 = bf16[1,16,4,128,128]{4,3,2,1,0:T(8,128)(2,1)S(1)} copy-done((bf16[1,16,4,128,128]{4,3,2,1,0:T(8,128)(2,1)S(1)}, bf16[1,16,4,128,128]{4,3,2,1,0:T(8,128)(2,1)}, u32[]{:S(2)}) %copy-start.3) | copy-done | bytes 2097176
  29.8 6.9 %rows_first.1 = (bf16[3,4,128,16,128]{4,3,2,1,0:T(8,128)(2,1)}, bf16[4,130,16,128]{3,2,1,0:T(8,128)(2,1)}) custom-call(bf16[16,4,128,128]{3,2,1,0:T(8,128)(2,1)S(1)} %bitcast.62, bf16[16,4,128,128]{3,2,1,0:T(8,128)(2,1)S(1)} %bitcast.61), custom_call_target="tpu_custom_call" | custom-call | tf_op jit(solution)/shard_map/rows_first/pallas_call | solution.py:76
  36.7 0.9 slice.84
  37.6 1.7 %collective-permute-start.6 = (f32[64,128]{1,0:T(8,128)S(1)}, f32[64,128]{1,0:T(8,128)S(1)}, u32[]{:S(2)}, u32[]{:S(2)}) collective-permute-start(f32[64,128]{1,0:T(8,128)S(1)} %add.83), channel_id=1, source_target_pairs={{0,4},{1,5},{2,6},{3,7},{4,0},{5,1},{6,2},{7,3},{8,12},{9,13},{10,... | collective-permute-start | bytes 98312 | tf_op jit(solution)/shard_map/ppermute | solution.py:425
  39.4 3.7 %collective-permute-done.6 = f32[64,128]{1,0:T(8,128)S(1)} collective-permute-done((f32[64,128]{1,0:T(8,128)S(1)}, f32[64,128]{1,0:T(8,128)S(1)}, u32[]{:S(2)}, u32[]{:S(2)}) %collective-permute-start.6) | collective-permute-done | bytes 32800 | tf_op jit(solution)/shard_map/ppermute | solution.py:425
  43.1 1.6 %copy-done = bf16[4,130,16,128]{3,2,1,0:T(8,128)(2,1)S(1)} copy-done((bf16[4,130,16,128]{3,2,1,0:T(8,128)(2,1)S(1)}, bf16[4,130,16,128]{3,2,1,0:T(8,128)(2,1)}, u32[]{:S(2)}) %copy-start) | copy-done | bytes 2129944
  44.7 9.2 %weight_sum.1 = (f32[48,256]{1,0:T(8,128)S(1)}, bf16[2,130,16,128]{3,2,1,0:T(8,128)(2,1)S(1)}) custom-call(s32[1]{0:T(128)} %bitcast.2.odd_ref, bf16[18,128,128]{2,1,0:T(8,128)(2,1)S(1)} %collective-permute-done.near_ref, bf16[18,128,128]{2,1,0:T(8,128)(2,1)S(1)} %collective-permute-done.1.far_ref, bf16[3,4,128,16,128]{4,3,2,1,0:T(8,128)(2,1)} %get-tuple-element.15.act_ref, ...), custom_call_target="tpu_custom_call" | custom-call | tf_op jit(solution)/shard_map/weight_sum/pallas_call | solution.py:159
  53.9 1.0 copy-done.5
  55.1 4.4 %collective-permute-done.7 = f32[160,128]{1,0:T(8,128)S(1)} collective-permute-done((f32[160,128]{1,0:T(8,128)S(1)}, f32[160,128]{1,0:T(8,128)S(1)}, u32[]{:S(2)}, u32[]{:S(2)}) %collective-permute-start.7) | collective-permute-done | bytes 81952 | tf_op jit(solution)/shard_map/ppermute | solution.py:425
  59.6 1.2 %collective-permute-done.8 = f32[160,128]{1,0:T(8,128)S(1)} collective-permute-done((f32[160,128]{1,0:T(8,128)S(1)}, f32[160,128]{1,0:T(8,128)S(1)}, u32[]{:S(2)}, u32[]{:S(2)}) %collective-permute-start.8) | collective-permute-done | bytes 81952 | tf_op jit(solution)/shard_map/ppermute | solution.py:425
  61.0 5.5 %collective-permute-done.9 = f32[96,128]{1,0:T(8,128)S(1)} collective-permute-done((f32[96,128]{1,0:T(8,128)S(1)}, f32[96,128]{1,0:T(8,128)S(1)}, u32[]{:S(2)}, u32[]{:S(2)}) %collective-permute-start.9) | collective-permute-done | bytes 49184 | tf_op jit(solution)/shard_map/ppermute | solution.py:425
  66.5 1.7 %collective-permute-start.10 = (f32[96,128]{1,0:T(8,128)S(1)}, f32[96,128]{1,0:T(8,128)}, u32[]{:S(2)}, u32[]{:S(2)}) collective-permute-start(f32[96,128]{1,0:T(8,128)S(1)} %slice_add_fusion.3), channel_id=1, source_target_pairs={{0,4},{1,5},{2,6},{3,7},{4,0},{5,1},{6,2},{7,3},{8,12},{9,13},{10,... | collective-permute-start | bytes 147464 | tf_op jit(solution)/shard_map/ppermute | solution.py:425
  68.9 1.8 %reshape.90 = f32[3,14288]{1,0:T(4,128)} reshape(f32[3,8,1786]{2,1,0:T(8,128)} %copy.18) | data formatting | bytes 342912 | tf_op jit(solution)/shard_map/reshape | solution.py:457
  70.8 1.5 %collective-permute-done.10 = f32[96,128]{1,0:T(8,128)} collective-permute-done((f32[96,128]{1,0:T(8,128)S(1)}, f32[96,128]{1,0:T(8,128)}, u32[]{:S(2)}, u32[]{:S(2)}) %collective-permute-start.10) | collective-permute-done | bytes 49184 | tf_op jit(solution)/shard_map/ppermute | solution.py:425
  73.9 1.9 %fusion.2 = (f32[6912]{0:T(1024)S(1)}, f32[6912]{0:T(1024)}, f32[6912]{0:T(1024)}) fusion(f32[3,14288]{1,0:T(4,128)} %reshape.90), kind=kLoop, calls=%fused_computation.40 | loop fusion | flops 13824 | bytes 165888 | tf_op jit(solution)/shard_map/mul | solution.py:275
  75.8 0.9 slice.93
  77.3 1.2 %copy-done.6 = bf16[2,130,16,128]{3,2,1,0:T(8,128)(2,1)S(1)} copy-done((bf16[2,130,16,128]{3,2,1,0:T(8,128)(2,1)S(1)}, bf16[2,130,16,128]{3,2,1,0:T(8,128)(2,1)}, u32[]{:S(2)}) %copy-start.6) | copy-done | bytes 1064984
  78.6 7.0 %input_grad.1 = bf16[16,4,128,128]{3,2,1,0:T(8,128)(2,1)} custom-call(bf16[27,16,16]{2,1,0:T(8,128)(2,1)S(1)} %copy.17.weight_ref, bf16[4,130,16,128]{3,2,1,0:T(8,128)(2,1)S(1)} %copy-done.1, bf16[2,130,16,128]{3,2,1,0:T(8,128)(2,1)S(1)} %copy-done.6), custom_call_target="tpu_custom_call" | custom-call | tf_op jit(solution)/shard_map/input_grad/pallas_call | solution.py:243
  85.9 1.1 %copy-done.4 = bf16[8,64,1408]{2,1,0:T(8,128)(2,1)S(1)} copy-done((bf16[8,64,1408]{2,1,0:T(8,128)(2,1)S(1)}, bf16[8,64,1408]{2,1,0:T(8,128)(2,1)}, u32[]{:S(2)}) %copy-start.4) | copy-done | bytes 1441816
  87.6 3.7 %collective-permute-start.13 = (f32[96,128]{1,0:T(8,128)S(1)}, f32[96,128]{1,0:T(8,128)S(1)}, u32[]{:S(2)}, u32[]{:S(2)}) collective-permute-start(f32[96,128]{1,0:T(8,128)S(1)} %add.90), channel_id=1, source_target_pairs={{0,64},{16,80},{32,96},{48,112},{64,0},{80,16},{96,32},{112,48},{1... | collective-permute-start | bytes 147464 | tf_op jit(solution)/shard_map/ppermute | solution.py:425
  91.3 9.5 %encode.1 = bf16[16,4,128,128]{3,2,1,0:T(8,128)(2,1)} custom-call(s32[2]{0:T(128)S(1)} %add_convert_fusion.inside_ref, bf16[256,256]{1,0:T(8,128)(2,1)S(1)} %get-tuple-element.19.one_ref, bf16[192,256]{1,0:T(8,128)(2,1)S(1)} %get-tuple-element.20.two_ref, f32[16,128]{1,0:T(8,128)S(1)} %get-tuple-element.21.bias_ref, ...), custom_call_target="tpu_custom_call" | custom-call | tf_op jit(solution)/shard_map/encode/pallas_call | solution.py:405
  (89 shorter events, 10.3 us)
Async XLA Ops:
  0.6 3.1 %copy-start.11 = (f32[1786]{0:T(1024)S(1)}, f32[1786]{0:T(1024)}, u32[]{:S(2)}) copy-start(f32[1786]{0:T(1024)} %param.16) | copy-start | bytes 21436
  0.6 3.1 %copy-start.12 = (f32[1786]{0:T(1024)S(1)}, f32[1786]{0:T(1024)}, u32[]{:S(2)}) copy-start(f32[1786]{0:T(1024)} %param.15) | copy-start | bytes 21436
  0.7 3.2 %copy-start.13 = (f32[1786]{0:T(1024)S(1)}, f32[1786]{0:T(1024)}, u32[]{:S(2)}) copy-start(f32[1786]{0:T(1024)} %param.14) | copy-start | bytes 21436
  0.7 3.2 %copy-start.10 = (f32[1,1,7376]{2,1,0:T(1,128)S(1)}, f32[1,1,7376]{2,1,0:T(1,128)}, u32[]{:S(2)}) copy-start(f32[1,1,7376]{2,1,0:T(1,128)} %param.13) | copy-start | bytes 88516
  2.9 25.3 %copy-start.2 = (bf16[1,16,4,128,128]{4,3,2,1,0:T(8,128)(2,1)S(1)}, bf16[1,16,4,128,128]{4,3,2,1,0:T(8,128)(2,1)}, u32[]{:S(2)}) copy-start(bf16[1,16,4,128,128]{4,3,2,1,0:T(8,128)(2,1)} %param.10) | copy-start | bytes 6291460
  3.8 39.3 %collective-permute-start = (bf16[18,128,128]{2,1,0:T(8,128)(2,1)}, bf16[18,128,128]{2,1,0:T(8,128)(2,1)S(1)}, u32[]{:S(2)}, u32[]{:S(2)}) collective-permute-start(bf16[18,128,128]{2,1,0:T(8,128)(2,1)} %pad_maximum_fusion), channel_id=1, source_target_pairs={{0,1},{1,0},{2,3},{3,2},{4,5},{5,4},{6,7},{7,6},{8,9},{9,8},{10,11... | collective-permute-start | bytes 1769480 | tf_op jit(solution)/shard_map/ppermute | solution.py:442
  3.9 4.4 %collective-permute-start.2 = (f32[112,128]{1,0:T(8,128)S(1)}, f32[112,128]{1,0:T(8,128)S(1)}, u32[]{:S(2)}, u32[]{:S(2)}) collective-permute-start(f32[112,128]{1,0:T(8,128)S(1)} %pad_maximum_fusion.8), channel_id=1, source_target_pairs={{0,16},{16,0},{32,48},{48,32},{64,80},{80,64},{96,112},{112,96},{1... | collective-permute-start | bytes 172040 | tf_op jit(solution)/shard_map/ppermute | solution.py:425
  8.4 4.5 %collective-permute-start.3 = (f32[160,128]{1,0:T(8,128)S(1)}, f32[160,128]{1,0:T(8,128)S(1)}, u32[]{:S(2)}, u32[]{:S(2)}) collective-permute-start(f32[160,128]{1,0:T(8,128)S(1)} %pad_maximum_fusion.5), channel_id=1, source_target_pairs={{0,32},{16,48},{32,0},{48,16},{64,96},{80,112},{96,64},{112,80},{1... | collective-permute-start | bytes 245768 | tf_op jit(solution)/shard_map/ppermute | solution.py:425
  11.3 31.8 %collective-permute-start.1 = (bf16[18,128,128]{2,1,0:T(8,128)(2,1)}, bf16[18,128,128]{2,1,0:T(8,128)(2,1)S(1)}, u32[]{:S(2)}, u32[]{:S(2)}) collective-permute-start(bf16[18,128,128]{2,1,0:T(8,128)(2,1)} %pad_maximum_fusion.1), channel_id=1, source_target_pairs={{1,2},{3,4},{5,6},{7,8},{9,10},{11,12},{13,14},{2,1},{4,3},{6,5},{... | collective-permute-start | bytes 1769480 | tf_op jit(solution)/shard_map/ppermute | solution.py:444
  13.6 7.7 %collective-permute-start.4 = (f32[256,128]{1,0:T(8,128)}, f32[256,128]{1,0:T(8,128)}, u32[]{:S(2)}, u32[]{:S(2)}) collective-permute-start(f32[256,128]{1,0:T(8,128)} %pad_maximum_fusion.3), channel_id=1, source_target_pairs={{0,64},{16,80},{32,96},{48,112},{64,0},{80,16},{96,32},{112,48},{1... | collective-permute-start | bytes 393224 | tf_op jit(solution)/shard_map/ppermute | solution.py:425
  22.1 15.4 %collective-permute-start.5 = (f32[64,128]{1,0:T(8,128)S(1)}, f32[64,128]{1,0:T(8,128)S(1)}, u32[]{:S(2)}, u32[]{:S(2)}) collective-permute-start(f32[64,128]{1,0:T(8,128)S(1)} %slice_add_fusion), channel_id=1, source_target_pairs={{0,8},{1,9},{2,10},{3,11},{4,12},{5,13},{6,14},{7,15},{8,0},{9,1},... | collective-permute-start | bytes 98312 | tf_op jit(solution)/shard_map/ppermute | solution.py:425
  28.2 1.6 %copy-start.3 = (bf16[1,16,4,128,128]{4,3,2,1,0:T(8,128)(2,1)S(1)}, bf16[1,16,4,128,128]{4,3,2,1,0:T(8,128)(2,1)}, u32[]{:S(2)}) copy-start(bf16[1,16,4,128,128]{4,3,2,1,0:T(8,128)(2,1)} %param.9) | copy-start | bytes 6291460
  37.6 5.5 %collective-permute-start.6 = (f32[64,128]{1,0:T(8,128)S(1)}, f32[64,128]{1,0:T(8,128)S(1)}, u32[]{:S(2)}, u32[]{:S(2)}) collective-permute-start(f32[64,128]{1,0:T(8,128)S(1)} %add.83), channel_id=1, source_target_pairs={{0,4},{1,5},{2,6},{3,7},{4,0},{5,1},{6,2},{7,3},{8,12},{9,13},{10,... | collective-permute-start | bytes 98312 | tf_op jit(solution)/shard_map/ppermute | solution.py:425
  43.1 1.6 %copy-start = (bf16[4,130,16,128]{3,2,1,0:T(8,128)(2,1)S(1)}, bf16[4,130,16,128]{3,2,1,0:T(8,128)(2,1)}, u32[]{:S(2)}) copy-start(bf16[4,130,16,128]{3,2,1,0:T(8,128)(2,1)} %get-tuple-element.14.cot_ref) | copy-start | bytes 6389764
  53.9 1.0 copy-start.5
  54.9 4.5 %collective-permute-start.7 = (f32[160,128]{1,0:T(8,128)S(1)}, f32[160,128]{1,0:T(8,128)S(1)}, u32[]{:S(2)}, u32[]{:S(2)}) collective-permute-start(f32[160,128]{1,0:T(8,128)S(1)} %pad_maximum_fusion.6), channel_id=1, source_target_pairs={{0,2},{1,3},{2,0},{3,1},{4,6},{5,7},{6,4},{7,5},{8,10},{9,11},{10,... | collective-permute-start | bytes 245768 | tf_op jit(solution)/shard_map/ppermute | solution.py:425
  55.1 22.3 %copy-start.1 = (bf16[4,130,16,128]{3,2,1,0:T(8,128)(2,1)S(1)}, bf16[4,130,16,128]{3,2,1,0:T(8,128)(2,1)}, u32[]{:S(2)}) copy-start(bf16[4,130,16,128]{3,2,1,0:T(8,128)(2,1)} %get-tuple-element.14.cot_ref) | copy-start | bytes 6389764
  59.4 1.4 %collective-permute-start.8 = (f32[160,128]{1,0:T(8,128)S(1)}, f32[160,128]{1,0:T(8,128)S(1)}, u32[]{:S(2)}, u32[]{:S(2)}) collective-permute-start(f32[160,128]{1,0:T(8,128)S(1)} %fusion.6), channel_id=1, source_target_pairs={{0,1},{1,0},{2,3},{3,2},{4,5},{5,4},{6,7},{7,6},{8,9},{9,8},{10,11... | collective-permute-start | bytes 245768 | tf_op jit(solution)/shard_map/ppermute | solution.py:425
  60.8 5.7 %collective-permute-start.9 = (f32[96,128]{1,0:T(8,128)S(1)}, f32[96,128]{1,0:T(8,128)S(1)}, u32[]{:S(2)}, u32[]{:S(2)}) collective-permute-start(f32[96,128]{1,0:T(8,128)S(1)} %slice.89), channel_id=1, source_target_pairs={{0,8},{1,9},{2,10},{3,11},{4,12},{5,13},{6,14},{7,15},{8,0},{9,1},... | collective-permute-start | bytes 147464 | tf_op jit(solution)/shard_map/ppermute | solution.py:425
  66.5 5.8 %collective-permute-start.10 = (f32[96,128]{1,0:T(8,128)S(1)}, f32[96,128]{1,0:T(8,128)}, u32[]{:S(2)}, u32[]{:S(2)}) collective-permute-start(f32[96,128]{1,0:T(8,128)S(1)} %slice_add_fusion.3), channel_id=1, source_target_pairs={{0,4},{1,5},{2,6},{3,7},{4,0},{5,1},{6,2},{7,3},{8,12},{9,13},{10,... | collective-permute-start | bytes 147464 | tf_op jit(solution)/shard_map/ppermute | solution.py:425
  73.1 4.1 %collective-permute-start.11 = (f32[96,128]{1,0:T(8,128)S(1)}, f32[96,128]{1,0:T(8,128)S(1)}, u32[]{:S(2)}, u32[]{:S(2)}) collective-permute-start(f32[96,128]{1,0:T(8,128)S(1)} %add.88), channel_id=1, source_target_pairs={{0,16},{16,0},{32,48},{48,32},{64,80},{80,64},{96,112},{112,96},{1... | collective-permute-start | bytes 147464 | tf_op jit(solution)/shard_map/ppermute | solution.py:425
  77.2 10.4 %collective-permute-start.12 = (f32[96,128]{1,0:T(8,128)S(1)}, f32[96,128]{1,0:T(8,128)S(1)}, u32[]{:S(2)}, u32[]{:S(2)}) collective-permute-start(f32[96,128]{1,0:T(8,128)S(1)} %add.89), channel_id=1, source_target_pairs={{0,32},{16,48},{32,0},{48,16},{64,96},{80,112},{96,64},{112,80},{1... | collective-permute-start | bytes 147464 | tf_op jit(solution)/shard_map/ppermute | solution.py:425
  77.3 1.2 %copy-start.6 = (bf16[2,130,16,128]{3,2,1,0:T(8,128)(2,1)S(1)}, bf16[2,130,16,128]{3,2,1,0:T(8,128)(2,1)}, u32[]{:S(2)}) copy-start(bf16[2,130,16,128]{3,2,1,0:T(8,128)(2,1)} %copy-done.5) | copy-start | bytes 3194884
  78.6 7.0 %copy-start.7 = (bf16[1,1,4,128,128]{4,3,2,1,0:T(8,128)(2,1)S(1)}, bf16[1,1,4,128,128]{4,3,2,1,0:T(8,128)(2,1)}, u32[]{:S(2)}) copy-start(bf16[1,1,4,128,128]{4,3,2,1,0:T(8,128)(2,1)} %param.11) | copy-start | bytes 393220
  85.6 1.4 %copy-start.4 = (bf16[8,64,1408]{2,1,0:T(8,128)(2,1)S(1)}, bf16[8,64,1408]{2,1,0:T(8,128)(2,1)}, u32[]{:S(2)}) copy-start(bf16[8,64,1408]{2,1,0:T(8,128)(2,1)} %constant.58.clone.refs_2_) | copy-start | bytes 4325380
  87.6 13.2 %collective-permute-start.13 = (f32[96,128]{1,0:T(8,128)S(1)}, f32[96,128]{1,0:T(8,128)S(1)}, u32[]{:S(2)}, u32[]{:S(2)}) collective-permute-start(f32[96,128]{1,0:T(8,128)S(1)} %add.90), channel_id=1, source_target_pairs={{0,64},{16,80},{32,96},{48,112},{64,0},{80,16},{96,32},{112,48},{1... | collective-permute-start | bytes 147464 | tf_op jit(solution)/shard_map/ppermute | solution.py:425
  100.8 0.7 copy-start.8
  100.8 0.8 copy-start.9

commit v2 on v0

v2 whole, which is shorter than its diff:
```python
import functools
import math

import jax
import jax.numpy as jnp
import numpy as np
from jax import lax
from jax.experimental import pallas as pl
from jax.experimental.pallas import tpu as pltpu
from jax.sharding import PartitionSpec as P

BF = jnp.bfloat16
F32 = jnp.float32
LIMIT = 32 * 1024 * 1024


def exchange_matrix():
    rows = lax.broadcasted_iota(jnp.int32, (256, 256), 0)
    cols = lax.broadcasted_iota(jnp.int32, (256, 256), 1)
    return jnp.where(cols == (rows % 16) * 16 + rows // 16, 1.0, 0.0).astype(BF)


def mm(left, right):
    return lax.dot_general(left, right, (((1,), (0,)), ((), ())), preferred_element_type=F32)


def mm_lanes(left, right):
    return lax.dot_general(left, right, (((1,), (1,)), ((), ())), preferred_element_type=F32)


def lane_masks(rows):
    lanes = lax.broadcasted_iota(jnp.int32, (rows, 128), 1)
    return lanes != 0, lanes != 127


def from_left(value, keep):
    return jnp.where(keep, pltpu.roll(value, 1, 1), 0.0)


def from_right(value, keep):
    return jnp.where(keep, pltpu.roll(value, 127, 1), 0.0)


VM = pl.BlockSpec(memory_space=pltpu.VMEM)
HBM = pl.BlockSpec(memory_space=pltpu.HBM)
SM = pl.BlockSpec(memory_space=pltpu.SMEM)


def kernel_call(
    body, name, in_specs, out_shape, scratch=(), micros=1.0, out_specs=None, aliases=None
):
    if out_specs is None:
        out_specs = jax.tree.map(lambda shape: VM, out_shape)
    return pl.pallas_call(
        body,
        in_specs=in_specs,
        out_specs=out_specs,
        out_shape=out_shape,
        input_output_aliases=aliases or {},
        scratch_shapes=list(scratch),
        compiler_params=pltpu.CompilerParams(vmem_limit_bytes=LIMIT),
        cost_estimate=pl.CostEstimate(
            flops=int(micros * 1.15e9), bytes_accessed=int(micros * 3.6e6), transcendentals=0
        ),
        name=name,
    )


def in_hbm(value):
    return pltpu.with_memory_space_constraint(value, pltpu.HBM)


def edges(odd_ref, cot_ref, vol_ref, far_ref, near_ref, planes, slabs, sems):
    odd = odd_ref[0]
    outs = (far_ref, near_ref)
    sides = (odd, 1 - odd)
    copies = []
    for n in range(2):
        pair = (
            pltpu.make_async_copy(cot_ref.at[:, 3 * sides[n]], planes.at[n], sems.at[n]),
            pltpu.make_async_copy(
                vol_ref.at[pl.ds(2 * sides[n], 2)], slabs.at[n], sems.at[2 + n]
            ),
        )
        for copy in pair:
            copy.start()
        copies.append(pair)
    for n in range(2):
        copies[n][0].wait()
        for j in range(8):
            rows = slice(j * 16, (j + 1) * 16)
            outs[n][rows] = jnp.swapaxes(planes[n, :, rows], 0, 1)
        copies[n][1].wait()
        outs[n][128:144] = slabs[n].reshape(16, 16, 128)


def call_edges(odd, cot, vol):
    shape = jax.ShapeDtypeStruct((144, 16, 128), BF)
    return kernel_call(
        edges,
        "edges",
        [SM, HBM, HBM],
        [shape, shape],
        [
            pltpu.VMEM((2, 16, 128, 128), BF),
            pltpu.VMEM((2, 2, 128, 128), BF),
            pltpu.SemaphoreType.DMA((4,)),
        ],
        1.3,
    )(odd, in_hbm(cot), in_hbm(vol))


def lateral(cells):
    zero = jnp.zeros((cells.shape[0], 1), BF)
    left = jnp.concatenate([zero, cells[:, :127]], axis=1)
    right = jnp.concatenate([cells[:, 1:], zero], axis=1)
    return left, cells, right


def aligned(total, rows, keep):
    out = []
    lanes = lax.broadcasted_iota(jnp.int32, (16, 256), 1) // 64
    for dx in range(3):
        summed = None
        for z, (turn, valid) in enumerate(keep):
            for r in range(2):
                start = ((dx * rows + z) * 2 + r) * 16
                part = total[start : start + 16]
                shift = (turn - r * 16) % 256
                if shift:
                    part = pltpu.roll(part, shift, 1)
                if valid is not None:
                    part = jnp.where((lanes >= valid[0]) & (lanes <= valid[1]), part, 0.0)
                summed = part if summed is None else summed + part
        out.append(summed)
    return jnp.concatenate(out, axis=0)


def inner(
    act_hbm, cot_hbm, token_ref, grad_ref, cot_rows, act_edge, act_ref, cot_ref, act_rows, total, sems
):
    def copies(step):
        rows = pl.ds(pl.multiple_of(step * 16, 16), 16)
        return [
            pltpu.make_async_copy(source.at[:, :, rows], target.at[:, :, rows], sems.at[n, step])
            for n, (source, target) in enumerate(((act_hbm, act_ref), (cot_hbm, cot_ref)))
        ]

    for step in range(8):
        for copy in copies(step):
            copy.start()
    edge = jnp.zeros((4, 1, 16, 128), BF)
    cot_rows[:, 0:1] = edge
    cot_rows[:, 129:130] = edge
    total[...] = jnp.zeros_like(total)

    def turn(step):
        for copy in copies(step):
            copy.wait()
        rows = pl.ds(pl.multiple_of(step * 16, 16), 16)
        for z in range(4):
            cot_rows[z, pl.ds(step * 16 + 1, 16)] = jnp.swapaxes(cot_ref[:, z, rows], 0, 1)
            cells = jnp.swapaxes(act_ref[:, z, rows], 0, 1).reshape(256, 128)
            for dx, value in enumerate(lateral(cells)):
                act_rows[dx, z, pl.ds(step * 16, 16)] = value.reshape(16, 16, 128)

    def gather(step):
        left, right = [], []
        for q in range(8):
            base = step * 16 + 2 * q
            left.append(
                jnp.concatenate(
                    [
                        act_rows[dx, z, pl.ds(base, 2)].reshape(32, 128)
                        for dx in range(3)
                        for z in range(4)
                    ],
                    axis=0,
                )
            )
            right.append(window([(cot_rows, z) for z in range(4)], base))
        total[...] += mm_lanes(jnp.concatenate(left, axis=1), jnp.concatenate(right, axis=1))

    turn(0)
    turn(1)

    def body(step, carry):
        turn(step + 2)
        gather(step)
        return carry

    lax.fori_loop(0, 6, body, 0)
    gather(6)
    gather(7)
    grad_ref[...] = aligned(
        total, 4, [(64, (1, 2)), (0, None), (192, None), (128, (0, 1))]
    )
    act_edge[0] = act_rows[:, 0]
    act_edge[1] = act_rows[:, 3]


def call_inner(act, cot, token):
    return kernel_call(
        inner,
        "inner",
        [HBM, HBM, VM],
        [
            jax.ShapeDtypeStruct((48, 256), F32),
            jax.ShapeDtypeStruct((4, 130, 16, 128), BF),
            jax.ShapeDtypeStruct((2, 3, 128, 16, 128), BF),
        ],
        [
            pltpu.VMEM((16, 4, 128, 128), BF),
            pltpu.VMEM((16, 4, 128, 128), BF),
            pltpu.VMEM((3, 4, 128, 16, 128), BF),
            pltpu.VMEM((384, 256), F32),
            pltpu.SemaphoreType.DMA((2, 8)),
        ],
        4.0,
    )(in_hbm(act), in_hbm(cot), token)


def window(planes, base):
    return jnp.concatenate(
        [ref[z, pl.ds(base, 4)].reshape(64, 128) for ref, z in planes], axis=0
    )


def outer(odd_ref, far_ref, near_ref, act_edge, inner_ref, token_ref, grad_ref, rim_ref, total):
    edge = jnp.zeros((2, 1, 16, 128), BF)
    rim_ref[:, 0:1] = edge
    rim_ref[:, 129:130] = edge
    rim_ref[odd_ref[0], 1:129] = far_ref[0:128]
    rim_ref[1 - odd_ref[0], 1:129] = near_ref[0:128]
    total[...] = jnp.zeros_like(total)

    def body(step, carry):
        left, right = [], []
        for q in range(16):
            base = step * 32 + 2 * q
            left.append(
                jnp.concatenate(
                    [
                        act_edge[side, dx, pl.ds(base, 2)].reshape(32, 128)
                        for dx in range(3)
                        for side in range(2)
                    ],
                    axis=0,
                )
            )
            right.append(window([(rim_ref, 0), (rim_ref, 1)], base))
        total[:, 0:128] += mm_lanes(
            jnp.concatenate(left, axis=1), jnp.concatenate(right, axis=1)
        )
        return carry

    lax.fori_loop(0, 4, body, 0)
    grad_ref[...] = inner_ref[...] + aligned(total, 2, [(0, (0, 0)), (64, (2, 2))])


def call_outer(odd, far, near, act_edge, inner_grad, token):
    return kernel_call(
        outer,
        "outer",
        [SM, VM, VM, VM, VM, VM],
        [
            jax.ShapeDtypeStruct((48, 256), F32),
            jax.ShapeDtypeStruct((2, 130, 16, 128), BF),
        ],
        [pltpu.VMEM((192, 256), F32)],
        2.5,
    )(odd, far, near, act_edge, inner_grad, token)


def conv_rows(part, planes, kernel, out_hbm, held, out, sems, finish):
    swap = exchange_matrix()
    not_first, not_last = lane_masks(64)
    first = part * 64

    def compute(pair):
        for block in range(2):
            for q in range(8):
                base = first + pair * 32 + block * 16 + 2 * q
                cells = jnp.concatenate(
                    [window(planes[2 * zt : 2 * zt + 4], base) for zt in range(2)], axis=1
                )
                product = mm(kernel, cells)
                for zt in range(2):
                    piece = product[:, zt * 128 : (zt + 1) * 128]
                    summed = (
                        piece[64:128]
                        + from_left(piece[0:64], not_first)
                        + from_right(piece[128:192], not_last)
                    )
                    rounded = finish(summed).astype(BF).reshape(2, 2, 16, 128)
                    for z in range(2):
                        held[pair, block, 2 * zt + z, 2 * q : 2 * q + 2] = rounded[z]

    def flush(pair):
        for block in range(2):
            rows = slice(pair * 32 + block * 16, pair * 32 + block * 16 + 16)
            for zt in range(2):
                cells = jnp.concatenate(
                    [held[pair, block, 2 * zt + z].reshape(256, 128) for z in range(2)], axis=1
                )
                moved = mm(swap, cells).astype(BF)
                for z in range(2):
                    piece = moved[:, z * 128 : (z + 1) * 128]
                    out[:, 2 * zt + z, rows] = piece.reshape(16, 16, 128)
        copy = pltpu.make_async_copy(
            out.at[:, :, pair * 32 : pair * 32 + 32],
            out_hbm.at[:, :, first + pair * 32 : first + pair * 32 + 32],
            sems.at[pair],
        )
        copy.start()
        return copy

    compute(0)
    compute(1)
    copies = [flush(0), flush(1)]
    for copy in copies:
        copy.wait()


FIELD = jax.ShapeDtypeStruct((16, 4, 128, 128), BF)
HELD = [
    pltpu.VMEM((2, 2, 4, 16, 16, 128), BF),
    pltpu.VMEM((16, 4, 64, 128), BF),
    pltpu.SemaphoreType.DMA((2,)),
]


def shifted_kernels(bases):
    return jnp.concatenate(
        [
            pltpu.roll(base, (z * 4 + r) * 16, 1) if z + r else base
            for base in bases
            for z in range(2)
            for r in range(2)
        ],
        axis=0,
    ).astype(BF)


def input_grad(part, kernel_ref, cot_ref, rim_ref, token_ref, *refs):
    out_ref, held, out, sems = refs[-4:]
    planes = [(rim_ref, 0)] + [(cot_ref, z) for z in range(4)] + [(rim_ref, 1)]
    conv_rows(part, planes, kernel_ref[...], out_ref, held, out, sems, lambda value: value)


def call_input_grad(part, kernel, cot_rows, rim_rows, token, *before):
    return kernel_call(
        functools.partial(input_grad, part),
        f"input_grad_{part}",
        [VM, VM, VM, VM] + [HBM] * len(before),
        FIELD,
        HELD,
        2.2,
        HBM,
        {4: 0} if before else None,
    )(kernel, cot_rows, rim_rows, token, *before)


def placement():
    table = np.zeros((8, 64, 1408), np.float32)

    def put(group, column):
        table[group % 8, group // 8, column] = 1.0

    for dz in range(3):
        for dy in range(3):
            for dx in range(3):
                k = 9 * dz + 3 * dy + dx
                for i in range(16):
                    put(28 + k * 16 + i, dx * 256 + (dz * 4 + dy) * 16 + i)
                put(k, 896 + dx * 64 + dz * 16 + 3 + dy)
    for lane in range(128):
        put(28 + 27 * 16, 768 + lane)
    put(27, 1152 + 192)
    return table.astype(BF)


def adam(params, moment, second, gradient):
    new_moment = 0.9 * moment + 0.1 * gradient
    new_second = 0.999 * second + 0.001 * gradient * gradient
    new_params = params - 0.01 * new_moment / (jnp.sqrt(new_second) + 1e-08)
    return new_params, new_moment, new_second


def update_encoder(scale, grad_ref, state_ref, table_ref, two_ref, one_ref, bias_ref):
    gradient = grad_ref[0:58] * scale
    new = adam(state_ref[0, 54:112], state_ref[1, 54:112], state_ref[2, 54:112], gradient)[0]
    rows = lax.broadcasted_iota(jnp.int32, (58, 128), 0)
    lanes = lax.broadcasted_iota(jnp.int32, (58, 128), 1)
    clean = jnp.where(rows * 128 + lanes < 7376, new, 0.0)
    clean = jnp.concatenate([clean, jnp.zeros((6, 128), F32)], axis=0)
    turned = jnp.transpose(clean).astype(BF)
    found = jnp.zeros((16, 1408), F32)
    for group in range(8):
        found = found + mm(turned[group * 16 : (group + 1) * 16], table_ref[group])
    two_ref[...] = shifted_kernels([found[:, dx * 256 : (dx + 1) * 256] for dx in range(3)])
    bias_ref[...] = found[:, 768:896]
    base, bias = found[:, 896:1152], found[:, 1152:1408]
    one_ref[...] = jnp.concatenate(
        [
            (pltpu.roll(base, z * 16 + r, 1) if z + r else base) + bias
            for z in range(2)
            for r in range(8)
        ],
        axis=0,
    ).astype(BF)


def call_update_encoder(scale, grad, state, table):
    return kernel_call(
        functools.partial(update_encoder, scale),
        "update_encoder",
        [VM, VM, VM],
        [
            jax.ShapeDtypeStruct((192, 256), BF),
            jax.ShapeDtypeStruct((256, 256), BF),
            jax.ShapeDtypeStruct((16, 128), F32),
        ],
        micros=0.6,
    )(grad, state, table)


def flat_state(data_ref, shards_ref, token_ref, out_ref):
    data = data_ref[0]
    lanes = lax.broadcasted_iota(jnp.int32, (16, 128), 1)
    for shard in range(8):
        block = shards_ref[lax.bitwise_xor(data, shard)]
        kept = 128 - 6 * shard
        for n in range(3):
            rows = block[16 * n : 16 * n + 16]
            if shard:
                rows = pltpu.roll(rows, kept, 1)
                start = out_ref[n, 14 * shard - 1 : 14 * shard]
                out_ref[n, 14 * shard - 1 : 14 * shard] = jnp.where(
                    lanes[:1] < kept, start, rows[:1]
                )
            out_ref[n, 14 * shard : 14 * shard + 14] = jnp.where(
                lanes[:14] < kept, rows[:14], rows[1:15]
            )


def call_flat_state(data, shards, token):
    return kernel_call(
        flat_state,
        "flat_state",
        [SM, VM, VM],
        jax.ShapeDtypeStruct((3, 112, 128), F32),
        micros=0.3,
    )(data, shards, token)


def finish(scales, dec_ref, enc_ref, state_ref, grad_ref, work_ref):
    lanes = lax.broadcasted_iota(jnp.int32, (16, 128), 1) // 16
    rows = lax.broadcasted_iota(jnp.int32, (16, 128), 0) % 8
    for dz in range(3):
        for dy in range(3):
            place = ((2 - dz) * 4 + 2 - dy) * 16
            for dx in range(3):
                block = dec_ref[dx * 16 : (dx + 1) * 16]
                if place:
                    block = pltpu.roll(block, 256 - place, 1)
                block = jnp.where(lanes == 0, block[:, :128], 0.0)
                for width in (16, 32, 64):
                    block = block + pltpu.roll(block, width, 1)
                block = jnp.where(lanes == rows, block, 0.0).reshape(2, 8, 128)
                k = 9 * dz + 3 * dy + dx
                grad_ref[2 * k : 2 * k + 2] = jnp.sum(block, axis=1) * scales[0]
    grad_ref[54:112] = enc_ref[0:58] * scales[1]
    new = adam(state_ref[0], state_ref[1], state_ref[2], grad_ref[...])[0]
    work_ref[...] = new.astype(BF)


def call_finish(scales, dec, enc, state):
    return kernel_call(
        functools.partial(finish, scales),
        "finish",
        [VM, VM, VM],
        [jax.ShapeDtypeStruct((112, 128), F32), jax.ShapeDtypeStruct((112, 128), BF)],
    )(dec, enc, state)


def prepare(odd_ref, far_ref, near_ref, volume_ref, weight_ref, token_ref, out_ref, kernel_ref):
    not_first, not_last = lane_masks(128)
    for plane in range(8):
        if plane < 2 or plane > 5:
            z = plane if plane < 2 else plane - 6
            far, near = [
                ref[128 + 8 * z : 136 + 8 * z].reshape(128, 128).astype(F32)
                for ref in (far_ref, near_ref)
            ]
            cells = jnp.where(odd_ref[0] == (0 if plane < 2 else 1), far, near)
        else:
            cells = volume_ref[plane - 2]
        cells = cells.astype(F32)
        sides = (from_left(cells, not_first), cells, from_right(cells, not_last))
        pad = jnp.zeros((4, 128), F32)
        for dx in range(3):
            value = sides[dx]
            down = jnp.concatenate([pad, value[:124]], axis=0)
            up = jnp.concatenate([value[4:], pad], axis=0)
            out_ref[0, dx, plane] = down.astype(BF).reshape(8, 16, 128)
            out_ref[1, dx, plane] = up.astype(BF).reshape(8, 16, 128)
    weight = weight_ref[...].reshape(256, 27)
    weight = jnp.concatenate([weight, jnp.zeros((256, 101), BF)], axis=1)
    taps = lax.broadcasted_iota(jnp.int32, (128, 256), 0)
    columns = lax.broadcasted_iota(jnp.int32, (128, 256), 1)
    dz, dy = columns // 64, columns // 16 % 4
    rows = lax.broadcasted_iota(jnp.int32, (256, 256), 0)
    lanes = lax.broadcasted_iota(jnp.int32, (256, 256), 1)
    same = rows % 16 == lanes % 16
    summing = jnp.where(rows[:16] == lanes[:16] // 16, 1.0, 0.0).astype(BF)
    bases = []
    for dx in range(3):
        wanted = (dz < 3) & (dy < 3) & (taps == 26 - (9 * dz + 3 * dy + dx))
        spread = mm(weight, jnp.where(wanted, 1.0, 0.0).astype(BF))
        bases.append(mm(summing, jnp.where(same, spread, 0.0).astype(BF)))
    kernel_ref[...] = shifted_kernels(bases)


def call_prepare(odd, far, near, volume, weight, token):
    return kernel_call(
        prepare,
        "prepare",
        [SM, VM, VM, VM, VM, VM],
        [
            jax.ShapeDtypeStruct((2, 3, 8, 8, 16, 128), BF),
            jax.ShapeDtypeStruct((192, 256), BF),
        ],
        micros=1.3,
    )(odd, far, near, volume, weight, token)


def first_layer(inside_ref, one_ref, cells_ref, token_ref, first):
    edge = jnp.zeros((6, 1, 16, 128), BF)
    first[:, 0:1] = edge
    first[:, 129:130] = edge
    rows = lax.broadcasted_iota(jnp.int32, (64, 256), 0)
    ones = jnp.where(rows == 0, 1.0, 0.0).astype(BF)
    kernel = one_ref[...]

    def body(half, carry):
        for part in range(4):
            j = half * 4 + part
            for zp in range(3):
                cells = jnp.concatenate(
                    [
                        jnp.concatenate(
                            [cells_ref[s, dx, 2 * zp + z, j] for s in range(2)], axis=1
                        )
                        for dx in range(3)
                        for z in range(4)
                    ]
                    + [ones],
                    axis=0,
                )
                product = jnp.maximum(mm(kernel, cells), 0.0)
                for s in range(2):
                    found = product[:, s * 128 : (s + 1) * 128].reshape(2, 128, 128)
                    for z in range(2):
                        plane = 2 * zp + z
                        value = found[z]
                        if plane == 0:
                            value = jnp.where(inside_ref[0] == 1, value, 0.0)
                        if plane == 5:
                            value = jnp.where(inside_ref[1] == 1, value, 0.0)
                        value = value.astype(BF).reshape(8, 16, 128)
                        first[plane, pl.ds(j * 16 + s * 8 + 1, 8)] = value
        return carry

    lax.fori_loop(0, 2, body, 0)


def call_first_layer(inside, one, cells, token):
    return kernel_call(
        first_layer,
        "first_layer",
        [SM, VM, VM, VM],
        jax.ShapeDtypeStruct((6, 130, 16, 128), BF),
        micros=1.5,
    )(inside, one, cells, token)


def second_layer(part, two_ref, bias_ref, first, token_ref, *refs):
    out_ref, held, out, sems = refs[-4:]
    bias = jnp.concatenate([bias_ref[...]] * 4, axis=0)
    finish = lambda value: jnp.maximum(value + bias, 0.0)
    planes = [(first, z) for z in range(6)]
    conv_rows(part, planes, two_ref[...], out_ref, held, out, sems, finish)


def call_second_layer(part, two, bias, first, token, *before):
    return kernel_call(
        functools.partial(second_layer, part),
        f"second_layer_{part}",
        [VM, VM, VM, VM] + [HBM] * len(before),
        FIELD,
        HELD,
        2.2,
        HBM,
        {4: 0} if before else None,
    )(two, bias, first, token, *before)


def partner(value, axis, bit):
    count = lax.axis_size(axis)
    return lax.ppermute(value, axis, [(i, i ^ bit) for i in range(count)])


def after(*values):
    return lax.optimization_barrier(values)


def local(activation, cotangent, volume, dec_weight, enc_grad, params, moment, second):
    act, cot, vol = activation[0], cotangent[0], volume[0, 0]
    space = lax.axis_index("space")
    count = lax.axis_size("space")
    n_dp = lax.axis_size("dp")
    data = lax.axis_index("dp")
    devices = n_dp * count
    voxels = devices * act.shape[1] * act.shape[2] * act.shape[3]

    odd = lax.rem(space, 2)
    odd_arg = odd.reshape(1).astype(jnp.int32)
    far, near = call_edges(odd_arg, cot, vol)
    pairs = [(i, i + 1) for i in range(1, count - 1, 2)]
    far_in = lax.ppermute(far, "space", pairs + [(b, a) for a, b in pairs])
    near_in = lax.ppermute(near, "space", [(i, i ^ 1) for i in range(count)])

    scales = (1.0 / math.sqrt(voxels), 1.0 / math.sqrt(devices))
    data_arg = data.reshape(1).astype(jnp.int32)
    inside = jnp.stack([space > 0, space < count - 1]).astype(jnp.int32)
    table = jnp.asarray(placement())

    far, enc_grad = after(far, enc_grad)
    enc = jnp.pad(enc_grad[0, 0], (0, 8192 - 7376)).reshape(64, 128)
    pad = lambda value: jnp.pad(value, (0, 2048 - 1786)).reshape(16, 128)
    state = jnp.concatenate([pad(params), pad(moment), pad(second)], axis=0)

    def dp_round(grads, state, bit):
        sent = jnp.concatenate([grads, state], axis=0)
        got = partner(sent, "dp", bit)
        size = grads.shape[0]
        return grads + got[:size], jnp.concatenate([state, got[size:]], axis=0)

    token = enc
    enc, state = dp_round(enc, state, 1)
    inner_grad, cot_rows, act_edge = call_inner(act, cot, token)
    enc, inner_grad = after(enc, inner_grad)
    enc, state = dp_round(enc, state, 2)
    dec, rim_rows = call_outer(odd_arg, far_in, near_in, act_edge, inner_grad, inner_grad)

    both = jnp.concatenate([enc, dec.reshape(96, 128)], axis=0)
    token = both
    both, state = dp_round(both, state, 4)
    cells, kernel = call_prepare(
        odd_arg, far_in, near_in, vol, dec_weight.transpose(1, 2, 0), token
    )
    token = both
    both = both + partner(both, "space", 8)
    grad_input = call_input_grad(0, kernel, cot_rows, rim_rows, token)
    token = both
    both, grad_input = after(both, grad_input)
    both = both + partner(both, "space", 4)
    grad_input = call_input_grad(1, kernel, cot_rows, rim_rows, token, grad_input)
    token = both
    both, grad_input = after(both, grad_input)
    both = both + partner(both, "space", 2)
    state = call_flat_state(data_arg, state.reshape(8, 48, 128), token)
    both, state = after(both, state)
    both = both + partner(both, "space", 1)
    enc, dec = both[:64], both[64:]

    two, one, bias = call_update_encoder(scales[1], enc, state, table)
    first = call_first_layer(inside, one, cells, enc)
    dec = dec + partner(dec, "dp", 1)
    token = dec
    dec, first = after(dec, first)
    dec = dec + partner(dec, "dp", 2)
    encoded = call_second_layer(0, two, bias, first, token)
    encoded = call_second_layer(1, two, bias, first, token, encoded)

    flat, working = call_finish(scales, dec.reshape(48, 256), enc, state)
    working = working.reshape(112 * 128)[:14288]
    own = lax.dynamic_slice_in_dim(flat.reshape(112 * 128), data * 1786, 1786, 0)
    own = adam(params, moment, second, own)
    return (grad_input[None], own[0], own[1], own[2], working, encoded[None])


def solution(mesh):
    in_specs = (
        P("dp", None, "space", None, None),
        P("dp", None, "space", None, None),
        P("dp", None, "space", None, None),
        P(),
        P("dp", "space", None),
        P("dp"),
        P("dp"),
        P("dp"),
    )
    out_specs = (
        P("dp", None, "space", None, None),
        P("dp"),
        P("dp"),
        P("dp"),
        P(),
        P("dp", None, "space", None, None),
    )
    return jax.shard_map(local, mesh=mesh, in_specs=in_specs, out_specs=out_specs, check_vma=False)
```

time: 343 us -> 63.3 us (0.18)
  the two profiles are of different devices: /device:TPU:16 before, /device:TPU:0 now
where the time goes in v2:
time: 63.3 us; the launch traced here: 63.1 us
  Pallas kernels  22.7 us (36%)
  starting transfers between devices  18.8 us (30%)
  waiting for transfers between devices  17.4 us (27%)
  local copies, waits for them, and re-layouts  2.23 us (4%)
  between operations  1.09 us (2%)
  other arithmetic  0.94 us (1%)
    ppermute x9, waiting for transfers between devices, partner(): return lax.ppermute(value, axis, [(i, i ^ bit) for i in range(count)])  17.4 us
    ppermute x9, starting transfers between devices, partner(): return lax.ppermute(value, axis, [(i, i ^ bit) for i in range(count)])  15.5 us
    pallas_call x1, Pallas kernels, call_inner(): kernel_call(inner, 'inner', [HBM, HBM, VM], [jax.ShapeDtypeStruct((48, 25...  5.31 us
    pallas_call x2, Pallas kernels, call_second_layer(): kernel_call(functools.partial(second_layer, part), f'second_layer_{part}'...  5.03 us
    pallas_call x2, Pallas kernels, call_input_grad(): kernel_call(functools.partial(input_grad, part), f'input_grad_{part}', [V...  4.88 us
    ppermute x1, starting transfers between devices, local(): near_in = lax.ppermute(near, 'space', [(i, i ^ 1) for i in range(count)])  2.54 us
    unnamed x28, local copies, waits for them, and re-layouts  2.17 us
    pallas_call x1, Pallas kernels, call_first_layer(): kernel_call(first_layer, 'first_layer', [SM, VM, VM, VM], jax.ShapeDtypeS...  1.7 us
  transfers between devices with their start and end apart: 11, of which 6 were waited for; matrix products, arithmetic and copies ran while one was open for 0% of the time, Pallas kernels for 29%

profile of v2, /device:TPU:0, one launch (start us, length us, event | category | flops | bytes accessed | tf_op | source)
XLA Modules:
  0.0 63.1 jit_solution(8412312091652471529)
XLA Ops:
  0.7 1.4 %edges.1 = (bf16[144,16,128]{2,1,0:T(8,128)(2,1)S(1)}, bf16[144,16,128]{2,1,0:T(8,128)(2,1)S(1)}) custom-call(s32[1]{0:T(128)} %bitcast.odd_ref, bf16[16,4,128,128]{3,2,1,0:T(8,128)(2,1)} %bitcast.47, bf16[4,128,128]{2,1,0:T(8,128)(2,1)} %bitcast.44), custom_call_target="tpu_custom_call" | custom-call | flops 1495000064 | bytes 4680000 | tf_op jit(solution)/shard_map/edges/pallas_call | solution.py:99
  2.1 0.7 %collective-permute-start.2 = (bf16[144,16,128]{2,1,0:T(8,128)(2,1)S(1)}, bf16[144,16,128]{2,1,0:T(8,128)(2,1)S(1)}, u32[]{:S(2)}, u32[]{:S(2)}) collective-permute-start(bf16[144,16,128]{2,1,0:T(8,128)(2,1)S(1)} %get-tuple-element.31), channel_id=1, source_target_pairs={{1,2},{3,4},{5,6},{7,8},{9,10},{11,12},{13,14},{2,1},{4,3},{6,5},{... | collective-permute-start | bytes 1769480 | tf_op jit(solution)/shard_map/ppermute | solution.py:631
  3.0 1.7 %collective-permute-start = (f32[112,128]{1,0:T(8,128)S(1)}, f32[112,128]{1,0:T(8,128)S(1)}, u32[]{:S(2)}, u32[]{:S(2)}) collective-permute-start(f32[112,128]{1,0:T(8,128)S(1)} %pad_maximum_fusion.1), channel_id=1, source_target_pairs={{0,16},{16,0},{32,48},{48,32},{64,80},{80,64},{96,112},{112,96},{1... | collective-permute-start | bytes 172040 | tf_op jit(solution)/shard_map/ppermute | solution.py:611
  4.8 2.5 %collective-permute-start.3 = (bf16[144,16,128]{2,1,0:T(8,128)(2,1)S(1)}, bf16[144,16,128]{2,1,0:T(8,128)(2,1)S(1)}, u32[]{:S(2)}, u32[]{:S(2)}) collective-permute-start(bf16[144,16,128]{2,1,0:T(8,128)(2,1)S(1)} %get-tuple-element.35), channel_id=1, source_target_pairs={{0,1},{1,0},{2,3},{3,2},{4,5},{5,4},{6,7},{7,6},{8,9},{9,8},{10,11... | collective-permute-start | bytes 1769480 | tf_op jit(solution)/shard_map/ppermute | solution.py:632
  7.3 5.3 %inner.1 = (f32[48,256]{1,0:T(8,128)S(1)}, bf16[4,130,16,128]{3,2,1,0:T(8,128)(2,1)S(1)}, bf16[2,3,128,16,128]{4,3,2,1,0:T(8,128)(2,1)S(1)}) custom-call(bf16[16,4,128,128]{3,2,1,0:T(8,128)(2,1)} %bitcast.49, bf16[16,4,128,128]{3,2,1,0:T(8,128)(2,1)} %bitcast.48, f32[64,128]{1,0:T(8,128)S(1)} %pad_bitcast_fusion.token_ref), custom_call_target="tpu_custom_call" | custom-call | flops 4600000000 | bytes 14400000 | tf_op jit(solution)/shard_map/inner/pallas_call | solution.py:203
  12.6 1.4 %copy-done.3 = bf16[4,130,16,128]{3,2,1,0:T(8,128)(2,1)} copy-done((bf16[4,130,16,128]{3,2,1,0:T(8,128)(2,1)}, bf16[4,130,16,128]{3,2,1,0:T(8,128)(2,1)S(1)}, u32[]{:S(2)}) %copy-start.3) | copy-done | bytes 2129944
  14.0 2.0 %collective-permute-start.1 = (f32[160,128]{1,0:T(8,128)S(1)}, f32[160,128]{1,0:T(8,128)S(1)}, u32[]{:S(2)}, u32[]{:S(2)}) collective-permute-start(f32[160,128]{1,0:T(8,128)S(1)} %constant_dynamic-update-slice_fusion), channel_id=1, source_target_pairs={{0,32},{16,48},{32,0},{48,16},{64,96},{80,112},{96,64},{112,80},{1... | collective-permute-start | bytes 245768 | tf_op jit(solution)/shard_map/ppermute | solution.py:611
  16.0 2.6 %collective-permute-done.1 = f32[160,128]{1,0:T(8,128)S(1)} collective-permute-done((f32[160,128]{1,0:T(8,128)S(1)}, f32[160,128]{1,0:T(8,128)S(1)}, u32[]{:S(2)}, u32[]{:S(2)}) %collective-permute-start.1) | collective-permute-done | bytes 81952 | tf_op jit(solution)/shard_map/ppermute | solution.py:611
  18.7 1.7 %outer.1 = (f32[48,256]{1,0:T(8,128)S(1)}, bf16[2,130,16,128]{3,2,1,0:T(8,128)(2,1)S(1)}) custom-call(s32[1]{0:T(128)} %bitcast.odd_ref, bf16[144,16,128]{2,1,0:T(8,128)(2,1)S(1)} %collective-permute-done.2.far_ref, bf16[144,16,128]{2,1,0:T(8,128)(2,1)S(1)} %collective-permute-done.3.near_ref, bf16[2,3,128,16,128]{4,3,2,1,0:T(8,128)(2,1)S(1)} %get-tuple-element.36.act_edge, ...), custom_call_target="tpu_custom_call" | custom-call | flops 2875000064 | bytes 9000000 | tf_op jit(solution)/shard_map/outer/pallas_call | solution.py:262
  20.5 3.9 %collective-permute-start.4 = (f32[352,128]{1,0:T(8,128)S(1)}, f32[352,128]{1,0:T(8,128)S(1)}, u32[]{:S(2)}, u32[]{:S(2)}) collective-permute-start(f32[352,128]{1,0:T(8,128)S(1)} %get-tuple-element.62), channel_id=1, source_target_pairs={{0,64},{16,80},{32,96},{48,112},{64,0},{80,16},{96,32},{112,48},{1... | collective-permute-start | bytes 540680 | tf_op jit(solution)/shard_map/ppermute | solution.py:611
  24.3 3.6 %collective-permute-done.4 = f32[352,128]{1,0:T(8,128)S(1)} collective-permute-done((f32[352,128]{1,0:T(8,128)S(1)}, f32[352,128]{1,0:T(8,128)S(1)}, u32[]{:S(2)}, u32[]{:S(2)}) %collective-permute-start.4) | collective-permute-done | bytes 180256 | tf_op jit(solution)/shard_map/ppermute | solution.py:611
  27.9 5.8 %collective-permute-start.5 = (f32[160,128]{1,0:T(8,128)S(1)}, f32[160,128]{1,0:T(8,128)S(1)}, u32[]{:S(2)}, u32[]{:S(2)}) collective-permute-start(f32[160,128]{1,0:T(8,128)S(1)} %get-tuple-element.64.token_ref), channel_id=1, source_target_pairs={{0,8},{1,9},{2,10},{3,11},{4,12},{5,13},{6,14},{7,15},{8,0},{9,1},... | collective-permute-start | bytes 245768 | tf_op jit(solution)/shard_map/ppermute | solution.py:611
  33.7 0.9 %prepare.1 = (bf16[2,3,8,8,16,128]{5,4,3,2,1,0:T(8,128)(2,1)S(1)}, bf16[192,256]{1,0:T(8,128)(2,1)S(1)}) custom-call(s32[1]{0:T(128)} %bitcast.odd_ref, bf16[144,16,128]{2,1,0:T(8,128)(2,1)S(1)} %collective-permute-done.2.far_ref, bf16[144,16,128]{2,1,0:T(8,128)(2,1)S(1)} %collective-permute-done.3.near_ref, bf16[4,128,128]{2,1,0:T(8,128)(2,1)S(1)} %bitcast.45, ...), custom_call_target="tpu_custom_call" | custom-call | flops 1495000064 | bytes 4680000 | tf_op jit(solution)/shard_map/prepare/pallas_call | solution.py:526
  34.6 0.7 %copy-done.4 = bf16[4,130,16,128]{3,2,1,0:T(8,128)(2,1)S(1)} copy-done((bf16[4,130,16,128]{3,2,1,0:T(8,128)(2,1)S(1)}, bf16[4,130,16,128]{3,2,1,0:T(8,128)(2,1)}, u32[]{:S(2)}) %copy-start.4) | copy-done | bytes 2129944
  35.3 2.4 %input_grad_0.1.refs_0_ = bf16[16,4,128,128]{3,2,1,0:T(8,128)(2,1)} custom-call(bf16[192,256]{1,0:T(8,128)(2,1)S(1)} %get-tuple-element.39.kernel_ref, bf16[4,130,16,128]{3,2,1,0:T(8,128)(2,1)S(1)} %copy-done.4, bf16[2,130,16,128]{3,2,1,0:T(8,128)(2,1)S(1)} %get-tuple-element.41.rim_ref, f32[160,128]{1,0:T(8,128)S(1)} %get-tuple-element.64.token_ref), custom_call_target="tpu_custom_call" | custom-call | flops 2529999872 | bytes 7920000 | tf_op jit(solution)/shard_map/input_grad_0/pallas_call | solution.py:352
  37.8 0.1 collective-permute-start.6
  37.9 2.5 %input_grad_1.1 = bf16[16,4,128,128]{3,2,1,0:T(8,128)(2,1)} custom-call(bf16[192,256]{1,0:T(8,128)(2,1)S(1)} %get-tuple-element.39.kernel_ref, bf16[4,130,16,128]{3,2,1,0:T(8,128)(2,1)S(1)} %copy-done.4, bf16[2,130,16,128]{3,2,1,0:T(8,128)(2,1)S(1)} %get-tuple-element.41.rim_ref, f32[160,128]{1,0:T(8,128)S(1)} %add.53.token_ref, ...), custom_call_target="tpu_custom_call", output_to_operand_aliasing={{}: (4, {})} | custom-call | flops 2529999872 | bytes 7920000 | tf_op jit(solution)/shard_map/input_grad_1/pallas_call | solution.py:352
  40.4 3.9 %collective-permute-done.6 = f32[160,128]{1,0:T(8,128)S(1)} collective-permute-done((f32[160,128]{1,0:T(8,128)S(1)}, f32[160,128]{1,0:T(8,128)S(1)}, u32[]{:S(2)}, u32[]{:S(2)}) %collective-permute-start.6) | collective-permute-done | bytes 81952 | tf_op jit(solution)/shard_map/ppermute | solution.py:611
  44.3 0.1 collective-permute-start.7
  44.4 0.1 flat_state.1.state_ref
  44.6 4.3 %collective-permute-done.7 = f32[160,128]{1,0:T(8,128)S(1)} collective-permute-done((f32[160,128]{1,0:T(8,128)S(1)}, f32[160,128]{1,0:T(8,128)S(1)}, u32[]{:S(2)}, u32[]{:S(2)}) %collective-permute-start.7) | collective-permute-done | bytes 81952 | tf_op jit(solution)/shard_map/ppermute | solution.py:611
  48.8 0.1 collective-permute-start.8
  49.0 1.2 %collective-permute-done.8 = f32[160,128]{1,0:T(8,128)S(1)} collective-permute-done((f32[160,128]{1,0:T(8,128)S(1)}, f32[160,128]{1,0:T(8,128)S(1)}, u32[]{:S(2)}, u32[]{:S(2)}) %collective-permute-start.8) | collective-permute-done | bytes 81952 | tf_op jit(solution)/shard_map/ppermute | solution.py:611
  50.2 0.1 collective-permute-start.9
  50.3 0.6 update_encoder.1
  50.9 1.7 %first_layer.1.first = bf16[6,130,16,128]{3,2,1,0:T(8,128)(2,1)S(1)} custom-call(s32[2]{0:T(128)S(1)} %add_convert_fusion.inside_ref, bf16[256,256]{1,0:T(8,128)(2,1)S(1)} %get-tuple-element.48.one_ref, bf16[2,3,8,8,16,128]{5,4,3,2,1,0:T(8,128)(2,1)S(1)} %get-tuple-element.49.cells_ref, f32[64,128]{1,0:T(8,128)S(1)} %slice.43.grad_ref.token_ref.enc_ref), custom_call_target="tpu_custom_call" | custom-call | flops 1724999936 | bytes 5400000 | tf_op jit(solution)/shard_map/first_layer/pallas_call | solution.py:579
  52.6 1.8 %collective-permute-done.9 = f32[96,128]{1,0:T(8,128)S(1)} collective-permute-done((f32[96,128]{1,0:T(8,128)S(1)}, f32[96,128]{1,0:T(8,128)S(1)}, u32[]{:S(2)}, u32[]{:S(2)}) %collective-permute-start.9) | collective-permute-done | bytes 49184 | tf_op jit(solution)/shard_map/ppermute | solution.py:611
  54.4 1.8 %collective-permute-start.10 = (f32[96,128]{1,0:T(8,128)S(1)}, f32[96,128]{1,0:T(8,128)S(1)}, u32[]{:S(2)}, u32[]{:S(2)}) collective-permute-start(f32[96,128]{1,0:T(8,128)S(1)} %slice_add_fusion.3.token_ref), channel_id=1, source_target_pairs={{0,32},{16,48},{32,0},{48,16},{64,96},{80,112},{96,64},{112,80},{1... | collective-permute-start | bytes 147464 | tf_op jit(solution)/shard_map/ppermute | solution.py:611
  56.2 2.5 %second_layer_0.1.refs_0_ = bf16[16,4,128,128]{3,2,1,0:T(8,128)(2,1)} custom-call(bf16[192,256]{1,0:T(8,128)(2,1)S(1)} %get-tuple-element.53.two_ref, f32[16,128]{1,0:T(8,128)S(1)} %get-tuple-element.54.bias_ref, bf16[6,130,16,128]{3,2,1,0:T(8,128)(2,1)S(1)} %first_layer.1.first, f32[96,128]{1,0:T(8,128)S(1)} %slice_add_fusion.3.token_ref), custom_call_target="tpu_custom_call" | custom-call | flops 2529999872 | bytes 7920000 | tf_op jit(solution)/shard_map/second_layer_0/pallas_call | solution.py:597
  58.8 2.5 %second_layer_1.1 = bf16[16,4,128,128]{3,2,1,0:T(8,128)(2,1)} custom-call(bf16[192,256]{1,0:T(8,128)(2,1)S(1)} %get-tuple-element.53.two_ref, f32[16,128]{1,0:T(8,128)S(1)} %get-tuple-element.54.bias_ref, bf16[6,130,16,128]{3,2,1,0:T(8,128)(2,1)S(1)} %first_layer.1.first, f32[96,128]{1,0:T(8,128)S(1)} %slice_add_fusion.3.token_ref, ...), custom_call_target="tpu_custom_call", output_to_operand_aliasing={{}: (4, {})} | custom-call | flops 2529999872 | bytes 7920000 | tf_op jit(solution)/shard_map/second_layer_1/pallas_call | solution.py:597
  61.3 1.1 %finish.1 = (f32[112,128]{1,0:T(8,128)S(1)}, bf16[112,128]{1,0:T(8,128)(2,1)}) custom-call(f32[48,256]{1,0:T(8,128)S(1)} %reshape.53.dec_ref, f32[64,128]{1,0:T(8,128)S(1)} %slice.43.grad_ref.token_ref.enc_ref, f32[3,112,128]{2,1,0:T(8,128)S(1)} %flat_state.1.state_ref), custom_call_target="tpu_custom_call" | custom-call | flops 1150000000 | bytes 3600000 | tf_op jit(solution)/shard_map/finish/pallas_call | solution.py:479
  62.4 0.7 %divide_subtract_fusion = (f32[1786]{0:T(1024)}, f32[1786]{0:T(1024)}, f32[1786]{0:T(1024)}) fusion(f32[1786]{0:T(1024)S(1)} %copy-done.5, f32[14336]{0:T(1024)S(1)} %bitcast.42, s32[]{:T(128)S(6)} %select_n.3, f32[1786]{0:T(1024)S(1)} %copy-done.7, f32[1786]{0:T(1024)S(1)} %copy-done.6), kind=kLoop, calls=%fused_computation.26 | loop fusion | flops 19646 | bytes 50012 | tf_op jit(solution)/shard_map/sub | solution.py:386
  (52 shorter events, 0.4 us)
Async XLA Ops:
  0.6 2.2 %copy-start.5 = (f32[1786]{0:T(1024)S(1)}, f32[1786]{0:T(1024)}, u32[]{:S(2)}) copy-start(f32[1786]{0:T(1024)} %param.14) | copy-start | bytes 21436
  0.6 2.2 %copy-start.8 = (f32[1,1,7376]{2,1,0:T(1,128)S(1)}, f32[1,1,7376]{2,1,0:T(1,128)}, u32[]{:S(2)}) copy-start(f32[1,1,7376]{2,1,0:T(1,128)} %param.13) | copy-start | bytes 88516
  0.7 2.3 %copy-start.6 = (f32[1786]{0:T(1024)S(1)}, f32[1786]{0:T(1024)}, u32[]{:S(2)}) copy-start(f32[1786]{0:T(1024)} %param.16) | copy-start | bytes 21436
  0.7 2.3 %copy-start.7 = (f32[1786]{0:T(1024)S(1)}, f32[1786]{0:T(1024)}, u32[]{:S(2)}) copy-start(f32[1786]{0:T(1024)} %param.15) | copy-start | bytes 21436
  2.1 16.5 %collective-permute-start.2 = (bf16[144,16,128]{2,1,0:T(8,128)(2,1)S(1)}, bf16[144,16,128]{2,1,0:T(8,128)(2,1)S(1)}, u32[]{:S(2)}, u32[]{:S(2)}) collective-permute-start(bf16[144,16,128]{2,1,0:T(8,128)(2,1)S(1)} %get-tuple-element.31), channel_id=1, source_target_pairs={{1,2},{3,4},{5,6},{7,8},{9,10},{11,12},{13,14},{2,1},{4,3},{6,5},{... | collective-permute-start | bytes 1769480 | tf_op jit(solution)/shard_map/ppermute | solution.py:631
  3.0 11.0 %collective-permute-start = (f32[112,128]{1,0:T(8,128)S(1)}, f32[112,128]{1,0:T(8,128)S(1)}, u32[]{:S(2)}, u32[]{:S(2)}) collective-permute-start(f32[112,128]{1,0:T(8,128)S(1)} %pad_maximum_fusion.1), channel_id=1, source_target_pairs={{0,16},{16,0},{32,48},{48,32},{64,80},{80,64},{96,112},{112,96},{1... | collective-permute-start | bytes 172040 | tf_op jit(solution)/shard_map/ppermute | solution.py:611
  4.8 13.9 %collective-permute-start.3 = (bf16[144,16,128]{2,1,0:T(8,128)(2,1)S(1)}, bf16[144,16,128]{2,1,0:T(8,128)(2,1)S(1)}, u32[]{:S(2)}, u32[]{:S(2)}) collective-permute-start(bf16[144,16,128]{2,1,0:T(8,128)(2,1)S(1)} %get-tuple-element.35), channel_id=1, source_target_pairs={{0,1},{1,0},{2,3},{3,2},{4,5},{5,4},{6,7},{7,6},{8,9},{9,8},{10,11... | collective-permute-start | bytes 1769480 | tf_op jit(solution)/shard_map/ppermute | solution.py:632
  12.6 1.4 %copy-start.3 = (bf16[4,130,16,128]{3,2,1,0:T(8,128)(2,1)}, bf16[4,130,16,128]{3,2,1,0:T(8,128)(2,1)S(1)}, u32[]{:S(2)}) copy-start(bf16[4,130,16,128]{3,2,1,0:T(8,128)(2,1)S(1)} %get-tuple-element.40.cot_ref) | copy-start | bytes 6389764
  14.0 4.6 %collective-permute-start.1 = (f32[160,128]{1,0:T(8,128)S(1)}, f32[160,128]{1,0:T(8,128)S(1)}, u32[]{:S(2)}, u32[]{:S(2)}) collective-permute-start(f32[160,128]{1,0:T(8,128)S(1)} %constant_dynamic-update-slice_fusion), channel_id=1, source_target_pairs={{0,32},{16,48},{32,0},{48,16},{64,96},{80,112},{96,64},{112,80},{1... | collective-permute-start | bytes 245768 | tf_op jit(solution)/shard_map/ppermute | solution.py:611
  18.7 15.1 %copy-start = (bf16[1,1,4,128,128]{4,3,2,1,0:T(8,128)(2,1)S(1)}, bf16[1,1,4,128,128]{4,3,2,1,0:T(8,128)(2,1)}, u32[]{:S(2)}) copy-start(bf16[1,1,4,128,128]{4,3,2,1,0:T(8,128)(2,1)} %param.11) | copy-start | bytes 393220
  18.7 15.0 %copy-start.1 = (bf16[27,16,16]{0,2,1:T(8,128)(2,1)S(1)}, bf16[27,16,16]{0,2,1:T(8,128)(2,1)}, u32[]{:S(2)}) copy-start(bf16[27,16,16]{0,2,1:T(8,128)(2,1)} %param.12) | copy-start | bytes 41476
  20.5 7.4 %collective-permute-start.4 = (f32[352,128]{1,0:T(8,128)S(1)}, f32[352,128]{1,0:T(8,128)S(1)}, u32[]{:S(2)}, u32[]{:S(2)}) collective-permute-start(f32[352,128]{1,0:T(8,128)S(1)} %get-tuple-element.62), channel_id=1, source_target_pairs={{0,64},{16,80},{32,96},{48,112},{64,0},{80,16},{96,32},{112,48},{1... | collective-permute-start | bytes 540680 | tf_op jit(solution)/shard_map/ppermute | solution.py:611
  27.9 9.8 %collective-permute-start.5 = (f32[160,128]{1,0:T(8,128)S(1)}, f32[160,128]{1,0:T(8,128)S(1)}, u32[]{:S(2)}, u32[]{:S(2)}) collective-permute-start(f32[160,128]{1,0:T(8,128)S(1)} %get-tuple-element.64.token_ref), channel_id=1, source_target_pairs={{0,8},{1,9},{2,10},{3,11},{4,12},{5,13},{6,14},{7,15},{8,0},{9,1},... | collective-permute-start | bytes 245768 | tf_op jit(solution)/shard_map/ppermute | solution.py:611
  33.7 1.6 %copy-start.4 = (bf16[4,130,16,128]{3,2,1,0:T(8,128)(2,1)S(1)}, bf16[4,130,16,128]{3,2,1,0:T(8,128)(2,1)}, u32[]{:S(2)}) copy-start(bf16[4,130,16,128]{3,2,1,0:T(8,128)(2,1)} %copy-done.3) | copy-start | bytes 6389764
  37.8 6.5 %collective-permute-start.6 = (f32[160,128]{1,0:T(8,128)S(1)}, f32[160,128]{1,0:T(8,128)S(1)}, u32[]{:S(2)}, u32[]{:S(2)}) collective-permute-start(f32[160,128]{1,0:T(8,128)S(1)} %add.53.token_ref), channel_id=1, source_target_pairs={{0,4},{1,5},{2,6},{3,7},{4,0},{5,1},{6,2},{7,3},{8,12},{9,13},{10,... | collective-permute-start | bytes 245768 | tf_op jit(solution)/shard_map/ppermute | solution.py:611
  40.4 10.0 %copy-start.2 = (bf16[8,64,1408]{2,1,0:T(8,128)(2,1)S(1)}, bf16[8,64,1408]{2,1,0:T(8,128)(2,1)}, u32[]{:S(2)}) copy-start(bf16[8,64,1408]{2,1,0:T(8,128)(2,1)} %constant.37.clone.table_ref) | copy-start | bytes 4325380
  44.3 4.5 %collective-permute-start.7 = (f32[160,128]{1,0:T(8,128)S(1)}, f32[160,128]{1,0:T(8,128)S(1)}, u32[]{:S(2)}, u32[]{:S(2)}) collective-permute-start(f32[160,128]{1,0:T(8,128)S(1)} %add.54.token_ref), channel_id=1, source_target_pairs={{0,2},{1,3},{2,0},{3,1},{4,6},{5,7},{6,4},{7,5},{8,10},{9,11},{10,... | collective-permute-start | bytes 245768 | tf_op jit(solution)/shard_map/ppermute | solution.py:611
  48.8 1.4 %collective-permute-start.8 = (f32[160,128]{1,0:T(8,128)S(1)}, f32[160,128]{1,0:T(8,128)S(1)}, u32[]{:S(2)}, u32[]{:S(2)}) collective-permute-start(f32[160,128]{1,0:T(8,128)S(1)} %add.55), channel_id=1, source_target_pairs={{0,1},{1,0},{2,3},{3,2},{4,5},{5,4},{6,7},{7,6},{8,9},{9,8},{10,11... | collective-permute-start | bytes 245768 | tf_op jit(solution)/shard_map/ppermute | solution.py:611
  50.2 4.2 %collective-permute-start.9 = (f32[96,128]{1,0:T(8,128)S(1)}, f32[96,128]{1,0:T(8,128)S(1)}, u32[]{:S(2)}, u32[]{:S(2)}) collective-permute-start(f32[96,128]{1,0:T(8,128)S(1)} %slice.42), channel_id=1, source_target_pairs={{0,16},{16,0},{32,48},{48,32},{64,80},{80,64},{96,112},{112,96},{1... | collective-permute-start | bytes 147464 | tf_op jit(solution)/shard_map/ppermute | solution.py:611
  54.4 6.9 %collective-permute-start.10 = (f32[96,128]{1,0:T(8,128)S(1)}, f32[96,128]{1,0:T(8,128)S(1)}, u32[]{:S(2)}, u32[]{:S(2)}) collective-permute-start(f32[96,128]{1,0:T(8,128)S(1)} %slice_add_fusion.3.token_ref), channel_id=1, source_target_pairs={{0,32},{16,48},{32,0},{48,16},{64,96},{80,112},{96,64},{112,80},{1... | collective-permute-start | bytes 147464 | tf_op jit(solution)/shard_map/ppermute | solution.py:611

commit v3 on v2

--- a/solution.py
+++ b/solution.py
@@ -226,6 +226,28 @@
     )
 
 
+def flatten(summed, out_ref):
+    lanes = lax.broadcasted_iota(jnp.int32, (8, 128), 1) // 16
+    rows = lax.broadcasted_iota(jnp.int32, (8, 128), 0)
+    out_ref[48:56] = jnp.zeros((8, 128), F32)
+    for dx in range(3):
+        for high in range(2):
+            for half in range(2):
+                start = dx * 16 + high * 8
+                value = summed[start : start + 8, half * 128 : (half + 1) * 128]
+                for bit in (1, 2, 4):
+                    row_on, lane_on = (rows & bit) != 0, (lanes & bit) != 0
+                    down = pltpu.roll(pltpu.roll(value, bit, 0), 128 - 16 * bit, 1)
+                    up = pltpu.roll(pltpu.roll(value, 8 - bit, 0), 16 * bit, 1)
+                    moved = jnp.where(row_on, down, up)
+                    value = jnp.where(row_on == lane_on, value, moved)
+                for place in range(8):
+                    dz, dy = 2 - (half * 2 + place // 4), 2 - place % 4
+                    if dz >= 0 and dy >= 0:
+                        row = 2 * (9 * dz + 3 * dy + dx) + high
+                        out_ref[row : row + 1] = value[place : place + 1]
+
+
 def outer(odd_ref, far_ref, near_ref, act_edge, inner_ref, token_ref, grad_ref, rim_ref, total):
     edge = jnp.zeros((2, 1, 16, 128), BF)
     rim_ref[:, 0:1] = edge
@@ -255,7 +277,8 @@
         return carry
 
     lax.fori_loop(0, 4, body, 0)
-    grad_ref[...] = inner_ref[...] + aligned(total, 2, [(0, (0, 0)), (64, (2, 2))])
+    summed = inner_ref[...] + aligned(total, 2, [(0, (0, 0)), (64, (2, 2))])
+    flatten(summed, grad_ref)
 
 
 def call_outer(odd, far, near, act_edge, inner_grad, token):
@@ -264,7 +287,7 @@
         "outer",
         [SM, VM, VM, VM, VM, VM],
         [
-            jax.ShapeDtypeStruct((48, 256), F32),
+            jax.ShapeDtypeStruct((56, 128), F32),
             jax.ShapeDtypeStruct((2, 130, 16, 128), BF),
         ],
         [pltpu.VMEM((192, 256), F32)],
@@ -388,7 +411,7 @@
 
 
 def update_encoder(scale, grad_ref, state_ref, table_ref, two_ref, one_ref, bias_ref):
-    gradient = grad_ref[0:58] * scale
+    gradient = grad_ref[54:112] * scale
     new = adam(state_ref[0, 54:112], state_ref[1, 54:112], state_ref[2, 54:112], gradient)[0]
     rows = lax.broadcasted_iota(jnp.int32, (58, 128), 0)
     lanes = lax.broadcasted_iota(jnp.int32, (58, 128), 1)
@@ -429,7 +452,8 @@
     data = data_ref[0]
     lanes = lax.broadcasted_iota(jnp.int32, (16, 128), 1)
     for shard in range(8):
-        block = shards_ref[lax.bitwise_xor(data, shard)]
+        away = lax.bitwise_xor(data, shard)
+        block = shards_ref[lax.rem(away, 2) * 4 + lax.bitwise_and(away, 2) + away // 4]
         kept = 128 - 6 * shard
         for n in range(3):
             rows = block[16 * n : 16 * n + 16]
@@ -455,22 +479,9 @@
 
 
 def finish(scales, dec_ref, enc_ref, state_ref, grad_ref, work_ref):
-    lanes = lax.broadcasted_iota(jnp.int32, (16, 128), 1) // 16
-    rows = lax.broadcasted_iota(jnp.int32, (16, 128), 0) % 8
-    for dz in range(3):
-        for dy in range(3):
-            place = ((2 - dz) * 4 + 2 - dy) * 16
-            for dx in range(3):
-                block = dec_ref[dx * 16 : (dx + 1) * 16]
-                if place:
-                    block = pltpu.roll(block, 256 - place, 1)
-                block = jnp.where(lanes == 0, block[:, :128], 0.0)
-                for width in (16, 32, 64):
-                    block = block + pltpu.roll(block, width, 1)
-                block = jnp.where(lanes == rows, block, 0.0).reshape(2, 8, 128)
-                k = 9 * dz + 3 * dy + dx
-                grad_ref[2 * k : 2 * k + 2] = jnp.sum(block, axis=1) * scales[0]
-    grad_ref[54:112] = enc_ref[0:58] * scales[1]
+    rows = lax.broadcasted_iota(jnp.int32, (112, 128), 0)
+    grad_ref[...] = enc_ref[...] * scales[1]
+    grad_ref[0:56] = jnp.where(rows[:56] < 54, dec_ref[...] * scales[0], grad_ref[0:56])
     new = adam(state_ref[0], state_ref[1], state_ref[2], grad_ref[...])[0]
     work_ref[...] = new.astype(BF)
 
@@ -611,6 +622,15 @@
     return lax.ppermute(value, axis, [(i, i ^ bit) for i in range(count)])
 
 
+def four(value, first, second):
+    count = lax.axis_size("dp") * lax.axis_size("space")
+    one, two, three = [
+        lax.ppermute(value, ("dp", "space"), [(i, i ^ bits) for i in range(count)])
+        for bits in (first, second, first ^ second)
+    ]
+    return (value + one) + (two + three)
+
+
 def after(*values):
     return lax.optimization_barrier(values)
 
@@ -626,67 +646,69 @@
 
     odd = lax.rem(space, 2)
     odd_arg = odd.reshape(1).astype(jnp.int32)
-    far, near = call_edges(odd_arg, cot, vol)
-    pairs = [(i, i + 1) for i in range(1, count - 1, 2)]
-    far_in = lax.ppermute(far, "space", pairs + [(b, a) for a, b in pairs])
-    near_in = lax.ppermute(near, "space", [(i, i ^ 1) for i in range(count)])
-
     scales = (1.0 / math.sqrt(voxels), 1.0 / math.sqrt(devices))
     data_arg = data.reshape(1).astype(jnp.int32)
     inside = jnp.stack([space > 0, space < count - 1]).astype(jnp.int32)
     table = jnp.asarray(placement())
 
+    own_start = data.astype(jnp.uint32) * 1786
+    odd_arg, data_arg, own_start, inside, cot = after(odd_arg, data_arg, own_start, inside, cot)
+    far, near = call_edges(odd_arg, cot, vol)
+    pairs = [(i, i + 1) for i in range(1, count - 1, 2)]
+    far_in = lax.ppermute(far, "space", pairs + [(b, a) for a, b in pairs])
+    near_in = partner(near, "space", 1)
+
     far, enc_grad = after(far, enc_grad)
     enc = jnp.pad(enc_grad[0, 0], (0, 8192 - 7376)).reshape(64, 128)
     pad = lambda value: jnp.pad(value, (0, 2048 - 1786)).reshape(16, 128)
     state = jnp.concatenate([pad(params), pad(moment), pad(second)], axis=0)
 
-    def dp_round(grads, state, bit):
-        sent = jnp.concatenate([grads, state], axis=0)
-        got = partner(sent, "dp", bit)
-        size = grads.shape[0]
-        return grads + got[:size], jnp.concatenate([state, got[size:]], axis=0)
-
-    token = enc
-    enc, state = dp_round(enc, state, 1)
-    inner_grad, cot_rows, act_edge = call_inner(act, cot, token)
-    enc, inner_grad = after(enc, inner_grad)
-    enc, state = dp_round(enc, state, 2)
-    dec, rim_rows = call_outer(odd_arg, far_in, near_in, act_edge, inner_grad, inner_grad)
-
-    both = jnp.concatenate([enc, dec.reshape(96, 128)], axis=0)
+    def state_round(enc, state, bit):
+        return partner(jnp.concatenate([enc, state], axis=0), "dp", bit)
+
+    def joined(enc, state, got):
+        return enc + got[:64], jnp.concatenate([state, got[64:]], axis=0)
+
+    enc = enc + partner(enc, "space", 1)
+    got = state_round(enc, state, 4)
+    inner_grad, cot_rows, act_edge = call_inner(act, cot, enc)
+    got, inner_grad = after(got, inner_grad)
+    enc, state = joined(enc, state, got)
+    got = state_round(enc, state, 2)
+    dec, rim_rows = call_outer(odd_arg, far_in, near_in, act_edge, inner_grad, enc)
+    got, dec = after(got, dec)
+    enc, state = joined(enc, state, got)
+
+    both = jnp.concatenate([dec[:54], enc[:58]], axis=0)
     token = both
-    both, state = dp_round(both, state, 4)
+    both = four(both, count, 8)
     cells, kernel = call_prepare(
         odd_arg, far_in, near_in, vol, dec_weight.transpose(1, 2, 0), token
     )
+    grad_input = call_input_grad(0, kernel, cot_rows, rim_rows, token)
+    both, grad_input = after(both, grad_input)
     token = both
-    both = both + partner(both, "space", 8)
-    grad_input = call_input_grad(0, kernel, cot_rows, rim_rows, token)
-    token = both
+    both = four(both, 2, 4)
+    state = jnp.concatenate([state, partner(state, "dp", 1)], axis=0)
+    grad_input = call_input_grad(1, kernel, cot_rows, rim_rows, token, grad_input)
     both, grad_input = after(both, grad_input)
-    both = both + partner(both, "space", 4)
-    grad_input = call_input_grad(1, kernel, cot_rows, rim_rows, token, grad_input)
-    token = both
-    both, grad_input = after(both, grad_input)
-    both = both + partner(both, "space", 2)
     state = call_flat_state(data_arg, state.reshape(8, 48, 128), token)
-    both, state = after(both, state)
-    both = both + partner(both, "space", 1)
-    enc, dec = both[:64], both[64:]
-
-    two, one, bias = call_update_encoder(scales[1], enc, state, table)
-    first = call_first_layer(inside, one, cells, enc)
-    dec = dec + partner(dec, "dp", 1)
+
+    two, one, bias = call_update_encoder(scales[1], both, state, table)
+    first = call_first_layer(inside, one, cells, both)
+    dec = both[:56]
+    dec = dec + partner(dec, "dp", 2)
     token = dec
     dec, first = after(dec, first)
-    dec = dec + partner(dec, "dp", 2)
+    dec = dec + partner(dec, "dp", 4)
     encoded = call_second_layer(0, two, bias, first, token)
+    dec, encoded = after(dec, encoded)
+    dec = dec + partner(dec, "space", 1)
     encoded = call_second_layer(1, two, bias, first, token, encoded)
 
-    flat, working = call_finish(scales, dec.reshape(48, 256), enc, state)
+    flat, working = call_finish(scales, dec, both, state)
     working = working.reshape(112 * 128)[:14288]
-    own = lax.dynamic_slice_in_dim(flat.reshape(112 * 128), data * 1786, 1786, 0)
+    own = lax.dynamic_slice(flat.reshape(112 * 128), (own_start,), (1786,))
     own = adam(params, moment, second, own)
     return (grad_input[None], own[0], own[1], own[2], working, encoded[None])
 

time: 63.3 us -> 53.9 us (0.85)
  the two profiles are of different devices: /device:TPU:0 before, /device:TPU:1 now
where the time goes in v3:
time: 53.9 us; the launch traced here: 53.8 us
  starting transfers between devices  27.6 us (51%)
  Pallas kernels  22.6 us (42%)
  waiting for transfers between devices  1.56 us (3%)
  between operations  0.99 us (2%)
  other arithmetic  0.94 us (2%)
    ppermute x8, starting transfers between devices, partner(): return lax.ppermute(value, axis, [(i, i ^ bit) for i in range(count)])  15 us
    ppermute x6, starting transfers between devices, four(): lax.ppermute(value, ('dp', 'space'), [(i, i ^ bits) for i in range(count)])  8.11 us
    pallas_call x1, Pallas kernels, call_inner(): kernel_call(inner, 'inner', [HBM, HBM, VM], [jax.ShapeDtypeStruct((48, 25...  5.32 us
    pallas_call x2, Pallas kernels, call_second_layer(): kernel_call(functools.partial(second_layer, part), f'second_layer_{part}'...  5.01 us
    pallas_call x2, Pallas kernels, call_input_grad(): kernel_call(functools.partial(input_grad, part), f'input_grad_{part}', [V...  4.95 us
    ppermute x1, starting transfers between devices, local(): far_in = lax.ppermute(far, 'space', pairs + [(b, a) for a, b in pairs])  4.51 us
    pallas_call x1, Pallas kernels, call_outer(): kernel_call(outer, 'outer', [SM, VM, VM, VM, VM, VM], [jax.ShapeDtypeStru...  1.89 us
    pallas_call x1, Pallas kernels, call_first_layer(): kernel_call(first_layer, 'first_layer', [SM, VM, VM, VM], jax.ShapeDtypeS...  1.7 us
  transfers between devices with their start and end apart: 15, of which 3 were waited for; matrix products, arithmetic and copies ran while one was open for 0% of the time, Pallas kernels for 38%

profile of v3, /device:TPU:1, one launch (start us, length us, event | category | flops | bytes accessed | tf_op | source)
XLA Modules:
  0.0 53.8 jit_solution(15605955324323196296)
XLA Ops:
  0.6 0.1 add_convert_fusion.inside_ref
  0.7 1.5 %edges.1 = (bf16[144,16,128]{2,1,0:T(8,128)(2,1)S(1)}, bf16[144,16,128]{2,1,0:T(8,128)(2,1)S(1)}) custom-call(s32[1]{0:T(128)} %bitcast.odd_ref, bf16[16,4,128,128]{3,2,1,0:T(8,128)(2,1)} %bitcast.52, bf16[4,128,128]{2,1,0:T(8,128)(2,1)} %bitcast.49), custom_call_target="tpu_custom_call" | custom-call | flops 1495000064 | bytes 4680000 | tf_op jit(solution)/shard_map/edges/pallas_call | solution.py:99
  2.2 4.5 %collective-permute-start.3 = (bf16[144,16,128]{2,1,0:T(8,128)(2,1)S(1)}, bf16[144,16,128]{2,1,0:T(8,128)(2,1)S(1)}, u32[]{:S(2)}, u32[]{:S(2)}) collective-permute-start(bf16[144,16,128]{2,1,0:T(8,128)(2,1)S(1)} %get-tuple-element.40), channel_id=1, source_target_pairs={{1,2},{3,4},{5,6},{7,8},{9,10},{11,12},{13,14},{2,1},{4,3},{6,5},{... | collective-permute-start | bytes 1769480 | tf_op jit(solution)/shard_map/ppermute | solution.py:658
  6.8 0.1 collective-permute-start
  6.9 0.5 collective-permute-start.4
  7.5 0.7 %collective-permute-done = f32[64,128]{1,0:T(8,128)S(1)} collective-permute-done((f32[64,128]{1,0:T(8,128)S(1)}, f32[64,128]{1,0:T(8,128)S(1)}, u32[]{:S(2)}, u32[]{:S(2)}) %collective-permute-start) | collective-permute-done | bytes 32800 | tf_op jit(solution)/shard_map/ppermute | solution.py:622
  8.1 3.7 %collective-permute-start.1 = (f32[112,128]{1,0:T(8,128)S(1)}, f32[112,128]{1,0:T(8,128)S(1)}, u32[]{:S(2)}, u32[]{:S(2)}) collective-permute-start(f32[112,128]{1,0:T(8,128)S(1)} %pad_maximum_fusion), channel_id=1, source_target_pairs={{0,64},{16,80},{32,96},{48,112},{64,0},{80,16},{96,32},{112,48},{1... | collective-permute-start | bytes 172040 | tf_op jit(solution)/shard_map/ppermute | solution.py:622
  11.8 5.3 %inner.1 = (f32[48,256]{1,0:T(8,128)S(1)}, bf16[4,130,16,128]{3,2,1,0:T(8,128)(2,1)S(1)}, bf16[2,3,128,16,128]{4,3,2,1,0:T(8,128)(2,1)S(1)}) custom-call(bf16[16,4,128,128]{3,2,1,0:T(8,128)(2,1)} %bitcast.54, bf16[16,4,128,128]{3,2,1,0:T(8,128)(2,1)} %bitcast.53, f32[64,128]{1,0:T(8,128)S(1)} %fusion.1.token_ref), custom_call_target="tpu_custom_call" | custom-call | flops 4600000000 | bytes 14400000 | tf_op jit(solution)/shard_map/inner/pallas_call | solution.py:203
  17.2 0.8 %collective-permute-start.2 = (f32[160,128]{1,0:T(8,128)S(1)}, f32[160,128]{1,0:T(8,128)S(1)}, u32[]{:S(2)}, u32[]{:S(2)}) collective-permute-start(f32[160,128]{1,0:T(8,128)S(1)} %get-tuple-element.79), channel_id=1, source_target_pairs={{0,32},{16,48},{32,0},{48,16},{64,96},{80,112},{96,64},{112,80},{1... | collective-permute-start | bytes 245768 | tf_op jit(solution)/shard_map/ppermute | solution.py:622
  18.1 1.9 %outer.1 = (f32[56,128]{1,0:T(8,128)S(1)}, bf16[2,130,16,128]{3,2,1,0:T(8,128)(2,1)S(1)}) custom-call(s32[1]{0:T(128)} %bitcast.odd_ref, bf16[144,16,128]{2,1,0:T(8,128)(2,1)S(1)} %collective-permute-done.3.far_ref, bf16[144,16,128]{2,1,0:T(8,128)(2,1)S(1)} %collective-permute-done.4.near_ref, bf16[2,3,128,16,128]{4,3,2,1,0:T(8,128)(2,1)S(1)} %get-tuple-element.45.act_edge, ...), custom_call_target="tpu_custom_call" | custom-call | flops 2875000064 | bytes 9000000 | tf_op jit(solution)/shard_map/outer/pallas_call | solution.py:285
  20.0 0.6 %collective-permute-done.2 = f32[160,128]{1,0:T(8,128)S(1)} collective-permute-done((f32[160,128]{1,0:T(8,128)S(1)}, f32[160,128]{1,0:T(8,128)S(1)}, u32[]{:S(2)}, u32[]{:S(2)}) %collective-permute-start.2) | collective-permute-done | bytes 81952 | tf_op jit(solution)/shard_map/ppermute | solution.py:622
  20.6 3.5 %collective-permute-start.6 = (f32[112,128]{1,0:T(8,128)S(1)}, f32[112,128]{1,0:T(8,128)S(1)}, u32[]{:S(2)}, u32[]{:S(2)}) collective-permute-start(f32[112,128]{1,0:T(8,128)S(1)} %pad_maximum_fusion.1.token_ref), channel_id=1, source_target_pairs={{0,8},{1,9},{2,10},{3,11},{4,12},{5,13},{6,14},{7,15},{8,0},{9,1},... | collective-permute-start | bytes 172040 | tf_op jit(solution)/shard_map/ppermute | solution.py:628
  24.1 0.8 %collective-permute-start.7 = (f32[112,128]{1,0:T(8,128)S(1)}, f32[112,128]{1,0:T(8,128)S(1)}, u32[]{:S(2)}, u32[]{:S(2)}) collective-permute-start(f32[112,128]{1,0:T(8,128)S(1)} %pad_maximum_fusion.1.token_ref), channel_id=1, source_target_pairs={{0,24},{1,25},{2,26},{3,27},{4,28},{5,29},{6,30},{7,31},{8,16},{9,... | collective-permute-start | bytes 172040 | tf_op jit(solution)/shard_map/ppermute | solution.py:628
  25.0 0.5 collective-permute-start.5
  25.5 1.1 %collective-permute-start.12 = (f32[192,128]{1,0:T(8,128)S(1)}, f32[192,128]{1,0:T(8,128)S(1)}, u32[]{:S(2)}, u32[]{:S(2)}) collective-permute-start(f32[192,128]{1,0:T(8,128)S(1)} %get-tuple-element.75), channel_id=1, source_target_pairs={{0,16},{16,0},{32,48},{48,32},{64,80},{80,64},{96,112},{112,96},{1... | collective-permute-start | bytes 294920 | tf_op jit(solution)/shard_map/ppermute | solution.py:622
  26.5 0.9 %prepare.1 = (bf16[2,3,8,8,16,128]{5,4,3,2,1,0:T(8,128)(2,1)S(1)}, bf16[192,256]{1,0:T(8,128)(2,1)S(1)}) custom-call(s32[1]{0:T(128)} %bitcast.odd_ref, bf16[144,16,128]{2,1,0:T(8,128)(2,1)S(1)} %collective-permute-done.3.far_ref, bf16[144,16,128]{2,1,0:T(8,128)(2,1)S(1)} %collective-permute-done.4.near_ref, bf16[4,128,128]{2,1,0:T(8,128)(2,1)S(1)} %bitcast.50, ...), custom_call_target="tpu_custom_call" | custom-call | flops 1495000064 | bytes 4680000 | tf_op jit(solution)/shard_map/prepare/pallas_call | solution.py:537
  27.4 2.5 %input_grad_0.1.refs_0_ = bf16[16,4,128,128]{3,2,1,0:T(8,128)(2,1)} custom-call(bf16[192,256]{1,0:T(8,128)(2,1)S(1)} %get-tuple-element.50.kernel_ref, bf16[4,130,16,128]{3,2,1,0:T(8,128)(2,1)S(1)} %get-tuple-element.51.cot_ref, bf16[2,130,16,128]{3,2,1,0:T(8,128)(2,1)S(1)} %get-tuple-element.52.rim_ref, f32[112,128]{1,0:T(8,128)S(1)} %pad_maximum_fusion.1.token_ref), custom_call_target="tpu_custom_call" | custom-call | flops 2529999872 | bytes 7920000 | tf_op jit(solution)/shard_map/input_grad_0/pallas_call | solution.py:375
  30.0 2.0 %collective-permute-start.9 = (f32[112,128]{1,0:T(8,128)S(1)}, f32[112,128]{1,0:T(8,128)S(1)}, u32[]{:S(2)}, u32[]{:S(2)}) collective-permute-start(f32[112,128]{1,0:T(8,128)S(1)} %add_add_fusion.1.token_ref), channel_id=1, source_target_pairs={{0,4},{1,5},{2,6},{3,7},{4,0},{5,1},{6,2},{7,3},{8,12},{9,13},{10,... | collective-permute-start | bytes 172040 | tf_op jit(solution)/shard_map/ppermute | solution.py:628
  31.9 1.2 %collective-permute-start.10 = (f32[112,128]{1,0:T(8,128)S(1)}, f32[112,128]{1,0:T(8,128)S(1)}, u32[]{:S(2)}, u32[]{:S(2)}) collective-permute-start(f32[112,128]{1,0:T(8,128)S(1)} %add_add_fusion.1.token_ref), channel_id=1, source_target_pairs={{0,6},{1,7},{2,4},{3,5},{4,2},{5,3},{6,0},{7,1},{8,14},{9,15},{10,... | collective-permute-start | bytes 172040 | tf_op jit(solution)/shard_map/ppermute | solution.py:628
  33.1 0.2 collective-permute-start.8
  33.3 2.5 %input_grad_1.1 = bf16[16,4,128,128]{3,2,1,0:T(8,128)(2,1)} custom-call(bf16[192,256]{1,0:T(8,128)(2,1)S(1)} %get-tuple-element.50.kernel_ref, bf16[4,130,16,128]{3,2,1,0:T(8,128)(2,1)S(1)} %get-tuple-element.51.cot_ref, bf16[2,130,16,128]{3,2,1,0:T(8,128)(2,1)S(1)} %get-tuple-element.52.rim_ref, ...), custom_call_target="tpu_custom_call", output_to_operand_aliasing={{}: (4, {})} | custom-call | flops 2529999872 | bytes 7920000 | tf_op jit(solution)/shard_map/input_grad_1/pallas_call | solution.py:375
  35.8 0.2 flat_state.1.state_ref
  35.9 0.2 collective-permute-done.10
  36.2 0.8 %collective-permute-start.11 = (f32[56,128]{1,0:T(8,128)S(1)}, f32[56,128]{1,0:T(8,128)S(1)}, u32[]{:S(2)}, u32[]{:S(2)}) collective-permute-start(f32[56,128]{1,0:T(8,128)S(1)} %slice.29), channel_id=1, source_target_pairs={{0,32},{16,48},{32,0},{48,16},{64,96},{80,112},{96,64},{112,80},{1... | collective-permute-start | bytes 86024 | tf_op jit(solution)/shard_map/ppermute | solution.py:622
  37.0 0.6 %update_encoder.1 = (bf16[192,256]{1,0:T(8,128)(2,1)S(1)}, bf16[256,256]{1,0:T(8,128)(2,1)S(1)}, f32[16,128]{1,0:T(8,128)S(1)}) custom-call(f32[112,128]{1,0:T(8,128)S(1)} %add_add_fusion.grad_ref.token_ref.enc_ref, f32[3,112,128]{2,1,0:T(8,128)S(1)} %flat_state.1.state_ref, bf16[8,64,1408]{2,1,0:T(8,128)(2,1)S(1)} %copy-done.2), custom_call_target="tpu_custom_call" | custom-call | flops 690000000 | bytes 2160000 | tf_op jit(solution)/shard_map/update_encoder/pallas_call | solution.py:438
  37.6 1.7 %first_layer.1.first = bf16[6,130,16,128]{3,2,1,0:T(8,128)(2,1)S(1)} custom-call(s32[2]{0:T(128)S(1)} %add_convert_fusion.inside_ref, bf16[256,256]{1,0:T(8,128)(2,1)S(1)} %get-tuple-element.59.one_ref, bf16[2,3,8,8,16,128]{5,4,3,2,1,0:T(8,128)(2,1)S(1)} %get-tuple-element.60.cells_ref, f32[112,128]{1,0:T(8,128)S(1)} %add_add_fusion.grad_ref.token_ref.enc_ref), custom_call_target="tpu_custom_call" | custom-call | flops 1724999936 | bytes 5400000 | tf_op jit(solution)/shard_map/first_layer/pallas_call | solution.py:590
  39.3 3.0 %collective-permute-start.13 = (f32[56,128]{1,0:T(8,128)S(1)}, f32[56,128]{1,0:T(8,128)S(1)}, u32[]{:S(2)}, u32[]{:S(2)}) collective-permute-start(f32[56,128]{1,0:T(8,128)S(1)} %slice_add_fusion.2.token_ref), channel_id=1, source_target_pairs={{0,64},{16,80},{32,96},{48,112},{64,0},{80,16},{96,32},{112,48},{1... | collective-permute-start | bytes 86024 | tf_op jit(solution)/shard_map/ppermute | solution.py:622
  42.3 2.5 %second_layer_0.1.refs_0_ = bf16[16,4,128,128]{3,2,1,0:T(8,128)(2,1)} custom-call(bf16[192,256]{1,0:T(8,128)(2,1)S(1)} %get-tuple-element.62.two_ref, f32[16,128]{1,0:T(8,128)S(1)} %get-tuple-element.63.bias_ref, bf16[6,130,16,128]{3,2,1,0:T(8,128)(2,1)S(1)} %first_layer.1.first, f32[56,128]{1,0:T(8,128)S(1)} %slice_add_fusion.2.token_ref), custom_call_target="tpu_custom_call" | custom-call | flops 2529999872 | bytes 7920000 | tf_op jit(solution)/shard_map/second_layer_0/pallas_call | solution.py:608
  44.9 5.0 %collective-permute-start.14 = (f32[56,128]{1,0:T(8,128)S(1)}, f32[56,128]{1,0:T(8,128)S(1)}, u32[]{:S(2)}, u32[]{:S(2)}) collective-permute-start(f32[56,128]{1,0:T(8,128)S(1)} %add.66), channel_id=1, source_target_pairs={{0,1},{1,0},{2,3},{3,2},{4,5},{5,4},{6,7},{7,6},{8,9},{9,8},{10,11... | collective-permute-start | bytes 86024 | tf_op jit(solution)/shard_map/ppermute | solution.py:622
  49.9 2.5 %second_layer_1.1 = bf16[16,4,128,128]{3,2,1,0:T(8,128)(2,1)} custom-call(bf16[192,256]{1,0:T(8,128)(2,1)S(1)} %get-tuple-element.62.two_ref, f32[16,128]{1,0:T(8,128)S(1)} %get-tuple-element.63.bias_ref, bf16[6,130,16,128]{3,2,1,0:T(8,128)(2,1)S(1)} %first_layer.1.first, f32[56,128]{1,0:T(8,128)S(1)} %slice_add_fusion.2.token_ref, ...), custom_call_target="tpu_custom_call", output_to_operand_aliasing={{}: (4, {})} | custom-call | flops 2529999872 | bytes 7920000 | tf_op jit(solution)/shard_map/second_layer_1/pallas_call | solution.py:608
  52.4 0.7 %finish.1 = (f32[112,128]{1,0:T(8,128)S(1)}, bf16[112,128]{1,0:T(8,128)(2,1)}) custom-call(f32[56,128]{1,0:T(8,128)S(1)} %add.67.dec_ref, f32[112,128]{1,0:T(8,128)S(1)} %add_add_fusion.grad_ref.token_ref.enc_ref, f32[3,112,128]{2,1,0:T(8,128)S(1)} %flat_state.1.state_ref), custom_call_target="tpu_custom_call" | custom-call | flops 1150000000 | bytes 3600000 | tf_op jit(solution)/shard_map/finish/pallas_call | solution.py:490
  53.1 0.7 %divide_subtract_fusion = (f32[1786]{0:T(1024)}, f32[1786]{0:T(1024)}, f32[1786]{0:T(1024)}) fusion(f32[1786]{0:T(1024)S(1)} %copy-done.3, f32[14336]{0:T(1024)S(1)} %bitcast.47, u32[]{:T(128)S(6)} %mul.36, f32[1786]{0:T(1024)S(1)} %copy-done.5, f32[1786]{0:T(1024)S(1)} %copy-done.4), kind=kLoop, calls=%fused_computation.25 | loop fusion | flops 19646 | bytes 50012 | tf_op jit(solution)/shard_map/sub | solution.py:409
  (48 shorter events, 0.3 us)
Async XLA Ops:
  0.7 6.0 %copy-start.6 = (f32[1,1,7376]{2,1,0:T(1,128)S(1)}, f32[1,1,7376]{2,1,0:T(1,128)}, u32[]{:S(2)}) copy-start(f32[1,1,7376]{2,1,0:T(1,128)} %param.13) | copy-start | bytes 88516
  0.7 6.7 %copy-start.4 = (f32[1786]{0:T(1024)S(1)}, f32[1786]{0:T(1024)}, u32[]{:S(2)}) copy-start(f32[1786]{0:T(1024)} %param.16) | copy-start | bytes 21436
  0.7 6.7 %copy-start.5 = (f32[1786]{0:T(1024)S(1)}, f32[1786]{0:T(1024)}, u32[]{:S(2)}) copy-start(f32[1786]{0:T(1024)} %param.15) | copy-start | bytes 21436
  0.7 6.7 %copy-start.3 = (f32[1786]{0:T(1024)S(1)}, f32[1786]{0:T(1024)}, u32[]{:S(2)}) copy-start(f32[1786]{0:T(1024)} %param.14) | copy-start | bytes 21436
  2.2 15.8 %collective-permute-start.3 = (bf16[144,16,128]{2,1,0:T(8,128)(2,1)S(1)}, bf16[144,16,128]{2,1,0:T(8,128)(2,1)S(1)}, u32[]{:S(2)}, u32[]{:S(2)}) collective-permute-start(bf16[144,16,128]{2,1,0:T(8,128)(2,1)S(1)} %get-tuple-element.40), channel_id=1, source_target_pairs={{1,2},{3,4},{5,6},{7,8},{9,10},{11,12},{13,14},{2,1},{4,3},{6,5},{... | collective-permute-start | bytes 1769480 | tf_op jit(solution)/shard_map/ppermute | solution.py:658
  6.8 1.3 %collective-permute-start = (f32[64,128]{1,0:T(8,128)S(1)}, f32[64,128]{1,0:T(8,128)S(1)}, u32[]{:S(2)}, u32[]{:S(2)}) collective-permute-start(f32[64,128]{1,0:T(8,128)S(1)} %pad_bitcast_fusion), channel_id=1, source_target_pairs={{0,1},{1,0},{2,3},{3,2},{4,5},{5,4},{6,7},{7,6},{8,9},{9,8},{10,11... | collective-permute-start | bytes 98312 | tf_op jit(solution)/shard_map/ppermute | solution.py:622
  6.9 11.1 %collective-permute-start.4 = (bf16[144,16,128]{2,1,0:T(8,128)(2,1)S(1)}, bf16[144,16,128]{2,1,0:T(8,128)(2,1)S(1)}, u32[]{:S(2)}, u32[]{:S(2)}) collective-permute-start(bf16[144,16,128]{2,1,0:T(8,128)(2,1)S(1)} %get-tuple-element.44), channel_id=1, source_target_pairs={{0,1},{1,0},{2,3},{3,2},{4,5},{5,4},{6,7},{7,6},{8,9},{9,8},{10,11... | collective-permute-start | bytes 1769480 | tf_op jit(solution)/shard_map/ppermute | solution.py:622
  8.1 9.0 %collective-permute-start.1 = (f32[112,128]{1,0:T(8,128)S(1)}, f32[112,128]{1,0:T(8,128)S(1)}, u32[]{:S(2)}, u32[]{:S(2)}) collective-permute-start(f32[112,128]{1,0:T(8,128)S(1)} %pad_maximum_fusion), channel_id=1, source_target_pairs={{0,64},{16,80},{32,96},{48,112},{64,0},{80,16},{96,32},{112,48},{1... | collective-permute-start | bytes 172040 | tf_op jit(solution)/shard_map/ppermute | solution.py:622
  17.2 3.4 %collective-permute-start.2 = (f32[160,128]{1,0:T(8,128)S(1)}, f32[160,128]{1,0:T(8,128)S(1)}, u32[]{:S(2)}, u32[]{:S(2)}) collective-permute-start(f32[160,128]{1,0:T(8,128)S(1)} %get-tuple-element.79), channel_id=1, source_target_pairs={{0,32},{16,48},{32,0},{48,16},{64,96},{80,112},{96,64},{112,80},{1... | collective-permute-start | bytes 245768 | tf_op jit(solution)/shard_map/ppermute | solution.py:622
  18.0 8.5 %copy-start = (bf16[1,1,4,128,128]{4,3,2,1,0:T(8,128)(2,1)S(1)}, bf16[1,1,4,128,128]{4,3,2,1,0:T(8,128)(2,1)}, u32[]{:S(2)}) copy-start(bf16[1,1,4,128,128]{4,3,2,1,0:T(8,128)(2,1)} %param.11) | copy-start | bytes 393220
  18.1 8.5 %copy-start.1 = (bf16[27,16,16]{0,2,1:T(8,128)(2,1)S(1)}, bf16[27,16,16]{0,2,1:T(8,128)(2,1)}, u32[]{:S(2)}) copy-start(bf16[27,16,16]{0,2,1:T(8,128)(2,1)} %param.12) | copy-start | bytes 41476
  20.6 9.3 %collective-permute-start.6 = (f32[112,128]{1,0:T(8,128)S(1)}, f32[112,128]{1,0:T(8,128)S(1)}, u32[]{:S(2)}, u32[]{:S(2)}) collective-permute-start(f32[112,128]{1,0:T(8,128)S(1)} %pad_maximum_fusion.1.token_ref), channel_id=1, source_target_pairs={{0,8},{1,9},{2,10},{3,11},{4,12},{5,13},{6,14},{7,15},{8,0},{9,1},... | collective-permute-start | bytes 172040 | tf_op jit(solution)/shard_map/ppermute | solution.py:628
  24.1 5.8 %collective-permute-start.7 = (f32[112,128]{1,0:T(8,128)S(1)}, f32[112,128]{1,0:T(8,128)S(1)}, u32[]{:S(2)}, u32[]{:S(2)}) collective-permute-start(f32[112,128]{1,0:T(8,128)S(1)} %pad_maximum_fusion.1.token_ref), channel_id=1, source_target_pairs={{0,24},{1,25},{2,26},{3,27},{4,28},{5,29},{6,30},{7,31},{8,16},{9,... | collective-permute-start | bytes 172040 | tf_op jit(solution)/shard_map/ppermute | solution.py:628
  25.0 5.0 %collective-permute-start.5 = (f32[112,128]{1,0:T(8,128)S(1)}, f32[112,128]{1,0:T(8,128)S(1)}, u32[]{:S(2)}, u32[]{:S(2)}) collective-permute-start(f32[112,128]{1,0:T(8,128)S(1)} %pad_maximum_fusion.1.token_ref), channel_id=1, source_target_pairs={{0,16},{1,17},{2,18},{3,19},{4,20},{5,21},{6,22},{7,23},{8,24},{9,... | collective-permute-start | bytes 172040 | tf_op jit(solution)/shard_map/ppermute | solution.py:628
  25.5 10.3 %collective-permute-start.12 = (f32[192,128]{1,0:T(8,128)S(1)}, f32[192,128]{1,0:T(8,128)S(1)}, u32[]{:S(2)}, u32[]{:S(2)}) collective-permute-start(f32[192,128]{1,0:T(8,128)S(1)} %get-tuple-element.75), channel_id=1, source_target_pairs={{0,16},{16,0},{32,48},{48,32},{64,80},{80,64},{96,112},{112,96},{1... | collective-permute-start | bytes 294920 | tf_op jit(solution)/shard_map/ppermute | solution.py:622
  30.0 7.1 %copy-start.2 = (bf16[8,64,1408]{2,1,0:T(8,128)(2,1)S(1)}, bf16[8,64,1408]{2,1,0:T(8,128)(2,1)}, u32[]{:S(2)}) copy-start(bf16[8,64,1408]{2,1,0:T(8,128)(2,1)} %constant.35.clone.table_ref) | copy-start | bytes 4325380
  30.0 6.0 %collective-permute-start.9 = (f32[112,128]{1,0:T(8,128)S(1)}, f32[112,128]{1,0:T(8,128)S(1)}, u32[]{:S(2)}, u32[]{:S(2)}) collective-permute-start(f32[112,128]{1,0:T(8,128)S(1)} %add_add_fusion.1.token_ref), channel_id=1, source_target_pairs={{0,4},{1,5},{2,6},{3,7},{4,0},{5,1},{6,2},{7,3},{8,12},{9,13},{10,... | collective-permute-start | bytes 172040 | tf_op jit(solution)/shard_map/ppermute | solution.py:628
  31.9 4.2 %collective-permute-start.10 = (f32[112,128]{1,0:T(8,128)S(1)}, f32[112,128]{1,0:T(8,128)S(1)}, u32[]{:S(2)}, u32[]{:S(2)}) collective-permute-start(f32[112,128]{1,0:T(8,128)S(1)} %add_add_fusion.1.token_ref), channel_id=1, source_target_pairs={{0,6},{1,7},{2,4},{3,5},{4,2},{5,3},{6,0},{7,1},{8,14},{9,15},{10,... | collective-permute-start | bytes 172040 | tf_op jit(solution)/shard_map/ppermute | solution.py:628
  33.1 3.1 %collective-permute-start.8 = (f32[112,128]{1,0:T(8,128)S(1)}, f32[112,128]{1,0:T(8,128)S(1)}, u32[]{:S(2)}, u32[]{:S(2)}) collective-permute-start(f32[112,128]{1,0:T(8,128)S(1)} %add_add_fusion.1.token_ref), channel_id=1, source_target_pairs={{0,2},{1,3},{2,0},{3,1},{4,6},{5,7},{6,4},{7,5},{8,10},{9,11},{10,... | collective-permute-start | bytes 172040 | tf_op jit(solution)/shard_map/ppermute | solution.py:628
  36.2 3.1 %collective-permute-start.11 = (f32[56,128]{1,0:T(8,128)S(1)}, f32[56,128]{1,0:T(8,128)S(1)}, u32[]{:S(2)}, u32[]{:S(2)}) collective-permute-start(f32[56,128]{1,0:T(8,128)S(1)} %slice.29), channel_id=1, source_target_pairs={{0,32},{16,48},{32,0},{48,16},{64,96},{80,112},{96,64},{112,80},{1... | collective-permute-start | bytes 86024 | tf_op jit(solution)/shard_map/ppermute | solution.py:622
  39.3 5.5 %collective-permute-start.13 = (f32[56,128]{1,0:T(8,128)S(1)}, f32[56,128]{1,0:T(8,128)S(1)}, u32[]{:S(2)}, u32[]{:S(2)}) collective-permute-start(f32[56,128]{1,0:T(8,128)S(1)} %slice_add_fusion.2.token_ref), channel_id=1, source_target_pairs={{0,64},{16,80},{32,96},{48,112},{64,0},{80,16},{96,32},{112,48},{1... | collective-permute-start | bytes 86024 | tf_op jit(solution)/shard_map/ppermute | solution.py:622
  44.9 7.6 %collective-permute-start.14 = (f32[56,128]{1,0:T(8,128)S(1)}, f32[56,128]{1,0:T(8,128)S(1)}, u32[]{:S(2)}, u32[]{:S(2)}) collective-permute-start(f32[56,128]{1,0:T(8,128)S(1)} %add.66), channel_id=1, source_target_pairs={{0,1},{1,0},{2,3},{3,2},{4,5},{5,4},{6,7},{7,6},{8,9},{9,8},{10,11... | collective-permute-start | bytes 86024 | tf_op jit(solution)/shard_map/ppermute | solution.py:622

commit v4 on v3

--- a/solution.py
+++ b/solution.py
@@ -43,7 +43,6 @@
 
 VM = pl.BlockSpec(memory_space=pltpu.VMEM)
 HBM = pl.BlockSpec(memory_space=pltpu.HBM)
-SM = pl.BlockSpec(memory_space=pltpu.SMEM)
 
 
 def kernel_call(
@@ -70,8 +69,12 @@
     return pltpu.with_memory_space_constraint(value, pltpu.HBM)
 
 
-def edges(odd_ref, cot_ref, vol_ref, far_ref, near_ref, planes, slabs, sems):
-    odd = odd_ref[0]
+def odd_place():
+    return lax.rem(lax.axis_index("space"), 2)
+
+
+def edges(cot_ref, vol_ref, far_ref, near_ref, planes, slabs, sems):
+    odd = odd_place()
     outs = (far_ref, near_ref)
     sides = (odd, 1 - odd)
     copies = []
@@ -94,12 +97,12 @@
         outs[n][128:144] = slabs[n].reshape(16, 16, 128)
 
 
-def call_edges(odd, cot, vol):
+def call_edges(cot, vol):
     shape = jax.ShapeDtypeStruct((144, 16, 128), BF)
     return kernel_call(
         edges,
         "edges",
-        [SM, HBM, HBM],
+        [HBM, HBM],
         [shape, shape],
         [
             pltpu.VMEM((2, 16, 128, 128), BF),
@@ -107,7 +110,7 @@
             pltpu.SemaphoreType.DMA((4,)),
         ],
         1.3,
-    )(odd, in_hbm(cot), in_hbm(vol))
+    )(in_hbm(cot), in_hbm(vol))
 
 
 def lateral(cells):
@@ -136,27 +139,13 @@
     return jnp.concatenate(out, axis=0)
 
 
-def inner(
-    act_hbm, cot_hbm, token_ref, grad_ref, cot_rows, act_edge, act_ref, cot_ref, act_rows, total, sems
-):
-    def copies(step):
-        rows = pl.ds(pl.multiple_of(step * 16, 16), 16)
-        return [
-            pltpu.make_async_copy(source.at[:, :, rows], target.at[:, :, rows], sems.at[n, step])
-            for n, (source, target) in enumerate(((act_hbm, act_ref), (cot_hbm, cot_ref)))
-        ]
-
-    for step in range(8):
-        for copy in copies(step):
-            copy.start()
+def inner(act_ref, cot_ref, token_ref, grad_ref, cot_rows, act_edge, act_rows, total):
     edge = jnp.zeros((4, 1, 16, 128), BF)
     cot_rows[:, 0:1] = edge
     cot_rows[:, 129:130] = edge
     total[...] = jnp.zeros_like(total)
 
     def turn(step):
-        for copy in copies(step):
-            copy.wait()
         rows = pl.ds(pl.multiple_of(step * 16, 16), 16)
         for z in range(4):
             cot_rows[z, pl.ds(step * 16 + 1, 16)] = jnp.swapaxes(cot_ref[:, z, rows], 0, 1)
@@ -184,12 +173,13 @@
     turn(0)
     turn(1)
 
-    def body(step, carry):
-        turn(step + 2)
-        gather(step)
+    def body(pair, carry):
+        for step in (2 * pair, 2 * pair + 1):
+            turn(step + 2)
+            gather(step)
         return carry
 
-    lax.fori_loop(0, 6, body, 0)
+    lax.fori_loop(0, 3, body, 0)
     gather(6)
     gather(7)
     grad_ref[...] = aligned(
@@ -203,21 +193,18 @@
     return kernel_call(
         inner,
         "inner",
-        [HBM, HBM, VM],
+        [VM, VM, VM],
         [
             jax.ShapeDtypeStruct((48, 256), F32),
             jax.ShapeDtypeStruct((4, 130, 16, 128), BF),
             jax.ShapeDtypeStruct((2, 3, 128, 16, 128), BF),
         ],
         [
-            pltpu.VMEM((16, 4, 128, 128), BF),
-            pltpu.VMEM((16, 4, 128, 128), BF),
             pltpu.VMEM((3, 4, 128, 16, 128), BF),
             pltpu.VMEM((384, 256), F32),
-            pltpu.SemaphoreType.DMA((2, 8)),
         ],
         4.0,
-    )(in_hbm(act), in_hbm(cot), token)
+    )(act, cot, token)
 
 
 def window(planes, base):
@@ -248,18 +235,18 @@
                         out_ref[row : row + 1] = value[place : place + 1]
 
 
-def outer(odd_ref, far_ref, near_ref, act_edge, inner_ref, token_ref, grad_ref, rim_ref, total):
+def outer(far_ref, near_ref, act_edge, inner_ref, token_ref, grad_ref, rim_ref, total):
     edge = jnp.zeros((2, 1, 16, 128), BF)
     rim_ref[:, 0:1] = edge
     rim_ref[:, 129:130] = edge
-    rim_ref[odd_ref[0], 1:129] = far_ref[0:128]
-    rim_ref[1 - odd_ref[0], 1:129] = near_ref[0:128]
+    rim_ref[odd_place(), 1:129] = far_ref[0:128]
+    rim_ref[1 - odd_place(), 1:129] = near_ref[0:128]
     total[...] = jnp.zeros_like(total)
 
     def body(step, carry):
         left, right = [], []
-        for q in range(16):
-            base = step * 32 + 2 * q
+        for q in range(32):
+            base = step * 64 + 2 * q
             left.append(
                 jnp.concatenate(
                     [
@@ -276,80 +263,76 @@
         )
         return carry
 
-    lax.fori_loop(0, 4, body, 0)
+    lax.fori_loop(0, 2, body, 0)
     summed = inner_ref[...] + aligned(total, 2, [(0, (0, 0)), (64, (2, 2))])
     flatten(summed, grad_ref)
 
 
-def call_outer(odd, far, near, act_edge, inner_grad, token):
+def call_outer(far, near, act_edge, inner_grad, token):
     return kernel_call(
         outer,
         "outer",
-        [SM, VM, VM, VM, VM, VM],
+        [VM, VM, VM, VM, VM],
         [
             jax.ShapeDtypeStruct((56, 128), F32),
             jax.ShapeDtypeStruct((2, 130, 16, 128), BF),
         ],
         [pltpu.VMEM((192, 256), F32)],
         2.5,
-    )(odd, far, near, act_edge, inner_grad, token)
-
-
-def conv_rows(part, planes, kernel, out_hbm, held, out, sems, finish):
+    )(far, near, act_edge, inner_grad, token)
+
+
+def conv_rows(blocks, planes, kernel, out_hbm, held, out, sems, finish):
     swap = exchange_matrix()
     not_first, not_last = lane_masks(64)
-    first = part * 64
-
-    def compute(pair):
-        for block in range(2):
-            for q in range(8):
-                base = first + pair * 32 + block * 16 + 2 * q
-                cells = jnp.concatenate(
-                    [window(planes[2 * zt : 2 * zt + 4], base) for zt in range(2)], axis=1
+
+    def compute(block):
+        for q in range(8):
+            base = block * 16 + 2 * q
+            cells = jnp.concatenate(
+                [window(planes[2 * zt : 2 * zt + 4], base) for zt in range(2)], axis=1
+            )
+            product = mm(kernel, cells)
+            for zt in range(2):
+                piece = product[:, zt * 128 : (zt + 1) * 128]
+                summed = (
+                    piece[64:128]
+                    + from_left(piece[0:64], not_first)
+                    + from_right(piece[128:192], not_last)
                 )
-                product = mm(kernel, cells)
-                for zt in range(2):
-                    piece = product[:, zt * 128 : (zt + 1) * 128]
-                    summed = (
-                        piece[64:128]
-                        + from_left(piece[0:64], not_first)
-                        + from_right(piece[128:192], not_last)
-                    )
-                    rounded = finish(summed).astype(BF).reshape(2, 2, 16, 128)
-                    for z in range(2):
-                        held[pair, block, 2 * zt + z, 2 * q : 2 * q + 2] = rounded[z]
-
-    def flush(pair):
-        for block in range(2):
-            rows = slice(pair * 32 + block * 16, pair * 32 + block * 16 + 16)
-            for zt in range(2):
-                cells = jnp.concatenate(
-                    [held[pair, block, 2 * zt + z].reshape(256, 128) for z in range(2)], axis=1
-                )
-                moved = mm(swap, cells).astype(BF)
+                rounded = finish(summed).astype(BF).reshape(2, 2, 16, 128)
                 for z in range(2):
-                    piece = moved[:, z * 128 : (z + 1) * 128]
-                    out[:, 2 * zt + z, rows] = piece.reshape(16, 16, 128)
-        copy = pltpu.make_async_copy(
-            out.at[:, :, pair * 32 : pair * 32 + 32],
-            out_hbm.at[:, :, first + pair * 32 : first + pair * 32 + 32],
-            sems.at[pair],
-        )
+                    held[block % 4, 2 * zt + z, 2 * q : 2 * q + 2] = rounded[z]
+
+    def flush(block):
+        rows = slice(block * 16, block * 16 + 16)
+        for zt in range(2):
+            cells = jnp.concatenate(
+                [held[block % 4, 2 * zt + z].reshape(256, 128) for z in range(2)], axis=1
+            )
+            moved = mm(swap, cells).astype(BF)
+            for z in range(2):
+                piece = moved[:, z * 128 : (z + 1) * 128]
+                out[:, 2 * zt + z, rows] = piece.reshape(16, 16, 128)
+        copy = pltpu.make_async_copy(out.at[:, :, rows], out_hbm.at[:, :, rows], sems.at[block])
         copy.start()
         return copy
 
-    compute(0)
-    compute(1)
-    copies = [flush(0), flush(1)]
+    copies = []
+    for place, block in enumerate(blocks):
+        compute(block)
+        if place % 2 and place > 1:
+            copies += [flush(blocks[place - 3]), flush(blocks[place - 2])]
+    copies += [flush(block) for block in blocks[-2:]]
     for copy in copies:
         copy.wait()
 
 
 FIELD = jax.ShapeDtypeStruct((16, 4, 128, 128), BF)
 HELD = [
-    pltpu.VMEM((2, 2, 4, 16, 16, 128), BF),
-    pltpu.VMEM((16, 4, 64, 128), BF),
-    pltpu.SemaphoreType.DMA((2,)),
+    pltpu.VMEM((4, 4, 16, 16, 128), BF),
+    pltpu.VMEM((16, 4, 128, 128), BF),
+    pltpu.SemaphoreType.DMA((8,)),
 ]
 
 
@@ -368,7 +351,8 @@
 def input_grad(part, kernel_ref, cot_ref, rim_ref, token_ref, *refs):
     out_ref, held, out, sems = refs[-4:]
     planes = [(rim_ref, 0)] + [(cot_ref, z) for z in range(4)] + [(rim_ref, 1)]
-    conv_rows(part, planes, kernel_ref[...], out_ref, held, out, sems, lambda value: value)
+    blocks = range(4 * part, 4 * part + 4)
+    conv_rows(blocks, planes, kernel_ref[...], out_ref, held, out, sems, lambda value: value)
 
 
 def call_input_grad(part, kernel, cot_rows, rim_rows, token, *before):
@@ -448,63 +432,103 @@
     )(grad, state, table)
 
 
-def flat_state(data_ref, shards_ref, token_ref, out_ref):
-    data = data_ref[0]
+def gather_state(both_ref, got_ref, half_ref, other_ref, sum_ref, out_ref):
+    sum_ref[...] = both_ref[...] + got_ref[0:112]
+    data = lax.axis_index("dp")
+    odd = odd_place()
     lanes = lax.broadcasted_iota(jnp.int32, (16, 128), 1)
     for shard in range(8):
         away = lax.bitwise_xor(data, shard)
-        block = shards_ref[lax.rem(away, 2) * 4 + lax.bitwise_and(away, 2) + away // 4]
+        slot = lax.bitwise_and(away, 2) + away // 4
+        start = pl.multiple_of(48 * slot, 48)
         kept = 128 - 6 * shard
         for n in range(3):
-            rows = block[16 * n : 16 * n + 16]
+            span = pl.ds(start + 16 * n, 16)
+            there = pl.ds(start + 112 + 16 * n, 16)
+            rows = jnp.where(odd == 1, got_ref[there], other_ref[span])
+            rows = jnp.where(lax.rem(away, 2) == 1, rows, half_ref[span])
             if shard:
                 rows = pltpu.roll(rows, kept, 1)
-                start = out_ref[n, 14 * shard - 1 : 14 * shard]
+                before = out_ref[n, 14 * shard - 1 : 14 * shard]
                 out_ref[n, 14 * shard - 1 : 14 * shard] = jnp.where(
-                    lanes[:1] < kept, start, rows[:1]
+                    lanes[:1] < kept, before, rows[:1]
                 )
             out_ref[n, 14 * shard : 14 * shard + 14] = jnp.where(
                 lanes[:14] < kept, rows[:14], rows[1:15]
             )
 
 
-def call_flat_state(data, shards, token):
-    return kernel_call(
-        flat_state,
-        "flat_state",
-        [SM, VM, VM],
-        jax.ShapeDtypeStruct((3, 112, 128), F32),
+def call_gather_state(both, got, half, other):
+    return kernel_call(
+        gather_state,
+        "gather_state",
+        [VM, VM, VM, VM],
+        [jax.ShapeDtypeStruct((112, 128), F32), jax.ShapeDtypeStruct((3, 112, 128), F32)],
         micros=0.3,
-    )(data, shards, token)
-
-
-def finish(scales, dec_ref, enc_ref, state_ref, grad_ref, work_ref):
+    )(both, got, half, other)
+
+
+def merge(dec_ref, enc_ref, got_ref, state_ref, both_ref, sent_ref, all_ref):
+    both_ref[0:54] = dec_ref[0:54]
+    both_ref[54:112] = enc_ref[0:58] + got_ref[0:58]
+    sent_ref[0:112] = both_ref[...]
+    for out, first in ((sent_ref, 112), (all_ref, 0)):
+        out[first : first + 96] = state_ref[...]
+        out[first + 96 : first + 192] = got_ref[64:160]
+
+
+def call_merge(dec, enc, got, state):
+    return kernel_call(
+        merge,
+        "merge",
+        [VM, VM, VM, VM],
+        [jax.ShapeDtypeStruct((rows, 128), F32) for rows in (112, 304, 192)],
+        micros=0.2,
+    )(dec, enc, got, state)
+
+
+def finish(scales, dec_ref, enc_ref, state_ref, own_ref, *refs):
+    work_ref, *own_refs, flat = refs
     rows = lax.broadcasted_iota(jnp.int32, (112, 128), 0)
-    grad_ref[...] = enc_ref[...] * scales[1]
-    grad_ref[0:56] = jnp.where(rows[:56] < 54, dec_ref[...] * scales[0], grad_ref[0:56])
-    new = adam(state_ref[0], state_ref[1], state_ref[2], grad_ref[...])[0]
-    work_ref[...] = new.astype(BF)
-
-
-def call_finish(scales, dec, enc, state):
+    gradient = enc_ref[...] * scales[1]
+    dec = jnp.concatenate([dec_ref[...], jnp.zeros((56, 128), F32)], axis=0) * scales[0]
+    gradient = jnp.where(rows < 54, dec, gradient)
+    work_ref[...] = adam(state_ref[0], state_ref[1], state_ref[2], gradient)[0].astype(BF)
+    flat[0:8] = jnp.zeros((8, 128), F32)
+    flat[8:120] = gradient
+    data = lax.axis_index("dp")
+    turned = pltpu.roll(flat[pl.ds(7 + 14 * data, 15)], 6 * data, 1)
+    lanes = lax.broadcasted_iota(jnp.int32, (14, 128), 1)
+    own = jnp.where(lanes >= 6 * data, turned[1:15], turned[0:14])
+    new = adam(own_ref[0:14], own_ref[16:30], own_ref[32:46], own)
+    for value, out in zip(new, own_refs):
+        for row in range(14):
+            width = min(128, 1786 - 128 * row)
+            out[pl.ds(128 * row, width)] = value[row][:width]
+
+
+def call_finish(scales, dec, enc, state, own):
+    shard = jax.ShapeDtypeStruct((1786,), F32)
     return kernel_call(
         functools.partial(finish, scales),
         "finish",
-        [VM, VM, VM],
-        [jax.ShapeDtypeStruct((112, 128), F32), jax.ShapeDtypeStruct((112, 128), BF)],
-    )(dec, enc, state)
-
-
-def prepare(odd_ref, far_ref, near_ref, volume_ref, weight_ref, token_ref, out_ref, kernel_ref):
+        [VM, VM, VM, VM],
+        [jax.ShapeDtypeStruct((112, 128), BF), shard, shard, shard],
+        [pltpu.VMEM((120, 128), F32)],
+    )(dec, enc, state, own)
+
+
+def volume_windows(far_ref, near_ref, volume_ref, token_ref, out_ref):
     not_first, not_last = lane_masks(128)
+    odd = odd_place()
     for plane in range(8):
         if plane < 2 or plane > 5:
             z = plane if plane < 2 else plane - 6
             far, near = [
-                ref[128 + 8 * z : 136 + 8 * z].reshape(128, 128).astype(F32)
-                for ref in (far_ref, near_ref)
+                ref[start : start + 8].reshape(128, 128).astype(F32)
+                for ref, start in ((far_ref, 128 + 8 * z), (near_ref, 128 + 8 * z))
             ]
-            cells = jnp.where(odd_ref[0] == (0 if plane < 2 else 1), far, near)
+            cells = jnp.where(odd == (0 if plane < 2 else 1), far, near)
         else:
             cells = volume_ref[plane - 2]
         cells = cells.astype(F32)
@@ -516,6 +540,19 @@
             up = jnp.concatenate([value[4:], pad], axis=0)
             out_ref[0, dx, plane] = down.astype(BF).reshape(8, 16, 128)
             out_ref[1, dx, plane] = up.astype(BF).reshape(8, 16, 128)
+
+
+def call_volume_windows(far, near, volume, token):
+    return kernel_call(
+        volume_windows,
+        "volume_windows",
+        [VM, VM, VM, VM],
+        jax.ShapeDtypeStruct((2, 3, 8, 8, 16, 128), BF),
+        micros=0.5,
+    )(far, near, volume, token)
+
+
+def turn_weights(weight_ref, token_ref, kernel_ref):
     weight = weight_ref[...].reshape(256, 27)
     weight = jnp.concatenate([weight, jnp.zeros((256, 101), BF)], axis=1)
     taps = lax.broadcasted_iota(jnp.int32, (128, 256), 0)
@@ -533,20 +570,18 @@
     kernel_ref[...] = shifted_kernels(bases)
 
 
-def call_prepare(odd, far, near, volume, weight, token):
-    return kernel_call(
-        prepare,
-        "prepare",
-        [SM, VM, VM, VM, VM, VM],
-        [
-            jax.ShapeDtypeStruct((2, 3, 8, 8, 16, 128), BF),
-            jax.ShapeDtypeStruct((192, 256), BF),
-        ],
-        micros=1.3,
-    )(odd, far, near, volume, weight, token)
-
-
-def first_layer(inside_ref, one_ref, cells_ref, token_ref, first):
+def call_turn_weights(weight, token):
+    return kernel_call(
+        turn_weights,
+        "turn_weights",
+        [VM, VM],
+        jax.ShapeDtypeStruct((192, 256), BF),
+        micros=0.5,
+    )(weight, token)
+
+
+def first_layer(one_ref, cells_ref, token_ref, first):
+    space = lax.axis_index("space")
     edge = jnp.zeros((6, 1, 16, 128), BF)
     first[:, 0:1] = edge
     first[:, 129:130] = edge
@@ -576,9 +611,9 @@
                         plane = 2 * zp + z
                         value = found[z]
                         if plane == 0:
-                            value = jnp.where(inside_ref[0] == 1, value, 0.0)
+                            value = jnp.where(space > 0, value, 0.0)
                         if plane == 5:
-                            value = jnp.where(inside_ref[1] == 1, value, 0.0)
+                            value = jnp.where(space < lax.axis_size("space") - 1, value, 0.0)
                         value = value.astype(BF).reshape(8, 16, 128)
                         first[plane, pl.ds(j * 16 + s * 8 + 1, 8)] = value
         return carry
@@ -586,35 +621,33 @@
     lax.fori_loop(0, 2, body, 0)
 
 
-def call_first_layer(inside, one, cells, token):
+def call_first_layer(one, cells, token):
     return kernel_call(
         first_layer,
         "first_layer",
-        [SM, VM, VM, VM],
+        [VM, VM, VM],
         jax.ShapeDtypeStruct((6, 130, 16, 128), BF),
         micros=1.5,
-    )(inside, one, cells, token)
-
-
-def second_layer(part, two_ref, bias_ref, first, token_ref, *refs):
-    out_ref, held, out, sems = refs[-4:]
+    )(one, cells, token)
+
+
+def second_layer(two_ref, bias_ref, first, token_ref, out_ref, held, out, sems):
     bias = jnp.concatenate([bias_ref[...]] * 4, axis=0)
     finish = lambda value: jnp.maximum(value + bias, 0.0)
     planes = [(first, z) for z in range(6)]
-    conv_rows(part, planes, two_ref[...], out_ref, held, out, sems, finish)
-
-
-def call_second_layer(part, two, bias, first, token, *before):
-    return kernel_call(
-        functools.partial(second_layer, part),
-        f"second_layer_{part}",
-        [VM, VM, VM, VM] + [HBM] * len(before),
+    conv_rows(range(8), planes, two_ref[...], out_ref, held, out, sems, finish)
+
+
+def call_second_layer(two, bias, first, token):
+    return kernel_call(
+        second_layer,
+        "second_layer",
+        [VM, VM, VM, VM],
         FIELD,
         HELD,
-        2.2,
+        4.2,
         HBM,
-        {4: 0} if before else None,
-    )(two, bias, first, token, *before)
+    )(two, bias, first, token)
 
 
 def partner(value, axis, bit):
@@ -622,13 +655,20 @@
     return lax.ppermute(value, axis, [(i, i ^ bit) for i in range(count)])
 
 
-def four(value, first, second):
+def four(value, even, odd, given=None):
     count = lax.axis_size("dp") * lax.axis_size("space")
+    size = value.shape[0]
+    even, odd = [(first, second, first ^ second) for first, second in (even, odd)]
     one, two, three = [
-        lax.ppermute(value, ("dp", "space"), [(i, i ^ bits) for i in range(count)])
-        for bits in (first, second, first ^ second)
+        lax.ppermute(
+            given if n == 2 and given is not None else value,
+            ("dp", "space"),
+            [(i, i ^ (odd if i % 2 else even)[n]) for i in range(count)],
+        )
+        for n in range(3)
     ]
-    return (value + one) + (two + three)
+    total = (value + one) + (two + three[:size])
+    return total if given is None else (total, three[size:])
 
 
 def after(*values):
@@ -637,31 +677,22 @@
 
 def local(activation, cotangent, volume, dec_weight, enc_grad, params, moment, second):
     act, cot, vol = activation[0], cotangent[0], volume[0, 0]
-    space = lax.axis_index("space")
     count = lax.axis_size("space")
-    n_dp = lax.axis_size("dp")
-    data = lax.axis_index("dp")
-    devices = n_dp * count
+    devices = lax.axis_size("dp") * count
     voxels = devices * act.shape[1] * act.shape[2] * act.shape[3]
-
-    odd = lax.rem(space, 2)
-    odd_arg = odd.reshape(1).astype(jnp.int32)
     scales = (1.0 / math.sqrt(voxels), 1.0 / math.sqrt(devices))
-    data_arg = data.reshape(1).astype(jnp.int32)
-    inside = jnp.stack([space > 0, space < count - 1]).astype(jnp.int32)
     table = jnp.asarray(placement())
 
-    own_start = data.astype(jnp.uint32) * 1786
-    odd_arg, data_arg, own_start, inside, cot = after(odd_arg, data_arg, own_start, inside, cot)
-    far, near = call_edges(odd_arg, cot, vol)
+    far, near = call_edges(cot, vol)
     pairs = [(i, i + 1) for i in range(1, count - 1, 2)]
     far_in = lax.ppermute(far, "space", pairs + [(b, a) for a, b in pairs])
     near_in = partner(near, "space", 1)
 
-    far, enc_grad = after(far, enc_grad)
-    enc = jnp.pad(enc_grad[0, 0], (0, 8192 - 7376)).reshape(64, 128)
+    far, enc_grad, act, cot = after(far, enc_grad, act, cot)
+    enc = jnp.pad(enc_grad, ((0, 0), (0, 0), (0, 8192 - 7376))).reshape(64, 128)
     pad = lambda value: jnp.pad(value, (0, 2048 - 1786)).reshape(16, 128)
-    state = jnp.concatenate([pad(params), pad(moment), pad(second)], axis=0)
+    own = jnp.concatenate([pad(params), pad(moment), pad(second)], axis=0)
+    state = own
 
     def state_round(enc, state, bit):
         return partner(jnp.concatenate([enc, state], axis=0), "dp", bit)
@@ -669,48 +700,44 @@
     def joined(enc, state, got):
         return enc + got[:64], jnp.concatenate([state, got[64:]], axis=0)
 
-    enc = enc + partner(enc, "space", 1)
     got = state_round(enc, state, 4)
     inner_grad, cot_rows, act_edge = call_inner(act, cot, enc)
     got, inner_grad = after(got, inner_grad)
     enc, state = joined(enc, state, got)
     got = state_round(enc, state, 2)
-    dec, rim_rows = call_outer(odd_arg, far_in, near_in, act_edge, inner_grad, enc)
+    kernel = call_turn_weights(dec_weight.transpose(1, 2, 0), enc)
+    act_edge, kernel = after(act_edge, kernel)
+    dec, rim_rows = call_outer(far_in, near_in, act_edge, inner_grad, enc)
     got, dec = after(got, dec)
-    enc, state = joined(enc, state, got)
-
-    both = jnp.concatenate([dec[:54], enc[:58]], axis=0)
+    both, sent, state = call_merge(dec, enc, got, state)
     token = both
-    both = four(both, count, 8)
-    cells, kernel = call_prepare(
-        odd_arg, far_in, near_in, vol, dec_weight.transpose(1, 2, 0), token
-    )
+    along_y, along_x = (8, 8 + count), (4, 6)
+    both, other = four(both, along_y, along_x, sent)
     grad_input = call_input_grad(0, kernel, cot_rows, rim_rows, token)
     both, grad_input = after(both, grad_input)
     token = both
-    both = four(both, 2, 4)
-    state = jnp.concatenate([state, partner(state, "dp", 1)], axis=0)
+    both = four(both, along_x, along_y)
     grad_input = call_input_grad(1, kernel, cot_rows, rim_rows, token, grad_input)
     both, grad_input = after(both, grad_input)
-    state = call_flat_state(data_arg, state.reshape(8, 48, 128), token)
-
+    token = both
+    got = partner(jnp.concatenate([both, other], axis=0), "space", 1)
+    cells = call_volume_windows(far_in, near_in, vol, token)
+    got, cells = after(got, cells)
+    both, state = call_gather_state(both, got, state, other)
+
+    dec = both[:56]
+    token = dec
+    dec = dec + partner(dec, "dp", 2)
     two, one, bias = call_update_encoder(scales[1], both, state, table)
-    first = call_first_layer(inside, one, cells, both)
-    dec = both[:56]
-    dec = dec + partner(dec, "dp", 2)
+    first = call_first_layer(one, cells, token)
+    dec, first = after(dec, first)
     token = dec
-    dec, first = after(dec, first)
     dec = dec + partner(dec, "dp", 4)
-    encoded = call_second_layer(0, two, bias, first, token)
+    encoded = call_second_layer(two, bias, first, token)
     dec, encoded = after(dec, encoded)
-    dec = dec + partner(dec, "space", 1)
-    encoded = call_second_layer(1, two, bias, first, token, encoded)
-
-    flat, working = call_finish(scales, dec, both, state)
+    working, *new = call_finish(scales, dec, both, state, own)
     working = working.reshape(112 * 128)[:14288]
-    own = lax.dynamic_slice(flat.reshape(112 * 128), (own_start,), (1786,))
-    own = adam(params, moment, second, own)
-    return (grad_input[None], own[0], own[1], own[2], working, encoded[None])
+    return (grad_input[None], *new, working, encoded[None])
 
 
 def solution(mesh):

time: 53.9 us -> 48.6 us (0.902)
  the two profiles are of different devices: /device:TPU:1 before, /device:TPU:0 now
where the time goes in v4:
time: 48.6 us; the launch traced here: 48.2 us
  starting transfers between devices  21.6 us (44%)
  Pallas kernels  19 us (39%)
  waiting for transfers between devices  6.43 us (13%)
  between operations  1.02 us (2%)
    ppermute x6, starting transfers between devices, partner(): return lax.ppermute(value, axis, [(i, i ^ bit) for i in range(count)])  10.6 us
    ppermute x6, starting transfers between devices, four(): lax.ppermute(given if n == 2 and given is not None else value, ('dp', 'sp...  10.2 us
    pallas_call x2, Pallas kernels, call_input_grad(): kernel_call(functools.partial(input_grad, part), f'input_grad_{part}', [V...  4.82 us
    pallas_call x1, Pallas kernels, call_inner(): kernel_call(inner, 'inner', [VM, VM, VM], [jax.ShapeDtypeStruct((48, 256)...  3.72 us
    pallas_call x1, Pallas kernels, call_second_layer(): kernel_call(second_layer, 'second_layer', [VM, VM, VM, VM], FIELD, HELD,...  3.59 us
    ppermute x6, waiting for transfers between devices, four(): lax.ppermute(given if n == 2 and given is not None else value, ('dp', 'sp...  3.23 us
    ppermute x6, waiting for transfers between devices, partner(): return lax.ppermute(value, axis, [(i, i ^ bit) for i in range(count)])  3.2 us
    pallas_call x1, Pallas kernels, call_edges(): kernel_call(edges, 'edges', [HBM, HBM], [shape, shape], [pltpu.VMEM((2, 1...  1.58 us
  transfers between devices with their start and end apart: 13, of which 5 were waited for; matrix products, arithmetic and copies ran while one was open for 0% of the time, Pallas kernels for 34%

profile of v4, /device:TPU:0, one launch (start us, length us, event | category | flops | bytes accessed | tf_op | source)
XLA Modules:
  0.0 48.2 jit_solution(653909308076104483)
XLA Ops:
  0.7 1.6 %edges.1 = (bf16[144,16,128]{2,1,0:T(8,128)(2,1)S(1)}, bf16[144,16,128]{2,1,0:T(8,128)(2,1)S(1)}) custom-call(bf16[16,4,128,128]{3,2,1,0:T(8,128)(2,1)} %bitcast.27, bf16[4,128,128]{2,1,0:T(8,128)(2,1)} %bitcast.24), custom_call_target="tpu_custom_call" | custom-call | flops 1495000064 | bytes 4680000 | tf_op jit(solution)/shard_map/edges/pallas_call | solution.py:102
  2.3 0.8 %collective-permute-start.2 = (bf16[144,16,128]{2,1,0:T(8,128)(2,1)S(1)}, bf16[144,16,128]{2,1,0:T(8,128)(2,1)S(1)}, u32[]{:S(2)}, u32[]{:S(2)}) collective-permute-start(bf16[144,16,128]{2,1,0:T(8,128)(2,1)S(1)} %get-tuple-element.44), channel_id=1, source_target_pairs={{1,2},{3,4},{5,6},{7,8},{9,10},{11,12},{13,14},{2,1},{4,3},{6,5},{... | collective-permute-start | bytes 1769480 | tf_op jit(solution)/shard_map/ppermute | solution.py:688
  3.2 4.0 %collective-permute-start = (f32[112,128]{1,0:T(8,128)S(1)}, f32[112,128]{1,0:T(8,128)S(1)}, u32[]{:S(2)}, u32[]{:S(2)}) collective-permute-start(f32[112,128]{1,0:T(8,128)S(1)} %pad_maximum_fusion.1), channel_id=1, source_target_pairs={{0,64},{16,80},{32,96},{48,112},{64,0},{80,16},{96,32},{112,48},{1... | collective-permute-start | bytes 172040 | tf_op jit(solution)/shard_map/ppermute | solution.py:655
  7.3 2.5 %collective-permute-start.3 = (bf16[144,16,128]{2,1,0:T(8,128)(2,1)S(1)}, bf16[144,16,128]{2,1,0:T(8,128)(2,1)S(1)}, u32[]{:S(2)}, u32[]{:S(2)}) collective-permute-start(bf16[144,16,128]{2,1,0:T(8,128)(2,1)S(1)} %get-tuple-element.50), channel_id=1, source_target_pairs={{0,1},{1,0},{2,3},{3,2},{4,5},{5,4},{6,7},{7,6},{8,9},{9,8},{10,11... | collective-permute-start | bytes 1769480 | tf_op jit(solution)/shard_map/ppermute | solution.py:655
  9.8 3.7 %inner.1 = (f32[48,256]{1,0:T(8,128)S(1)}, bf16[4,130,16,128]{3,2,1,0:T(8,128)(2,1)S(1)}, bf16[2,3,128,16,128]{4,3,2,1,0:T(8,128)(2,1)S(1)}) custom-call(bf16[16,4,128,128]{3,2,1,0:T(8,128)(2,1)S(1)} %bitcast.26, bf16[16,4,128,128]{3,2,1,0:T(8,128)(2,1)S(1)} %bitcast.28, f32[64,128]{1,0:T(8,128)S(1)} %bitcast.22), custom_call_target="tpu_custom_call" | custom-call | flops 4600000000 | bytes 14400000 | tf_op jit(solution)/shard_map/inner/pallas_call | solution.py:193
  13.6 1.1 %collective-permute-start.1 = (f32[160,128]{1,0:T(8,128)S(1)}, f32[160,128]{1,0:T(8,128)S(1)}, u32[]{:S(2)}, u32[]{:S(2)}) collective-permute-start(f32[160,128]{1,0:T(8,128)S(1)} %get-tuple-element.85), channel_id=1, source_target_pairs={{0,32},{16,48},{32,0},{48,16},{64,96},{80,112},{96,64},{112,80},{1... | collective-permute-start | bytes 245768 | tf_op jit(solution)/shard_map/ppermute | solution.py:655
  14.7 0.8 %turn_weights.1.kernel_ref = bf16[192,256]{1,0:T(8,128)(2,1)S(1)} custom-call(bf16[16,16,27]{2,1,0:T(8,128)(2,1)S(1)} %bitcast.29, f32[64,128]{1,0:T(8,128)S(1)} %get-tuple-element.83.token_ref.enc_ref), custom_call_target="tpu_custom_call" | custom-call | flops 575000000 | bytes 1800000 | tf_op jit(solution)/shard_map/turn_weights/pallas_call | solution.py:574
  15.6 1.6 %outer.1 = (f32[56,128]{1,0:T(8,128)S(1)}, bf16[2,130,16,128]{3,2,1,0:T(8,128)(2,1)S(1)}) custom-call(bf16[144,16,128]{2,1,0:T(8,128)(2,1)S(1)} %collective-permute-done.2.far_ref, bf16[144,16,128]{2,1,0:T(8,128)(2,1)S(1)} %collective-permute-done.3.near_ref, bf16[2,3,128,16,128]{4,3,2,1,0:T(8,128)(2,1)S(1)} %get-tuple-element.52.act_edge, ...), custom_call_target="tpu_custom_call" | custom-call | flops 2875000064 | bytes 9000000 | tf_op jit(solution)/shard_map/outer/pallas_call | solution.py:272
  17.1 1.0 %collective-permute-done.1.got_ref = f32[160,128]{1,0:T(8,128)S(1)} collective-permute-done((f32[160,128]{1,0:T(8,128)S(1)}, f32[160,128]{1,0:T(8,128)S(1)}, u32[]{:S(2)}, u32[]{:S(2)}) %collective-permute-start.1) | collective-permute-done | bytes 81952 | tf_op jit(solution)/shard_map/ppermute | solution.py:655
  18.2 5.1 %collective-permute-start.5 = (f32[112,128]{1,0:T(8,128)S(1)}, f32[112,128]{1,0:T(8,128)S(1)}, u32[]{:S(2)}, u32[]{:S(2)}) collective-permute-start(f32[112,128]{1,0:T(8,128)S(1)} %get-tuple-element.57.token_ref), channel_id=1, source_target_pairs={{0,24},{1,7},{2,26},{3,5},{4,28},{5,3},{6,30},{7,1},{8,16},{9,15},... | collective-permute-start | bytes 172040 | tf_op jit(solution)/shard_map/ppermute | solution.py:663
  23.2 0.9 %collective-permute-start.6 = (f32[304,128]{1,0:T(8,128)S(1)}, f32[304,128]{1,0:T(8,128)S(1)}, u32[]{:S(2)}, u32[]{:S(2)}) collective-permute-start(f32[304,128]{1,0:T(8,128)S(1)} %get-tuple-element.58), channel_id=1, source_target_pairs={{0,16},{1,3},{2,18},{3,1},{4,20},{5,7},{6,22},{7,5},{8,24},{9,11},... | collective-permute-start | bytes 466952 | tf_op jit(solution)/shard_map/ppermute | solution.py:663
  24.2 2.4 %input_grad_0.1.refs_0_ = bf16[16,4,128,128]{3,2,1,0:T(8,128)(2,1)} custom-call(bf16[192,256]{1,0:T(8,128)(2,1)S(1)} %turn_weights.1.kernel_ref, bf16[4,130,16,128]{3,2,1,0:T(8,128)(2,1)S(1)} %get-tuple-element.60.cot_ref, bf16[2,130,16,128]{3,2,1,0:T(8,128)(2,1)S(1)} %get-tuple-element.61.rim_ref, f32[112,128]{1,0:T(8,128)S(1)} %get-tuple-element.57.token_ref), custom_call_target="tpu_custom_call" | custom-call | flops 2529999872 | bytes 7920000 | tf_op jit(solution)/shard_map/input_grad_0/pallas_call | solution.py:359
  26.6 2.3 %collective-permute-done.4 = f32[112,128]{1,0:T(8,128)S(1)} collective-permute-done((f32[112,128]{1,0:T(8,128)S(1)}, f32[112,128]{1,0:T(8,128)S(1)}, u32[]{:S(2)}, u32[]{:S(2)}) %collective-permute-start.4) | collective-permute-done | bytes 57376 | tf_op jit(solution)/shard_map/ppermute | solution.py:663
  28.9 0.0 copy-start
  29.0 0.1 collective-permute-start.9
  29.1 1.8 %collective-permute-start.8 = (f32[112,128]{1,0:T(8,128)S(1)}, f32[112,128]{1,0:T(8,128)S(1)}, u32[]{:S(2)}, u32[]{:S(2)}) collective-permute-start(f32[112,128]{1,0:T(8,128)S(1)} %fusion.token_ref), channel_id=1, source_target_pairs={{0,6},{1,25},{2,4},{3,27},{4,2},{5,29},{6,0},{7,31},{8,14},{9,17},... | collective-permute-start | bytes 172040 | tf_op jit(solution)/shard_map/ppermute | solution.py:663
  30.8 2.3 %collective-permute-start.7 = (f32[112,128]{1,0:T(8,128)S(1)}, f32[112,128]{1,0:T(8,128)S(1)}, u32[]{:S(2)}, u32[]{:S(2)}) collective-permute-start(f32[112,128]{1,0:T(8,128)S(1)} %fusion.token_ref), channel_id=1, source_target_pairs={{0,4},{1,9},{2,6},{3,11},{4,0},{5,13},{6,2},{7,15},{8,12},{9,1},{1... | collective-permute-start | bytes 172040 | tf_op jit(solution)/shard_map/ppermute | solution.py:663
  33.1 2.4 %input_grad_1.1 = bf16[16,4,128,128]{3,2,1,0:T(8,128)(2,1)} custom-call(bf16[192,256]{1,0:T(8,128)(2,1)S(1)} %turn_weights.1.kernel_ref, bf16[4,130,16,128]{3,2,1,0:T(8,128)(2,1)S(1)} %get-tuple-element.60.cot_ref, bf16[2,130,16,128]{3,2,1,0:T(8,128)(2,1)S(1)} %get-tuple-element.61.rim_ref, ...), custom_call_target="tpu_custom_call", output_to_operand_aliasing={{}: (4, {})} | custom-call | flops 2529999872 | bytes 7920000 | tf_op jit(solution)/shard_map/input_grad_1/pallas_call | solution.py:359
  35.6 0.9 %collective-permute-done.7 = f32[112,128]{1,0:T(8,128)S(1)} collective-permute-done((f32[112,128]{1,0:T(8,128)S(1)}, f32[112,128]{1,0:T(8,128)S(1)}, u32[]{:S(2)}, u32[]{:S(2)}) %collective-permute-start.7) | collective-permute-done | bytes 57376 | tf_op jit(solution)/shard_map/ppermute | solution.py:663
  36.5 0.1 collective-permute-start.10
  36.7 0.0 copy-start.4
  36.7 0.3 volume_windows.1.cells_ref
  37.0 1.0 %collective-permute-done.10.got_ref = f32[304,128]{1,0:T(8,128)S(1)} collective-permute-done((f32[304,128]{1,0:T(8,128)S(1)}, f32[304,128]{1,0:T(8,128)S(1)}, u32[]{:S(2)}, u32[]{:S(2)}) %collective-permute-start.10) | collective-permute-done | bytes 155680 | tf_op jit(solution)/shard_map/ppermute | solution.py:655
  38.0 0.2 gather_state.1
  38.2 1.1 %collective-permute-start.11 = (f32[56,128]{1,0:T(8,128)S(1)}, f32[56,128]{1,0:T(8,128)S(1)}, u32[]{:S(2)}, u32[]{:S(2)}) collective-permute-start(f32[56,128]{1,0:T(8,128)S(1)} %slice.22.token_ref), channel_id=1, source_target_pairs={{0,32},{16,48},{32,0},{48,16},{64,96},{80,112},{96,64},{112,80},{1... | collective-permute-start | bytes 86024 | tf_op jit(solution)/shard_map/ppermute | solution.py:655
  39.3 0.6 %update_encoder.1 = (bf16[192,256]{1,0:T(8,128)(2,1)S(1)}, bf16[256,256]{1,0:T(8,128)(2,1)S(1)}, f32[16,128]{1,0:T(8,128)S(1)}) custom-call(f32[112,128]{1,0:T(8,128)S(1)} %get-tuple-element.68.grad_ref.enc_ref, f32[3,112,128]{2,1,0:T(8,128)S(1)} %get-tuple-element.69.state_ref, bf16[8,64,1408]{2,1,0:T(8,128)(2,1)S(1)} %copy-done.4), custom_call_target="tpu_custom_call" | custom-call | flops 690000000 | bytes 2160000 | tf_op jit(solution)/shard_map/update_encoder/pallas_call | solution.py:422
  39.9 1.2 %first_layer.1.first = bf16[6,130,16,128]{3,2,1,0:T(8,128)(2,1)S(1)} custom-call(bf16[256,256]{1,0:T(8,128)(2,1)S(1)} %get-tuple-element.70.one_ref, bf16[2,3,8,8,16,128]{5,4,3,2,1,0:T(8,128)(2,1)S(1)} %volume_windows.1.cells_ref, f32[56,128]{1,0:T(8,128)S(1)} %slice.22.token_ref), custom_call_target="tpu_custom_call" | custom-call | flops 1724999936 | bytes 5400000 | tf_op jit(solution)/shard_map/first_layer/pallas_call | solution.py:625
  41.0 1.1 %collective-permute-done.11 = f32[56,128]{1,0:T(8,128)S(1)} collective-permute-done((f32[56,128]{1,0:T(8,128)S(1)}, f32[56,128]{1,0:T(8,128)S(1)}, u32[]{:S(2)}, u32[]{:S(2)}) %collective-permute-start.11) | collective-permute-done | bytes 28704 | tf_op jit(solution)/shard_map/ppermute | solution.py:655
  42.1 1.8 %collective-permute-start.12 = (f32[56,128]{1,0:T(8,128)S(1)}, f32[56,128]{1,0:T(8,128)S(1)}, u32[]{:S(2)}, u32[]{:S(2)}) collective-permute-start(f32[56,128]{1,0:T(8,128)S(1)} %slice_add_fusion.2.token_ref), channel_id=1, source_target_pairs={{0,64},{16,80},{32,96},{48,112},{64,0},{80,16},{96,32},{112,48},{1... | collective-permute-start | bytes 86024 | tf_op jit(solution)/shard_map/ppermute | solution.py:655
  43.9 3.6 %second_layer.1 = bf16[16,4,128,128]{3,2,1,0:T(8,128)(2,1)} custom-call(bf16[192,256]{1,0:T(8,128)(2,1)S(1)} %get-tuple-element.73.two_ref, f32[16,128]{1,0:T(8,128)S(1)} %get-tuple-element.74.bias_ref, bf16[6,130,16,128]{3,2,1,0:T(8,128)(2,1)S(1)} %first_layer.1.first, f32[56,128]{1,0:T(8,128)S(1)} %slice_add_fusion.2.token_ref), custom_call_target="tpu_custom_call" | custom-call | flops 4830000128 | bytes 15120000 | tf_op jit(solution)/shard_map/second_layer/pallas_call | solution.py:642
  47.5 0.0 collective-permute-done.12
  47.5 0.7 %finish.1 = (bf16[112,128]{1,0:T(8,128)(2,1)}, f32[1786]{0:T(1024)}, f32[1786]{0:T(1024)}, f32[1786]{0:T(1024)}) custom-call(f32[56,128]{1,0:T(8,128)S(1)} %add.43.dec_ref, f32[112,128]{1,0:T(8,128)S(1)} %get-tuple-element.68.grad_ref.enc_ref, f32[3,112,128]{2,1,0:T(8,128)S(1)} %get-tuple-element.69.state_ref, f32[48,128]{1,0:T(8,128)S(1)} %pad_maximum_fusion.3.own_ref), custom_call_target="tpu_custom_call" | custom-call | flops 1150000000 | bytes 3600000 | tf_op jit(solution)/shard_map/finish/pallas_call | solution.py:512
  (43 shorter events, 0.2 us)
Async XLA Ops:
  0.6 2.5 %copy-start.5 = (f32[1786]{0:T(1024)S(1)}, f32[1786]{0:T(1024)}, u32[]{:S(2)}) copy-start(f32[1786]{0:T(1024)} %param.14) | copy-start | bytes 21436
  0.6 2.5 %copy-start.6 = (f32[1786]{0:T(1024)S(1)}, f32[1786]{0:T(1024)}, u32[]{:S(2)}) copy-start(f32[1786]{0:T(1024)} %param.15) | copy-start | bytes 21436
  0.7 2.5 %copy-start.7 = (f32[1786]{0:T(1024)S(1)}, f32[1786]{0:T(1024)}, u32[]{:S(2)}) copy-start(f32[1786]{0:T(1024)} %param.16) | copy-start | bytes 21436
  0.7 2.5 %copy-start.8 = (f32[1,1,7376]{2,1,0:T(1,128)S(1)}, f32[1,1,7376]{2,1,0:T(1,128)}, u32[]{:S(2)}) copy-start(f32[1,1,7376]{2,1,0:T(1,128)} %param.13) | copy-start | bytes 88516
  0.7 9.1 %copy-start.1 = (bf16[1,16,4,128,128]{4,3,2,1,0:T(8,128)(2,1)S(1)}, bf16[1,16,4,128,128]{4,3,2,1,0:T(8,128)(2,1)}, u32[]{:S(2)}) copy-start(bf16[1,16,4,128,128]{4,3,2,1,0:T(8,128)(2,1)} %param.9) | copy-start | bytes 6291460
  0.7 9.1 %copy-start.2 = (bf16[1,16,4,128,128]{4,3,2,1,0:T(8,128)(2,1)S(1)}, bf16[1,16,4,128,128]{4,3,2,1,0:T(8,128)(2,1)}, u32[]{:S(2)}) copy-start(bf16[1,16,4,128,128]{4,3,2,1,0:T(8,128)(2,1)} %param.10) | copy-start | bytes 6291460
  2.3 13.3 %collective-permute-start.2 = (bf16[144,16,128]{2,1,0:T(8,128)(2,1)S(1)}, bf16[144,16,128]{2,1,0:T(8,128)(2,1)S(1)}, u32[]{:S(2)}, u32[]{:S(2)}) collective-permute-start(bf16[144,16,128]{2,1,0:T(8,128)(2,1)S(1)} %get-tuple-element.44), channel_id=1, source_target_pairs={{1,2},{3,4},{5,6},{7,8},{9,10},{11,12},{13,14},{2,1},{4,3},{6,5},{... | collective-permute-start | bytes 1769480 | tf_op jit(solution)/shard_map/ppermute | solution.py:688
  3.2 10.3 %collective-permute-start = (f32[112,128]{1,0:T(8,128)S(1)}, f32[112,128]{1,0:T(8,128)S(1)}, u32[]{:S(2)}, u32[]{:S(2)}) collective-permute-start(f32[112,128]{1,0:T(8,128)S(1)} %pad_maximum_fusion.1), channel_id=1, source_target_pairs={{0,64},{16,80},{32,96},{48,112},{64,0},{80,16},{96,32},{112,48},{1... | collective-permute-start | bytes 172040 | tf_op jit(solution)/shard_map/ppermute | solution.py:655
  7.3 7.5 %copy-start.3 = (bf16[27,16,16]{0,2,1:T(8,128)(2,1)S(1)}, bf16[27,16,16]{0,2,1:T(8,128)(2,1)}, u32[]{:S(2)}) copy-start(bf16[27,16,16]{0,2,1:T(8,128)(2,1)} %param.12) | copy-start | bytes 41476
  7.3 8.3 %collective-permute-start.3 = (bf16[144,16,128]{2,1,0:T(8,128)(2,1)S(1)}, bf16[144,16,128]{2,1,0:T(8,128)(2,1)S(1)}, u32[]{:S(2)}, u32[]{:S(2)}) collective-permute-start(bf16[144,16,128]{2,1,0:T(8,128)(2,1)S(1)} %get-tuple-element.50), channel_id=1, source_target_pairs={{0,1},{1,0},{2,3},{3,2},{4,5},{5,4},{6,7},{7,6},{8,9},{9,8},{10,11... | collective-permute-start | bytes 1769480 | tf_op jit(solution)/shard_map/ppermute | solution.py:655
  13.6 4.5 %collective-permute-start.1 = (f32[160,128]{1,0:T(8,128)S(1)}, f32[160,128]{1,0:T(8,128)S(1)}, u32[]{:S(2)}, u32[]{:S(2)}) collective-permute-start(f32[160,128]{1,0:T(8,128)S(1)} %get-tuple-element.85), channel_id=1, source_target_pairs={{0,32},{16,48},{32,0},{48,16},{64,96},{80,112},{96,64},{112,80},{1... | collective-permute-start | bytes 245768 | tf_op jit(solution)/shard_map/ppermute | solution.py:655
  18.2 8.4 %collective-permute-start.5 = (f32[112,128]{1,0:T(8,128)S(1)}, f32[112,128]{1,0:T(8,128)S(1)}, u32[]{:S(2)}, u32[]{:S(2)}) collective-permute-start(f32[112,128]{1,0:T(8,128)S(1)} %get-tuple-element.57.token_ref), channel_id=1, source_target_pairs={{0,24},{1,7},{2,26},{3,5},{4,28},{5,3},{6,30},{7,1},{8,16},{9,15},... | collective-permute-start | bytes 172040 | tf_op jit(solution)/shard_map/ppermute | solution.py:663
  23.2 5.7 %collective-permute-start.4 = (f32[112,128]{1,0:T(8,128)S(1)}, f32[112,128]{1,0:T(8,128)S(1)}, u32[]{:S(2)}, u32[]{:S(2)}) collective-permute-start(f32[112,128]{1,0:T(8,128)S(1)} %get-tuple-element.57.token_ref), channel_id=1, source_target_pairs={{0,8},{1,5},{2,10},{3,7},{4,12},{5,1},{6,14},{7,3},{8,0},{9,13},{1... | collective-permute-start | bytes 172040 | tf_op jit(solution)/shard_map/ppermute | solution.py:663
  23.2 5.7 %collective-permute-start.6 = (f32[304,128]{1,0:T(8,128)S(1)}, f32[304,128]{1,0:T(8,128)S(1)}, u32[]{:S(2)}, u32[]{:S(2)}) collective-permute-start(f32[304,128]{1,0:T(8,128)S(1)} %get-tuple-element.58), channel_id=1, source_target_pairs={{0,16},{1,3},{2,18},{3,1},{4,20},{5,7},{6,22},{7,5},{8,24},{9,11},... | collective-permute-start | bytes 466952 | tf_op jit(solution)/shard_map/ppermute | solution.py:663
  28.9 7.7 %copy-start = (bf16[1,1,4,128,128]{4,3,2,1,0:T(8,128)(2,1)S(1)}, bf16[1,1,4,128,128]{4,3,2,1,0:T(8,128)(2,1)}, u32[]{:S(2)}) copy-start(bf16[1,1,4,128,128]{4,3,2,1,0:T(8,128)(2,1)} %param.11) | copy-start | bytes 393220
  29.0 6.6 %collective-permute-start.9 = (f32[112,128]{1,0:T(8,128)S(1)}, f32[112,128]{1,0:T(8,128)S(1)}, u32[]{:S(2)}, u32[]{:S(2)}) collective-permute-start(f32[112,128]{1,0:T(8,128)S(1)} %fusion.token_ref), channel_id=1, source_target_pairs={{0,2},{1,17},{2,0},{3,19},{4,6},{5,21},{6,4},{7,23},{8,10},{9,25},... | collective-permute-start | bytes 172040 | tf_op jit(solution)/shard_map/ppermute | solution.py:663
  29.1 6.5 %collective-permute-start.8 = (f32[112,128]{1,0:T(8,128)S(1)}, f32[112,128]{1,0:T(8,128)S(1)}, u32[]{:S(2)}, u32[]{:S(2)}) collective-permute-start(f32[112,128]{1,0:T(8,128)S(1)} %fusion.token_ref), channel_id=1, source_target_pairs={{0,6},{1,25},{2,4},{3,27},{4,2},{5,29},{6,0},{7,31},{8,14},{9,17},... | collective-permute-start | bytes 172040 | tf_op jit(solution)/shard_map/ppermute | solution.py:663
  30.8 5.7 %collective-permute-start.7 = (f32[112,128]{1,0:T(8,128)S(1)}, f32[112,128]{1,0:T(8,128)S(1)}, u32[]{:S(2)}, u32[]{:S(2)}) collective-permute-start(f32[112,128]{1,0:T(8,128)S(1)} %fusion.token_ref), channel_id=1, source_target_pairs={{0,4},{1,9},{2,6},{3,11},{4,0},{5,13},{6,2},{7,15},{8,12},{9,1},{1... | collective-permute-start | bytes 172040 | tf_op jit(solution)/shard_map/ppermute | solution.py:663
  36.5 1.5 %collective-permute-start.10 = (f32[304,128]{1,0:T(8,128)S(1)}, f32[304,128]{1,0:T(8,128)S(1)}, u32[]{:S(2)}, u32[]{:S(2)}) collective-permute-start(f32[304,128]{1,0:T(8,128)S(1)} %pad_maximum_fusion), channel_id=1, source_target_pairs={{0,1},{1,0},{2,3},{3,2},{4,5},{5,4},{6,7},{7,6},{8,9},{9,8},{10,11... | collective-permute-start | bytes 466952 | tf_op jit(solution)/shard_map/ppermute | solution.py:655
  36.7 2.6 %copy-start.4 = (bf16[8,64,1408]{2,1,0:T(8,128)(2,1)S(1)}, bf16[8,64,1408]{2,1,0:T(8,128)(2,1)}, u32[]{:S(2)}) copy-start(bf16[8,64,1408]{2,1,0:T(8,128)(2,1)} %constant.5.clone.table_ref) | copy-start | bytes 4325380
  38.2 4.0 %collective-permute-start.11 = (f32[56,128]{1,0:T(8,128)S(1)}, f32[56,128]{1,0:T(8,128)S(1)}, u32[]{:S(2)}, u32[]{:S(2)}) collective-permute-start(f32[56,128]{1,0:T(8,128)S(1)} %slice.22.token_ref), channel_id=1, source_target_pairs={{0,32},{16,48},{32,0},{48,16},{64,96},{80,112},{96,64},{112,80},{1... | collective-permute-start | bytes 86024 | tf_op jit(solution)/shard_map/ppermute | solution.py:655
  42.1 5.4 %collective-permute-start.12 = (f32[56,128]{1,0:T(8,128)S(1)}, f32[56,128]{1,0:T(8,128)S(1)}, u32[]{:S(2)}, u32[]{:S(2)}) collective-permute-start(f32[56,128]{1,0:T(8,128)S(1)} %slice_add_fusion.2.token_ref), channel_id=1, source_target_pairs={{0,64},{16,80},{32,96},{48,112},{64,0},{80,16},{96,32},{112,48},{1... | collective-permute-start | bytes 86024 | tf_op jit(solution)/shard_map/ppermute | solution.py:655

commit v5 on v4

--- a/solution.py
+++ b/solution.py
@@ -73,43 +73,43 @@
     return lax.rem(lax.axis_index("space"), 2)
 
 
-def edges(cot_ref, vol_ref, far_ref, near_ref, planes, slabs, sems):
-    odd = odd_place()
-    outs = (far_ref, near_ref)
-    sides = (odd, 1 - odd)
-    copies = []
-    for n in range(2):
-        pair = (
-            pltpu.make_async_copy(cot_ref.at[:, 3 * sides[n]], planes.at[n], sems.at[n]),
-            pltpu.make_async_copy(
-                vol_ref.at[pl.ds(2 * sides[n], 2)], slabs.at[n], sems.at[2 + n]
-            ),
+def far_edge(cot_ref, vol_ref, far_ref, plane, slab, sems):
+    side = odd_place()
+    copies = [
+        pltpu.make_async_copy(
+            cot_ref.at[:, 3 * side, 32 * n : 32 * n + 32],
+            plane.at[:, 32 * n : 32 * n + 32],
+            sems.at[n],
         )
-        for copy in pair:
-            copy.start()
-        copies.append(pair)
-    for n in range(2):
-        copies[n][0].wait()
-        for j in range(8):
+        for n in range(4)
+    ]
+    copies.append(pltpu.make_async_copy(vol_ref.at[pl.ds(2 * side, 2)], slab, sems.at[4]))
+    for copy in copies:
+        copy.start()
+    for n in range(4):
+        copies[n].wait()
+        for j in (2 * n, 2 * n + 1):
             rows = slice(j * 16, (j + 1) * 16)
-            outs[n][rows] = jnp.swapaxes(planes[n, :, rows], 0, 1)
-        copies[n][1].wait()
-        outs[n][128:144] = slabs[n].reshape(16, 16, 128)
-
-
-def call_edges(cot, vol):
-    shape = jax.ShapeDtypeStruct((144, 16, 128), BF)
-    return kernel_call(
-        edges,
-        "edges",
+            far_ref[rows] = jnp.swapaxes(plane[:, rows], 0, 1)
+    copies[4].wait()
+    far_ref[128:144] = slab[...].reshape(16, 16, 128)
+
+
+EDGE = jax.ShapeDtypeStruct((144, 16, 128), BF)
+
+
+def call_far_edge(cot, vol):
+    return kernel_call(
+        far_edge,
+        "far_edge",
         [HBM, HBM],
-        [shape, shape],
+        EDGE,
         [
-            pltpu.VMEM((2, 16, 128, 128), BF),
-            pltpu.VMEM((2, 2, 128, 128), BF),
-            pltpu.SemaphoreType.DMA((4,)),
+            pltpu.VMEM((16, 128, 128), BF),
+            pltpu.VMEM((2, 128, 128), BF),
+            pltpu.SemaphoreType.DMA((5,)),
         ],
-        1.3,
+        1.2,
     )(in_hbm(cot), in_hbm(vol))
 
 
@@ -139,14 +139,16 @@
     return jnp.concatenate(out, axis=0)
 
 
-def inner(act_ref, cot_ref, token_ref, grad_ref, cot_rows, act_edge, act_rows, total):
+def inner(
+    act_ref, cot_ref, vol_ref, token_ref, grad_ref, cot_rows, act_edge, near_ref, act_rows, total
+):
     edge = jnp.zeros((4, 1, 16, 128), BF)
     cot_rows[:, 0:1] = edge
     cot_rows[:, 129:130] = edge
     total[...] = jnp.zeros_like(total)
 
     def turn(step):
-        rows = pl.ds(pl.multiple_of(step * 16, 16), 16)
+        rows = pl.ds(step * 16, 16)
         for z in range(4):
             cot_rows[z, pl.ds(step * 16 + 1, 16)] = jnp.swapaxes(cot_ref[:, z, rows], 0, 1)
             cells = jnp.swapaxes(act_ref[:, z, rows], 0, 1).reshape(256, 128)
@@ -173,38 +175,38 @@
     turn(0)
     turn(1)
 
-    def body(pair, carry):
-        for step in (2 * pair, 2 * pair + 1):
-            turn(step + 2)
-            gather(step)
-        return carry
-
-    lax.fori_loop(0, 3, body, 0)
+    for step in range(6):
+        turn(step + 2)
+        gather(step)
     gather(6)
     gather(7)
     grad_ref[...] = aligned(
         total, 4, [(64, (1, 2)), (0, None), (192, None), (128, (0, 1))]
     )
+    side = 1 - odd_place()
+    near_ref[0:128] = cot_rows[3 * side, 1:129]
+    near_ref[128:144] = vol_ref[pl.ds(2 * side, 2)].reshape(16, 16, 128)
     act_edge[0] = act_rows[:, 0]
     act_edge[1] = act_rows[:, 3]
 
 
-def call_inner(act, cot, token):
+def call_inner(act, cot, vol, token):
     return kernel_call(
         inner,
         "inner",
-        [VM, VM, VM],
+        [VM, VM, VM, VM],
         [
             jax.ShapeDtypeStruct((48, 256), F32),
             jax.ShapeDtypeStruct((4, 130, 16, 128), BF),
             jax.ShapeDtypeStruct((2, 3, 128, 16, 128), BF),
+            EDGE,
         ],
         [
             pltpu.VMEM((3, 4, 128, 16, 128), BF),
             pltpu.VMEM((384, 256), F32),
         ],
         4.0,
-    )(act, cot, token)
+    )(act, cot, vol, token)
 
 
 def window(planes, base):
@@ -235,51 +237,65 @@
                         out_ref[row : row + 1] = value[place : place + 1]
 
 
-def outer(far_ref, near_ref, act_edge, inner_ref, token_ref, grad_ref, rim_ref, total):
-    edge = jnp.zeros((2, 1, 16, 128), BF)
-    rim_ref[:, 0:1] = edge
-    rim_ref[:, 129:130] = edge
-    rim_ref[odd_place(), 1:129] = far_ref[0:128]
-    rim_ref[1 - odd_place(), 1:129] = near_ref[0:128]
+def border_sum(side, rows, act_edge, total):
     total[...] = jnp.zeros_like(total)
-
-    def body(step, carry):
+    for step in range(2):
         left, right = [], []
         for q in range(32):
             base = step * 64 + 2 * q
             left.append(
                 jnp.concatenate(
-                    [
-                        act_edge[side, dx, pl.ds(base, 2)].reshape(32, 128)
-                        for dx in range(3)
-                        for side in range(2)
-                    ],
+                    [act_edge[side, dx, base : base + 2].reshape(32, 128) for dx in range(3)],
                     axis=0,
                 )
             )
-            right.append(window([(rim_ref, 0), (rim_ref, 1)], base))
-        total[:, 0:128] += mm_lanes(
-            jnp.concatenate(left, axis=1), jnp.concatenate(right, axis=1)
-        )
-        return carry
-
-    lax.fori_loop(0, 2, body, 0)
-    summed = inner_ref[...] + aligned(total, 2, [(0, (0, 0)), (64, (2, 2))])
-    flatten(summed, grad_ref)
-
-
-def call_outer(far, near, act_edge, inner_grad, token):
-    return kernel_call(
-        outer,
-        "outer",
-        [VM, VM, VM, VM, VM],
+            right.append(rows[base : base + 4].reshape(64, 128))
+        total[:, 0:64] += mm_lanes(jnp.concatenate(left, axis=1), jnp.concatenate(right, axis=1))
+    return pltpu.roll(aligned(total, 1, [(0, (0, 0))]), 128 * side, 1)
+
+
+def outer_near(near_ref, act_edge, inner_ref, token_ref, grad_ref, rows_ref, total):
+    edge = jnp.zeros((1, 16, 128), BF)
+    rows_ref[0:1] = edge
+    rows_ref[129:130] = edge
+    rows_ref[1:129] = near_ref[0:128]
+    grad_ref[...] = inner_ref[...] + border_sum(1 - odd_place(), rows_ref, act_edge, total)
+
+
+def call_outer_near(near, act_edge, inner_grad, token):
+    return kernel_call(
+        outer_near,
+        "outer_near",
+        [VM, VM, VM, VM],
+        [jax.ShapeDtypeStruct((48, 256), F32), jax.ShapeDtypeStruct((130, 16, 128), BF)],
+        [pltpu.VMEM((96, 256), F32)],
+        0.9,
+    )(near, act_edge, inner_grad, token)
+
+
+def outer_far(far_ref, act_edge, before_ref, near_rows, grad_ref, rim_ref, total):
+    odd = odd_place()
+    edge = jnp.zeros((1, 16, 128), BF)
+    rows = rim_ref.at[odd]
+    rows[0:1] = edge
+    rows[129:130] = edge
+    rows[1:129] = far_ref[0:128]
+    flatten(before_ref[...] + border_sum(odd, rows, act_edge, total), grad_ref)
+    rim_ref[1 - odd] = near_rows[...]
+
+
+def call_outer_far(far, act_edge, before, near_rows):
+    return kernel_call(
+        outer_far,
+        "outer_far",
+        [VM, VM, VM, VM],
         [
             jax.ShapeDtypeStruct((56, 128), F32),
             jax.ShapeDtypeStruct((2, 130, 16, 128), BF),
         ],
-        [pltpu.VMEM((192, 256), F32)],
-        2.5,
-    )(far, near, act_edge, inner_grad, token)
+        [pltpu.VMEM((96, 256), F32)],
+        1.0,
+    )(far, act_edge, before, near_rows)
 
 
 def conv_rows(blocks, planes, kernel, out_hbm, held, out, sems, finish):
@@ -402,9 +418,8 @@
     clean = jnp.where(rows * 128 + lanes < 7376, new, 0.0)
     clean = jnp.concatenate([clean, jnp.zeros((6, 128), F32)], axis=0)
     turned = jnp.transpose(clean).astype(BF)
-    found = jnp.zeros((16, 1408), F32)
-    for group in range(8):
-        found = found + mm(turned[group * 16 : (group + 1) * 16], table_ref[group])
+    groups = [turned[group * 16 : (group + 1) * 16] for group in range(8)]
+    found = mm(jnp.concatenate(groups, axis=1), table_ref[...].reshape(512, 1408))
     two_ref[...] = shifted_kernels([found[:, dx * 256 : (dx + 1) * 256] for dx in range(3)])
     bias_ref[...] = found[:, 768:896]
     base, bias = found[:, 896:1152], found[:, 1152:1408]
@@ -555,18 +570,18 @@
 def turn_weights(weight_ref, token_ref, kernel_ref):
     weight = weight_ref[...].reshape(256, 27)
     weight = jnp.concatenate([weight, jnp.zeros((256, 101), BF)], axis=1)
-    taps = lax.broadcasted_iota(jnp.int32, (128, 256), 0)
-    columns = lax.broadcasted_iota(jnp.int32, (128, 256), 1)
-    dz, dy = columns // 64, columns // 16 % 4
-    rows = lax.broadcasted_iota(jnp.int32, (256, 256), 0)
-    lanes = lax.broadcasted_iota(jnp.int32, (256, 256), 1)
-    same = rows % 16 == lanes % 16
-    summing = jnp.where(rows[:16] == lanes[:16] // 16, 1.0, 0.0).astype(BF)
-    bases = []
-    for dx in range(3):
-        wanted = (dz < 3) & (dy < 3) & (taps == 26 - (9 * dz + 3 * dy + dx))
-        spread = mm(weight, jnp.where(wanted, 1.0, 0.0).astype(BF))
-        bases.append(mm(summing, jnp.where(same, spread, 0.0).astype(BF)))
+    taps = lax.broadcasted_iota(jnp.int32, (128, 768), 0)
+    columns = lax.broadcasted_iota(jnp.int32, (128, 768), 1)
+    dx, dz, dy = columns // 256, columns % 256 // 64, columns // 16 % 4
+    wanted = (dz < 3) & (dy < 3) & (taps == 26 - (9 * dz + 3 * dy + dx))
+    spread = mm(weight, jnp.where(wanted, 1.0, 0.0).astype(BF))
+    rows = lax.broadcasted_iota(jnp.int32, (256, 768), 0)
+    lanes = lax.broadcasted_iota(jnp.int32, (256, 768), 1)
+    spread = jnp.where(rows % 16 == lanes % 16, spread, 0.0).astype(BF)
+    places = lax.broadcasted_iota(jnp.int32, (16, 256), 0)
+    inputs = lax.broadcasted_iota(jnp.int32, (16, 256), 1)
+    found = mm(jnp.where(places == inputs // 16, 1.0, 0.0).astype(BF), spread)
+    bases = [found[:, dx * 256 : (dx + 1) * 256] for dx in range(3)]
     kernel_ref[...] = shifted_kernels(bases)
 
 
@@ -683,10 +698,9 @@
     scales = (1.0 / math.sqrt(voxels), 1.0 / math.sqrt(devices))
     table = jnp.asarray(placement())
 
-    far, near = call_edges(cot, vol)
+    far = call_far_edge(cot, vol)
     pairs = [(i, i + 1) for i in range(1, count - 1, 2)]
     far_in = lax.ppermute(far, "space", pairs + [(b, a) for a, b in pairs])
-    near_in = partner(near, "space", 1)
 
     far, enc_grad, act, cot = after(far, enc_grad, act, cot)
     enc = jnp.pad(enc_grad, ((0, 0), (0, 0), (0, 8192 - 7376))).reshape(64, 128)
@@ -701,13 +715,15 @@
         return enc + got[:64], jnp.concatenate([state, got[64:]], axis=0)
 
     got = state_round(enc, state, 4)
-    inner_grad, cot_rows, act_edge = call_inner(act, cot, enc)
+    inner_grad, cot_rows, act_edge, near = call_inner(act, cot, vol, enc)
+    near_in = partner(near, "space", 1)
     got, inner_grad = after(got, inner_grad)
     enc, state = joined(enc, state, got)
     got = state_round(enc, state, 2)
     kernel = call_turn_weights(dec_weight.transpose(1, 2, 0), enc)
     act_edge, kernel = after(act_edge, kernel)
-    dec, rim_rows = call_outer(far_in, near_in, act_edge, inner_grad, enc)
+    before, near_rows = call_outer_near(near_in, act_edge, inner_grad, enc)
+    dec, rim_rows = call_outer_far(far_in, act_edge, before, near_rows)
     got, dec = after(got, dec)
     both, sent, state = call_merge(dec, enc, got, state)
     token = both

time: 48.6 us -> 48.2 us (level)
  waiting for transfers between devices: 6.43 us -> 7 us
  Pallas kernels: 19 us -> 18.5 us
    ppermute x6, waiting for transfers between devices: 3.2 us -> 3.79 us  [partner(): return lax.ppermute(value, axis, [(i, i ^ bit) for i in range(count)])]
    pallas_call x3 -> x4, Pallas kernels: 6.87 us -> 6.61 us  [the longest x1 3.56 us: call_inner(): kernel_call(inner, 'inner', [VM, VM, VM, VM], [jax.ShapeDtypeStruct((48,...]
  transfers between devices with their start and end apart: 13 -> 13, of which waited for: 5 -> 6; matrix products, arithmetic and copies ran while one was open for 0% -> 0% of each run, Pallas kernels for 34% -> 34%
where the time goes in v5:
time: 48.2 us; the launch traced here: 48.1 us
  starting transfers between devices  21.4 us (44%)
  Pallas kernels  18.5 us (38%)
  waiting for transfers between devices  7 us (15%)
  between operations  1.01 us (2%)
    ppermute x6, starting transfers between devices, partner(): return lax.ppermute(value, axis, [(i, i ^ bit) for i in range(count)])  10.4 us
    ppermute x6, starting transfers between devices, four(): lax.ppermute(given if n == 2 and given is not None else value, ('dp', 'sp...  10.2 us
    pallas_call x2, Pallas kernels, call_input_grad(): kernel_call(functools.partial(input_grad, part), f'input_grad_{part}', [V...  4.81 us
    ppermute x6, waiting for transfers between devices, partner(): return lax.ppermute(value, axis, [(i, i ^ bit) for i in range(count)])  3.79 us
    pallas_call x1, Pallas kernels, call_second_layer(): kernel_call(second_layer, 'second_layer', [VM, VM, VM, VM], FIELD, HELD,...  3.65 us
    pallas_call x1, Pallas kernels, call_inner(): kernel_call(inner, 'inner', [VM, VM, VM, VM], [jax.ShapeDtypeStruct((48,...  3.56 us
    ppermute x6, waiting for transfers between devices, four(): lax.ppermute(given if n == 2 and given is not None else value, ('dp', 'sp...  3.21 us
    pallas_call x1, Pallas kernels, call_far_edge(): kernel_call(far_edge, 'far_edge', [HBM, HBM], EDGE, [pltpu.VMEM((16, 128,...  1.35 us
  transfers between devices with their start and end apart: 13, of which 6 were waited for; matrix products, arithmetic and copies ran while one was open for 0% of the time, Pallas kernels for 34%

profile of v5, /device:TPU:0, one launch (start us, length us, event | category | flops | bytes accessed | tf_op | source)
XLA Modules:
  0.0 48.1 jit_solution(12967208313809809966)
XLA Ops:
  0.7 1.4 %far_edge.1 = bf16[144,16,128]{2,1,0:T(8,128)(2,1)S(1)} custom-call(bf16[16,4,128,128]{3,2,1,0:T(8,128)(2,1)} %bitcast.28, bf16[4,128,128]{2,1,0:T(8,128)(2,1)} %bitcast.24), custom_call_target="tpu_custom_call" | custom-call | flops 1380000000 | bytes 4320000 | tf_op jit(solution)/shard_map/far_edge/pallas_call | solution.py:102
  2.1 0.8 %collective-permute-start.2 = (bf16[144,16,128]{2,1,0:T(8,128)(2,1)S(1)}, bf16[144,16,128]{2,1,0:T(8,128)(2,1)S(1)}, u32[]{:S(2)}, u32[]{:S(2)}) collective-permute-start(bf16[144,16,128]{2,1,0:T(8,128)(2,1)S(1)} %far_edge.1), channel_id=1, source_target_pairs={{1,2},{3,4},{5,6},{7,8},{9,10},{11,12},{13,14},{2,1},{4,3},{6,5},{... | collective-permute-start | bytes 1769480 | tf_op jit(solution)/shard_map/ppermute | solution.py:703
  3.0 4.0 %collective-permute-start = (f32[112,128]{1,0:T(8,128)S(1)}, f32[112,128]{1,0:T(8,128)S(1)}, u32[]{:S(2)}, u32[]{:S(2)}) collective-permute-start(f32[112,128]{1,0:T(8,128)S(1)} %pad_maximum_fusion.1), channel_id=1, source_target_pairs={{0,64},{16,80},{32,96},{48,112},{64,0},{80,16},{96,32},{112,48},{1... | collective-permute-start | bytes 172040 | tf_op jit(solution)/shard_map/ppermute | solution.py:670
  7.1 3.6 %inner.1 = (f32[48,256]{1,0:T(8,128)S(1)}, bf16[4,130,16,128]{3,2,1,0:T(8,128)(2,1)S(1)}, bf16[2,3,128,16,128]{4,3,2,1,0:T(8,128)(2,1)S(1)}, bf16[144,16,128]{2,1,0:T(8,128)(2,1)S(1)}) custom-call(bf16[16,4,128,128]{3,2,1,0:T(8,128)(2,1)S(1)} %bitcast.27, bf16[16,4,128,128]{3,2,1,0:T(8,128)(2,1)S(1)} %bitcast.29, bf16[4,128,128]{2,1,0:T(8,128)(2,1)S(1)} %bitcast.25, ...), custom_call_target="tpu_custom_call" | custom-call | flops 4600000000 | bytes 14400000 | tf_op jit(solution)/shard_map/inner/pallas_call | solution.py:194
  10.6 2.6 %collective-permute-start.3 = (bf16[144,16,128]{2,1,0:T(8,128)(2,1)S(1)}, bf16[144,16,128]{2,1,0:T(8,128)(2,1)S(1)}, u32[]{:S(2)}, u32[]{:S(2)}) collective-permute-start(bf16[144,16,128]{2,1,0:T(8,128)(2,1)S(1)} %get-tuple-element.52), channel_id=1, source_target_pairs={{0,1},{1,0},{2,3},{3,2},{4,5},{5,4},{6,7},{7,6},{8,9},{9,8},{10,11... | collective-permute-start | bytes 1769480 | tf_op jit(solution)/shard_map/ppermute | solution.py:670
  13.3 1.1 %collective-permute-start.1 = (f32[160,128]{1,0:T(8,128)S(1)}, f32[160,128]{1,0:T(8,128)S(1)}, u32[]{:S(2)}, u32[]{:S(2)}) collective-permute-start(f32[160,128]{1,0:T(8,128)S(1)} %get-tuple-element.87), channel_id=1, source_target_pairs={{0,32},{16,48},{32,0},{48,16},{64,96},{80,112},{96,64},{112,80},{1... | collective-permute-start | bytes 245768 | tf_op jit(solution)/shard_map/ppermute | solution.py:670
  14.4 0.5 turn_weights.1.kernel_ref
  14.9 0.7 %outer_near.1 = (f32[48,256]{1,0:T(8,128)S(1)}, bf16[130,16,128]{2,1,0:T(8,128)(2,1)S(1)}) custom-call(bf16[144,16,128]{2,1,0:T(8,128)(2,1)S(1)} %collective-permute-done.3.near_ref, bf16[2,3,128,16,128]{4,3,2,1,0:T(8,128)(2,1)S(1)} %get-tuple-element.51.act_edge, f32[48,256]{1,0:T(8,128)S(1)} %get-tuple-element.53.inner_ref, ...), custom_call_target="tpu_custom_call" | custom-call | flops 1035000000 | bytes 3240000 | tf_op jit(solution)/shard_map/outer_near/pallas_call | solution.py:266
  15.6 1.0 %outer_far.1 = (f32[56,128]{1,0:T(8,128)S(1)}, bf16[2,130,16,128]{3,2,1,0:T(8,128)(2,1)S(1)}) custom-call(bf16[144,16,128]{2,1,0:T(8,128)(2,1)S(1)} %collective-permute-done.2.far_ref, bf16[2,3,128,16,128]{4,3,2,1,0:T(8,128)(2,1)S(1)} %get-tuple-element.51.act_edge, f32[48,256]{1,0:T(8,128)S(1)} %get-tuple-element.54.before_ref, ...), custom_call_target="tpu_custom_call" | custom-call | flops 1150000000 | bytes 3600000 | tf_op jit(solution)/shard_map/outer_far/pallas_call | solution.py:288
  16.6 1.2 %collective-permute-done.1.got_ref = f32[160,128]{1,0:T(8,128)S(1)} collective-permute-done((f32[160,128]{1,0:T(8,128)S(1)}, f32[160,128]{1,0:T(8,128)S(1)}, u32[]{:S(2)}, u32[]{:S(2)}) %collective-permute-start.1) | collective-permute-done | bytes 81952 | tf_op jit(solution)/shard_map/ppermute | solution.py:670
  17.9 5.1 %collective-permute-start.5 = (f32[112,128]{1,0:T(8,128)S(1)}, f32[112,128]{1,0:T(8,128)S(1)}, u32[]{:S(2)}, u32[]{:S(2)}) collective-permute-start(f32[112,128]{1,0:T(8,128)S(1)} %get-tuple-element.59.token_ref), channel_id=1, source_target_pairs={{0,24},{1,7},{2,26},{3,5},{4,28},{5,3},{6,30},{7,1},{8,16},{9,15},... | collective-permute-start | bytes 172040 | tf_op jit(solution)/shard_map/ppermute | solution.py:678
  22.9 0.9 %collective-permute-start.6 = (f32[304,128]{1,0:T(8,128)S(1)}, f32[304,128]{1,0:T(8,128)S(1)}, u32[]{:S(2)}, u32[]{:S(2)}) collective-permute-start(f32[304,128]{1,0:T(8,128)S(1)} %get-tuple-element.60), channel_id=1, source_target_pairs={{0,16},{1,3},{2,18},{3,1},{4,20},{5,7},{6,22},{7,5},{8,24},{9,11},... | collective-permute-start | bytes 466952 | tf_op jit(solution)/shard_map/ppermute | solution.py:678
  23.9 2.4 %input_grad_0.1.refs_0_ = bf16[16,4,128,128]{3,2,1,0:T(8,128)(2,1)} custom-call(bf16[192,256]{1,0:T(8,128)(2,1)S(1)} %turn_weights.1.kernel_ref, bf16[4,130,16,128]{3,2,1,0:T(8,128)(2,1)S(1)} %get-tuple-element.62.cot_ref, bf16[2,130,16,128]{3,2,1,0:T(8,128)(2,1)S(1)} %get-tuple-element.63.rim_ref, f32[112,128]{1,0:T(8,128)S(1)} %get-tuple-element.59.token_ref), custom_call_target="tpu_custom_call" | custom-call | flops 2529999872 | bytes 7920000 | tf_op jit(solution)/shard_map/input_grad_0/pallas_call | solution.py:375
  26.3 2.3 %collective-permute-done.4 = f32[112,128]{1,0:T(8,128)S(1)} collective-permute-done((f32[112,128]{1,0:T(8,128)S(1)}, f32[112,128]{1,0:T(8,128)S(1)}, u32[]{:S(2)}, u32[]{:S(2)}) %collective-permute-start.4) | collective-permute-done | bytes 57376 | tf_op jit(solution)/shard_map/ppermute | solution.py:678
  28.6 0.1 collective-permute-start.9
  28.7 1.7 %collective-permute-start.8 = (f32[112,128]{1,0:T(8,128)S(1)}, f32[112,128]{1,0:T(8,128)S(1)}, u32[]{:S(2)}, u32[]{:S(2)}) collective-permute-start(f32[112,128]{1,0:T(8,128)S(1)} %fusion.token_ref), channel_id=1, source_target_pairs={{0,6},{1,25},{2,4},{3,27},{4,2},{5,29},{6,0},{7,31},{8,14},{9,17},... | collective-permute-start | bytes 172040 | tf_op jit(solution)/shard_map/ppermute | solution.py:678
  30.5 2.3 %collective-permute-start.7 = (f32[112,128]{1,0:T(8,128)S(1)}, f32[112,128]{1,0:T(8,128)S(1)}, u32[]{:S(2)}, u32[]{:S(2)}) collective-permute-start(f32[112,128]{1,0:T(8,128)S(1)} %fusion.token_ref), channel_id=1, source_target_pairs={{0,4},{1,9},{2,6},{3,11},{4,0},{5,13},{6,2},{7,15},{8,12},{9,1},{1... | collective-permute-start | bytes 172040 | tf_op jit(solution)/shard_map/ppermute | solution.py:678
  32.8 2.4 %input_grad_1.1 = bf16[16,4,128,128]{3,2,1,0:T(8,128)(2,1)} custom-call(bf16[192,256]{1,0:T(8,128)(2,1)S(1)} %turn_weights.1.kernel_ref, bf16[4,130,16,128]{3,2,1,0:T(8,128)(2,1)S(1)} %get-tuple-element.62.cot_ref, bf16[2,130,16,128]{3,2,1,0:T(8,128)(2,1)S(1)} %get-tuple-element.63.rim_ref, ...), custom_call_target="tpu_custom_call", output_to_operand_aliasing={{}: (4, {})} | custom-call | flops 2529999872 | bytes 7920000 | tf_op jit(solution)/shard_map/input_grad_1/pallas_call | solution.py:375
  35.3 0.9 %collective-permute-done.7 = f32[112,128]{1,0:T(8,128)S(1)} collective-permute-done((f32[112,128]{1,0:T(8,128)S(1)}, f32[112,128]{1,0:T(8,128)S(1)}, u32[]{:S(2)}, u32[]{:S(2)}) %collective-permute-start.7) | collective-permute-done | bytes 57376 | tf_op jit(solution)/shard_map/ppermute | solution.py:678
  36.2 0.1 collective-permute-start.10
  36.3 0.0 copy-start.4
  36.3 0.3 volume_windows.1.cells_ref
  36.6 1.1 %collective-permute-done.10.got_ref = f32[304,128]{1,0:T(8,128)S(1)} collective-permute-done((f32[304,128]{1,0:T(8,128)S(1)}, f32[304,128]{1,0:T(8,128)S(1)}, u32[]{:S(2)}, u32[]{:S(2)}) %collective-permute-start.10) | collective-permute-done | bytes 155680 | tf_op jit(solution)/shard_map/ppermute | solution.py:670
  37.7 0.2 gather_state.1
  37.8 1.3 %collective-permute-start.11 = (f32[56,128]{1,0:T(8,128)S(1)}, f32[56,128]{1,0:T(8,128)S(1)}, u32[]{:S(2)}, u32[]{:S(2)}) collective-permute-start(f32[56,128]{1,0:T(8,128)S(1)} %slice.22.token_ref), channel_id=1, source_target_pairs={{0,32},{16,48},{32,0},{48,16},{64,96},{80,112},{96,64},{112,80},{1... | collective-permute-start | bytes 86024 | tf_op jit(solution)/shard_map/ppermute | solution.py:670
  39.1 0.6 %update_encoder.1 = (bf16[192,256]{1,0:T(8,128)(2,1)S(1)}, bf16[256,256]{1,0:T(8,128)(2,1)S(1)}, f32[16,128]{1,0:T(8,128)S(1)}) custom-call(f32[112,128]{1,0:T(8,128)S(1)} %get-tuple-element.70.grad_ref.enc_ref, f32[3,112,128]{2,1,0:T(8,128)S(1)} %get-tuple-element.71.state_ref, bf16[8,64,1408]{2,1,0:T(8,128)(2,1)S(1)} %copy-done.4), custom_call_target="tpu_custom_call" | custom-call | flops 690000000 | bytes 2160000 | tf_op jit(solution)/shard_map/update_encoder/pallas_call | solution.py:437
  39.7 1.2 %first_layer.1.first = bf16[6,130,16,128]{3,2,1,0:T(8,128)(2,1)S(1)} custom-call(bf16[256,256]{1,0:T(8,128)(2,1)S(1)} %get-tuple-element.72.one_ref, bf16[2,3,8,8,16,128]{5,4,3,2,1,0:T(8,128)(2,1)S(1)} %volume_windows.1.cells_ref, f32[56,128]{1,0:T(8,128)S(1)} %slice.22.token_ref), custom_call_target="tpu_custom_call" | custom-call | flops 1724999936 | bytes 5400000 | tf_op jit(solution)/shard_map/first_layer/pallas_call | solution.py:640
  40.9 1.1 %collective-permute-done.11 = f32[56,128]{1,0:T(8,128)S(1)} collective-permute-done((f32[56,128]{1,0:T(8,128)S(1)}, f32[56,128]{1,0:T(8,128)S(1)}, u32[]{:S(2)}, u32[]{:S(2)}) %collective-permute-start.11) | collective-permute-done | bytes 28704 | tf_op jit(solution)/shard_map/ppermute | solution.py:670
  42.0 1.3 %collective-permute-start.12 = (f32[56,128]{1,0:T(8,128)S(1)}, f32[56,128]{1,0:T(8,128)S(1)}, u32[]{:S(2)}, u32[]{:S(2)}) collective-permute-start(f32[56,128]{1,0:T(8,128)S(1)} %slice_add_fusion.2.token_ref), channel_id=1, source_target_pairs={{0,64},{16,80},{32,96},{48,112},{64,0},{80,16},{96,32},{112,48},{1... | collective-permute-start | bytes 86024 | tf_op jit(solution)/shard_map/ppermute | solution.py:670
  43.3 3.7 %second_layer.1 = bf16[16,4,128,128]{3,2,1,0:T(8,128)(2,1)} custom-call(bf16[192,256]{1,0:T(8,128)(2,1)S(1)} %get-tuple-element.75.two_ref, f32[16,128]{1,0:T(8,128)S(1)} %get-tuple-element.76.bias_ref, bf16[6,130,16,128]{3,2,1,0:T(8,128)(2,1)S(1)} %first_layer.1.first, f32[56,128]{1,0:T(8,128)S(1)} %slice_add_fusion.2.token_ref), custom_call_target="tpu_custom_call" | custom-call | flops 4830000128 | bytes 15120000 | tf_op jit(solution)/shard_map/second_layer/pallas_call | solution.py:657
  46.9 0.4 collective-permute-done.12
  47.3 0.7 %finish.1 = (bf16[112,128]{1,0:T(8,128)(2,1)}, f32[1786]{0:T(1024)}, f32[1786]{0:T(1024)}, f32[1786]{0:T(1024)}) custom-call(f32[56,128]{1,0:T(8,128)S(1)} %add.43.dec_ref, f32[112,128]{1,0:T(8,128)S(1)} %get-tuple-element.70.grad_ref.enc_ref, f32[3,112,128]{2,1,0:T(8,128)S(1)} %get-tuple-element.71.state_ref, f32[48,128]{1,0:T(8,128)S(1)} %pad_maximum_fusion.3.own_ref), custom_call_target="tpu_custom_call" | custom-call | flops 1150000000 | bytes 3600000 | tf_op jit(solution)/shard_map/finish/pallas_call | solution.py:527
  (44 shorter events, 0.2 us)
Async XLA Ops:
  0.6 2.3 %copy-start.5 = (f32[1786]{0:T(1024)S(1)}, f32[1786]{0:T(1024)}, u32[]{:S(2)}) copy-start(f32[1786]{0:T(1024)} %param.14) | copy-start | bytes 21436
  0.6 2.3 %copy-start.6 = (f32[1786]{0:T(1024)S(1)}, f32[1786]{0:T(1024)}, u32[]{:S(2)}) copy-start(f32[1786]{0:T(1024)} %param.15) | copy-start | bytes 21436
  0.7 2.3 %copy-start.7 = (f32[1786]{0:T(1024)S(1)}, f32[1786]{0:T(1024)}, u32[]{:S(2)}) copy-start(f32[1786]{0:T(1024)} %param.16) | copy-start | bytes 21436
  0.7 2.3 %copy-start.8 = (f32[1,1,7376]{2,1,0:T(1,128)S(1)}, f32[1,1,7376]{2,1,0:T(1,128)}, u32[]{:S(2)}) copy-start(f32[1,1,7376]{2,1,0:T(1,128)} %param.13) | copy-start | bytes 88516
  0.7 6.4 %copy-start = (bf16[1,1,4,128,128]{4,3,2,1,0:T(8,128)(2,1)S(1)}, bf16[1,1,4,128,128]{4,3,2,1,0:T(8,128)(2,1)}, u32[]{:S(2)}) copy-start(bf16[1,1,4,128,128]{4,3,2,1,0:T(8,128)(2,1)} %param.11) | copy-start | bytes 393220
  0.7 6.4 %copy-start.1 = (bf16[1,16,4,128,128]{4,3,2,1,0:T(8,128)(2,1)S(1)}, bf16[1,16,4,128,128]{4,3,2,1,0:T(8,128)(2,1)}, u32[]{:S(2)}) copy-start(bf16[1,16,4,128,128]{4,3,2,1,0:T(8,128)(2,1)} %param.9) | copy-start | bytes 6291460
  0.7 6.4 %copy-start.2 = (bf16[1,16,4,128,128]{4,3,2,1,0:T(8,128)(2,1)S(1)}, bf16[1,16,4,128,128]{4,3,2,1,0:T(8,128)(2,1)}, u32[]{:S(2)}) copy-start(bf16[1,16,4,128,128]{4,3,2,1,0:T(8,128)(2,1)} %param.10) | copy-start | bytes 6291460
  2.1 13.5 %collective-permute-start.2 = (bf16[144,16,128]{2,1,0:T(8,128)(2,1)S(1)}, bf16[144,16,128]{2,1,0:T(8,128)(2,1)S(1)}, u32[]{:S(2)}, u32[]{:S(2)}) collective-permute-start(bf16[144,16,128]{2,1,0:T(8,128)(2,1)S(1)} %far_edge.1), channel_id=1, source_target_pairs={{1,2},{3,4},{5,6},{7,8},{9,10},{11,12},{13,14},{2,1},{4,3},{6,5},{... | collective-permute-start | bytes 1769480 | tf_op jit(solution)/shard_map/ppermute | solution.py:703
  3.0 11.4 %copy-start.3 = (bf16[27,16,16]{0,2,1:T(8,128)(2,1)S(1)}, bf16[27,16,16]{0,2,1:T(8,128)(2,1)}, u32[]{:S(2)}) copy-start(bf16[27,16,16]{0,2,1:T(8,128)(2,1)} %param.12) | copy-start | bytes 41476
  3.0 10.2 %collective-permute-start = (f32[112,128]{1,0:T(8,128)S(1)}, f32[112,128]{1,0:T(8,128)S(1)}, u32[]{:S(2)}, u32[]{:S(2)}) collective-permute-start(f32[112,128]{1,0:T(8,128)S(1)} %pad_maximum_fusion.1), channel_id=1, source_target_pairs={{0,64},{16,80},{32,96},{48,112},{64,0},{80,16},{96,32},{112,48},{1... | collective-permute-start | bytes 172040 | tf_op jit(solution)/shard_map/ppermute | solution.py:670
  10.6 4.2 %collective-permute-start.3 = (bf16[144,16,128]{2,1,0:T(8,128)(2,1)S(1)}, bf16[144,16,128]{2,1,0:T(8,128)(2,1)S(1)}, u32[]{:S(2)}, u32[]{:S(2)}) collective-permute-start(bf16[144,16,128]{2,1,0:T(8,128)(2,1)S(1)} %get-tuple-element.52), channel_id=1, source_target_pairs={{0,1},{1,0},{2,3},{3,2},{4,5},{5,4},{6,7},{7,6},{8,9},{9,8},{10,11... | collective-permute-start | bytes 1769480 | tf_op jit(solution)/shard_map/ppermute | solution.py:670
  13.3 4.5 %collective-permute-start.1 = (f32[160,128]{1,0:T(8,128)S(1)}, f32[160,128]{1,0:T(8,128)S(1)}, u32[]{:S(2)}, u32[]{:S(2)}) collective-permute-start(f32[160,128]{1,0:T(8,128)S(1)} %get-tuple-element.87), channel_id=1, source_target_pairs={{0,32},{16,48},{32,0},{48,16},{64,96},{80,112},{96,64},{112,80},{1... | collective-permute-start | bytes 245768 | tf_op jit(solution)/shard_map/ppermute | solution.py:670
  17.9 8.4 %collective-permute-start.5 = (f32[112,128]{1,0:T(8,128)S(1)}, f32[112,128]{1,0:T(8,128)S(1)}, u32[]{:S(2)}, u32[]{:S(2)}) collective-permute-start(f32[112,128]{1,0:T(8,128)S(1)} %get-tuple-element.59.token_ref), channel_id=1, source_target_pairs={{0,24},{1,7},{2,26},{3,5},{4,28},{5,3},{6,30},{7,1},{8,16},{9,15},... | collective-permute-start | bytes 172040 | tf_op jit(solution)/shard_map/ppermute | solution.py:678
  22.9 5.7 %collective-permute-start.4 = (f32[112,128]{1,0:T(8,128)S(1)}, f32[112,128]{1,0:T(8,128)S(1)}, u32[]{:S(2)}, u32[]{:S(2)}) collective-permute-start(f32[112,128]{1,0:T(8,128)S(1)} %get-tuple-element.59.token_ref), channel_id=1, source_target_pairs={{0,8},{1,5},{2,10},{3,7},{4,12},{5,1},{6,14},{7,3},{8,0},{9,13},{1... | collective-permute-start | bytes 172040 | tf_op jit(solution)/shard_map/ppermute | solution.py:678
  22.9 5.7 %collective-permute-start.6 = (f32[304,128]{1,0:T(8,128)S(1)}, f32[304,128]{1,0:T(8,128)S(1)}, u32[]{:S(2)}, u32[]{:S(2)}) collective-permute-start(f32[304,128]{1,0:T(8,128)S(1)} %get-tuple-element.60), channel_id=1, source_target_pairs={{0,16},{1,3},{2,18},{3,1},{4,20},{5,7},{6,22},{7,5},{8,24},{9,11},... | collective-permute-start | bytes 466952 | tf_op jit(solution)/shard_map/ppermute | solution.py:678
  28.6 6.6 %collective-permute-start.9 = (f32[112,128]{1,0:T(8,128)S(1)}, f32[112,128]{1,0:T(8,128)S(1)}, u32[]{:S(2)}, u32[]{:S(2)}) collective-permute-start(f32[112,128]{1,0:T(8,128)S(1)} %fusion.token_ref), channel_id=1, source_target_pairs={{0,2},{1,17},{2,0},{3,19},{4,6},{5,21},{6,4},{7,23},{8,10},{9,25},... | collective-permute-start | bytes 172040 | tf_op jit(solution)/shard_map/ppermute | solution.py:678
  28.7 6.5 %collective-permute-start.8 = (f32[112,128]{1,0:T(8,128)S(1)}, f32[112,128]{1,0:T(8,128)S(1)}, u32[]{:S(2)}, u32[]{:S(2)}) collective-permute-start(f32[112,128]{1,0:T(8,128)S(1)} %fusion.token_ref), channel_id=1, source_target_pairs={{0,6},{1,25},{2,4},{3,27},{4,2},{5,29},{6,0},{7,31},{8,14},{9,17},... | collective-permute-start | bytes 172040 | tf_op jit(solution)/shard_map/ppermute | solution.py:678
  30.5 5.7 %collective-permute-start.7 = (f32[112,128]{1,0:T(8,128)S(1)}, f32[112,128]{1,0:T(8,128)S(1)}, u32[]{:S(2)}, u32[]{:S(2)}) collective-permute-start(f32[112,128]{1,0:T(8,128)S(1)} %fusion.token_ref), channel_id=1, source_target_pairs={{0,4},{1,9},{2,6},{3,11},{4,0},{5,13},{6,2},{7,15},{8,12},{9,1},{1... | collective-permute-start | bytes 172040 | tf_op jit(solution)/shard_map/ppermute | solution.py:678
  36.2 1.5 %collective-permute-start.10 = (f32[304,128]{1,0:T(8,128)S(1)}, f32[304,128]{1,0:T(8,128)S(1)}, u32[]{:S(2)}, u32[]{:S(2)}) collective-permute-start(f32[304,128]{1,0:T(8,128)S(1)} %pad_maximum_fusion), channel_id=1, source_target_pairs={{0,1},{1,0},{2,3},{3,2},{4,5},{5,4},{6,7},{7,6},{8,9},{9,8},{10,11... | collective-permute-start | bytes 466952 | tf_op jit(solution)/shard_map/ppermute | solution.py:670
  36.3 2.8 %copy-start.4 = (bf16[8,64,1408]{2,1,0:T(8,128)(2,1)S(1)}, bf16[8,64,1408]{2,1,0:T(8,128)(2,1)}, u32[]{:S(2)}) copy-start(bf16[8,64,1408]{2,1,0:T(8,128)(2,1)} %constant.5.clone.table_ref) | copy-start | bytes 4325380
  37.8 4.1 %collective-permute-start.11 = (f32[56,128]{1,0:T(8,128)S(1)}, f32[56,128]{1,0:T(8,128)S(1)}, u32[]{:S(2)}, u32[]{:S(2)}) collective-permute-start(f32[56,128]{1,0:T(8,128)S(1)} %slice.22.token_ref), channel_id=1, source_target_pairs={{0,32},{16,48},{32,0},{48,16},{64,96},{80,112},{96,64},{112,80},{1... | collective-permute-start | bytes 86024 | tf_op jit(solution)/shard_map/ppermute | solution.py:670
  42.0 5.4 %collective-permute-start.12 = (f32[56,128]{1,0:T(8,128)S(1)}, f32[56,128]{1,0:T(8,128)S(1)}, u32[]{:S(2)}, u32[]{:S(2)}) collective-permute-start(f32[56,128]{1,0:T(8,128)S(1)} %slice_add_fusion.2.token_ref), channel_id=1, source_target_pairs={{0,64},{16,80},{32,96},{48,112},{64,0},{80,16},{96,32},{112,48},{1... | collective-permute-start | bytes 86024 | tf_op jit(solution)/shard_map/ppermute | solution.py:670

commit v6 on v5

--- a/solution.py
+++ b/solution.py
@@ -337,9 +337,9 @@
     copies = []
     for place, block in enumerate(blocks):
         compute(block)
-        if place % 2 and place > 1:
-            copies += [flush(blocks[place - 3]), flush(blocks[place - 2])]
-    copies += [flush(block) for block in blocks[-2:]]
+        if place:
+            copies.append(flush(blocks[place - 1]))
+    copies.append(flush(blocks[-1]))
     for copy in copies:
         copy.wait()
 
@@ -702,7 +702,7 @@
     pairs = [(i, i + 1) for i in range(1, count - 1, 2)]
     far_in = lax.ppermute(far, "space", pairs + [(b, a) for a, b in pairs])
 
-    far, enc_grad, act, cot = after(far, enc_grad, act, cot)
+    far, enc_grad, act, cot, vol = after(far, enc_grad, act, cot, vol)
     enc = jnp.pad(enc_grad, ((0, 0), (0, 0), (0, 8192 - 7376))).reshape(64, 128)
     pad = lambda value: jnp.pad(value, (0, 2048 - 1786)).reshape(16, 128)
     own = jnp.concatenate([pad(params), pad(moment), pad(second)], axis=0)

time: 48.2 us -> 48.2 us (level)
  no operation moved by 1% of the time
where the time goes in v6:
time: 48.2 us; the launch traced here: 48.1 us
  starting transfers between devices  21.4 us (44%)
  Pallas kernels  18.5 us (38%)
  waiting for transfers between devices  6.96 us (14%)
  between operations  1.01 us (2%)
    ppermute x6, starting transfers between devices, partner(): return lax.ppermute(value, axis, [(i, i ^ bit) for i in range(count)])  10.4 us
    ppermute x6, starting transfers between devices, four(): lax.ppermute(given if n == 2 and given is not None else value, ('dp', 'sp...  10.2 us
    pallas_call x2, Pallas kernels, call_input_grad(): kernel_call(functools.partial(input_grad, part), f'input_grad_{part}', [V...  4.83 us
    ppermute x6, waiting for transfers between devices, partner(): return lax.ppermute(value, axis, [(i, i ^ bit) for i in range(count)])  3.76 us
    pallas_call x1, Pallas kernels, call_second_layer(): kernel_call(second_layer, 'second_layer', [VM, VM, VM, VM], FIELD, HELD,...  3.68 us
    pallas_call x1, Pallas kernels, call_inner(): kernel_call(inner, 'inner', [VM, VM, VM, VM], [jax.ShapeDtypeStruct((48,...  3.56 us
    ppermute x6, waiting for transfers between devices, four(): lax.ppermute(given if n == 2 and given is not None else value, ('dp', 'sp...  3.2 us
    pallas_call x1, Pallas kernels, call_far_edge(): kernel_call(far_edge, 'far_edge', [HBM, HBM], EDGE, [pltpu.VMEM((16, 128,...  1.35 us
  transfers between devices with their start and end apart: 13, of which 6 were waited for; matrix products, arithmetic and copies ran while one was open for 0% of the time, Pallas kernels for 34%

profile of v6, /device:TPU:0, one launch (start us, length us, event | category | flops | bytes accessed | tf_op | source)
XLA Modules:
  0.0 48.1 jit_solution(16008758507065478898)
XLA Ops:
  0.7 1.4 %far_edge.1 = bf16[144,16,128]{2,1,0:T(8,128)(2,1)S(1)} custom-call(bf16[16,4,128,128]{3,2,1,0:T(8,128)(2,1)} %bitcast.28, bf16[4,128,128]{2,1,0:T(8,128)(2,1)} %bitcast.24), custom_call_target="tpu_custom_call" | custom-call | flops 1380000000 | bytes 4320000 | tf_op jit(solution)/shard_map/far_edge/pallas_call | solution.py:102
  2.1 0.8 %collective-permute-start.2 = (bf16[144,16,128]{2,1,0:T(8,128)(2,1)S(1)}, bf16[144,16,128]{2,1,0:T(8,128)(2,1)S(1)}, u32[]{:S(2)}, u32[]{:S(2)}) collective-permute-start(bf16[144,16,128]{2,1,0:T(8,128)(2,1)S(1)} %far_edge.1), channel_id=1, source_target_pairs={{1,2},{3,4},{5,6},{7,8},{9,10},{11,12},{13,14},{2,1},{4,3},{6,5},{... | collective-permute-start | bytes 1769480 | tf_op jit(solution)/shard_map/ppermute | solution.py:703
  3.0 4.0 %collective-permute-start = (f32[112,128]{1,0:T(8,128)S(1)}, f32[112,128]{1,0:T(8,128)S(1)}, u32[]{:S(2)}, u32[]{:S(2)}) collective-permute-start(f32[112,128]{1,0:T(8,128)S(1)} %pad_maximum_fusion.1), channel_id=1, source_target_pairs={{0,64},{16,80},{32,96},{48,112},{64,0},{80,16},{96,32},{112,48},{1... | collective-permute-start | bytes 172040 | tf_op jit(solution)/shard_map/ppermute | solution.py:670
  7.1 3.6 %inner.1 = (f32[48,256]{1,0:T(8,128)S(1)}, bf16[4,130,16,128]{3,2,1,0:T(8,128)(2,1)S(1)}, bf16[2,3,128,16,128]{4,3,2,1,0:T(8,128)(2,1)S(1)}, bf16[144,16,128]{2,1,0:T(8,128)(2,1)S(1)}) custom-call(bf16[16,4,128,128]{3,2,1,0:T(8,128)(2,1)S(1)} %bitcast.27, bf16[16,4,128,128]{3,2,1,0:T(8,128)(2,1)S(1)} %bitcast.29, bf16[4,128,128]{2,1,0:T(8,128)(2,1)S(1)} %bitcast.25, ...), custom_call_target="tpu_custom_call" | custom-call | flops 4600000000 | bytes 14400000 | tf_op jit(solution)/shard_map/inner/pallas_call | solution.py:194
  10.6 2.6 %collective-permute-start.3 = (bf16[144,16,128]{2,1,0:T(8,128)(2,1)S(1)}, bf16[144,16,128]{2,1,0:T(8,128)(2,1)S(1)}, u32[]{:S(2)}, u32[]{:S(2)}) collective-permute-start(bf16[144,16,128]{2,1,0:T(8,128)(2,1)S(1)} %get-tuple-element.54), channel_id=1, source_target_pairs={{0,1},{1,0},{2,3},{3,2},{4,5},{5,4},{6,7},{7,6},{8,9},{9,8},{10,11... | collective-permute-start | bytes 1769480 | tf_op jit(solution)/shard_map/ppermute | solution.py:670
  13.3 1.1 %collective-permute-start.1 = (f32[160,128]{1,0:T(8,128)S(1)}, f32[160,128]{1,0:T(8,128)S(1)}, u32[]{:S(2)}, u32[]{:S(2)}) collective-permute-start(f32[160,128]{1,0:T(8,128)S(1)} %get-tuple-element.89), channel_id=1, source_target_pairs={{0,32},{16,48},{32,0},{48,16},{64,96},{80,112},{96,64},{112,80},{1... | collective-permute-start | bytes 245768 | tf_op jit(solution)/shard_map/ppermute | solution.py:670
  14.4 0.5 turn_weights.1.kernel_ref
  14.9 0.7 %outer_near.1 = (f32[48,256]{1,0:T(8,128)S(1)}, bf16[130,16,128]{2,1,0:T(8,128)(2,1)S(1)}) custom-call(bf16[144,16,128]{2,1,0:T(8,128)(2,1)S(1)} %collective-permute-done.3.near_ref, bf16[2,3,128,16,128]{4,3,2,1,0:T(8,128)(2,1)S(1)} %get-tuple-element.53.act_edge, f32[48,256]{1,0:T(8,128)S(1)} %get-tuple-element.55.inner_ref, ...), custom_call_target="tpu_custom_call" | custom-call | flops 1035000000 | bytes 3240000 | tf_op jit(solution)/shard_map/outer_near/pallas_call | solution.py:266
  15.6 1.0 %outer_far.1 = (f32[56,128]{1,0:T(8,128)S(1)}, bf16[2,130,16,128]{3,2,1,0:T(8,128)(2,1)S(1)}) custom-call(bf16[144,16,128]{2,1,0:T(8,128)(2,1)S(1)} %collective-permute-done.2.far_ref, bf16[2,3,128,16,128]{4,3,2,1,0:T(8,128)(2,1)S(1)} %get-tuple-element.53.act_edge, f32[48,256]{1,0:T(8,128)S(1)} %get-tuple-element.56.before_ref, ...), custom_call_target="tpu_custom_call" | custom-call | flops 1150000000 | bytes 3600000 | tf_op jit(solution)/shard_map/outer_far/pallas_call | solution.py:288
  16.6 1.2 %collective-permute-done.1.got_ref = f32[160,128]{1,0:T(8,128)S(1)} collective-permute-done((f32[160,128]{1,0:T(8,128)S(1)}, f32[160,128]{1,0:T(8,128)S(1)}, u32[]{:S(2)}, u32[]{:S(2)}) %collective-permute-start.1) | collective-permute-done | bytes 81952 | tf_op jit(solution)/shard_map/ppermute | solution.py:670
  17.9 5.1 %collective-permute-start.5 = (f32[112,128]{1,0:T(8,128)S(1)}, f32[112,128]{1,0:T(8,128)S(1)}, u32[]{:S(2)}, u32[]{:S(2)}) collective-permute-start(f32[112,128]{1,0:T(8,128)S(1)} %get-tuple-element.61.token_ref), channel_id=1, source_target_pairs={{0,24},{1,7},{2,26},{3,5},{4,28},{5,3},{6,30},{7,1},{8,16},{9,15},... | collective-permute-start | bytes 172040 | tf_op jit(solution)/shard_map/ppermute | solution.py:678
  22.9 0.9 %collective-permute-start.6 = (f32[304,128]{1,0:T(8,128)S(1)}, f32[304,128]{1,0:T(8,128)S(1)}, u32[]{:S(2)}, u32[]{:S(2)}) collective-permute-start(f32[304,128]{1,0:T(8,128)S(1)} %get-tuple-element.62), channel_id=1, source_target_pairs={{0,16},{1,3},{2,18},{3,1},{4,20},{5,7},{6,22},{7,5},{8,24},{9,11},... | collective-permute-start | bytes 466952 | tf_op jit(solution)/shard_map/ppermute | solution.py:678
  23.9 2.4 %input_grad_0.1.refs_0_ = bf16[16,4,128,128]{3,2,1,0:T(8,128)(2,1)} custom-call(bf16[192,256]{1,0:T(8,128)(2,1)S(1)} %turn_weights.1.kernel_ref, bf16[4,130,16,128]{3,2,1,0:T(8,128)(2,1)S(1)} %get-tuple-element.64.cot_ref, bf16[2,130,16,128]{3,2,1,0:T(8,128)(2,1)S(1)} %get-tuple-element.65.rim_ref, f32[112,128]{1,0:T(8,128)S(1)} %get-tuple-element.61.token_ref), custom_call_target="tpu_custom_call" | custom-call | flops 2529999872 | bytes 7920000 | tf_op jit(solution)/shard_map/input_grad_0/pallas_call | solution.py:375
  26.3 2.3 %collective-permute-done.4 = f32[112,128]{1,0:T(8,128)S(1)} collective-permute-done((f32[112,128]{1,0:T(8,128)S(1)}, f32[112,128]{1,0:T(8,128)S(1)}, u32[]{:S(2)}, u32[]{:S(2)}) %collective-permute-start.4) | collective-permute-done | bytes 57376 | tf_op jit(solution)/shard_map/ppermute | solution.py:678
  28.6 0.1 collective-permute-start.9
  28.7 1.7 %collective-permute-start.8 = (f32[112,128]{1,0:T(8,128)S(1)}, f32[112,128]{1,0:T(8,128)S(1)}, u32[]{:S(2)}, u32[]{:S(2)}) collective-permute-start(f32[112,128]{1,0:T(8,128)S(1)} %fusion.token_ref), channel_id=1, source_target_pairs={{0,6},{1,25},{2,4},{3,27},{4,2},{5,29},{6,0},{7,31},{8,14},{9,17},... | collective-permute-start | bytes 172040 | tf_op jit(solution)/shard_map/ppermute | solution.py:678
  30.5 2.3 %collective-permute-start.7 = (f32[112,128]{1,0:T(8,128)S(1)}, f32[112,128]{1,0:T(8,128)S(1)}, u32[]{:S(2)}, u32[]{:S(2)}) collective-permute-start(f32[112,128]{1,0:T(8,128)S(1)} %fusion.token_ref), channel_id=1, source_target_pairs={{0,4},{1,9},{2,6},{3,11},{4,0},{5,13},{6,2},{7,15},{8,12},{9,1},{1... | collective-permute-start | bytes 172040 | tf_op jit(solution)/shard_map/ppermute | solution.py:678
  32.8 2.4 %input_grad_1.1 = bf16[16,4,128,128]{3,2,1,0:T(8,128)(2,1)} custom-call(bf16[192,256]{1,0:T(8,128)(2,1)S(1)} %turn_weights.1.kernel_ref, bf16[4,130,16,128]{3,2,1,0:T(8,128)(2,1)S(1)} %get-tuple-element.64.cot_ref, bf16[2,130,16,128]{3,2,1,0:T(8,128)(2,1)S(1)} %get-tuple-element.65.rim_ref, ...), custom_call_target="tpu_custom_call", output_to_operand_aliasing={{}: (4, {})} | custom-call | flops 2529999872 | bytes 7920000 | tf_op jit(solution)/shard_map/input_grad_1/pallas_call | solution.py:375
  35.3 0.9 %collective-permute-done.7 = f32[112,128]{1,0:T(8,128)S(1)} collective-permute-done((f32[112,128]{1,0:T(8,128)S(1)}, f32[112,128]{1,0:T(8,128)S(1)}, u32[]{:S(2)}, u32[]{:S(2)}) %collective-permute-start.7) | collective-permute-done | bytes 57376 | tf_op jit(solution)/shard_map/ppermute | solution.py:678
  36.2 0.1 collective-permute-start.10
  36.3 0.0 copy-start.4
  36.3 0.3 volume_windows.1.cells_ref
  36.6 1.1 %collective-permute-done.10.got_ref = f32[304,128]{1,0:T(8,128)S(1)} collective-permute-done((f32[304,128]{1,0:T(8,128)S(1)}, f32[304,128]{1,0:T(8,128)S(1)}, u32[]{:S(2)}, u32[]{:S(2)}) %collective-permute-start.10) | collective-permute-done | bytes 155680 | tf_op jit(solution)/shard_map/ppermute | solution.py:670
  37.7 0.2 gather_state.1
  37.8 1.3 %collective-permute-start.11 = (f32[56,128]{1,0:T(8,128)S(1)}, f32[56,128]{1,0:T(8,128)S(1)}, u32[]{:S(2)}, u32[]{:S(2)}) collective-permute-start(f32[56,128]{1,0:T(8,128)S(1)} %slice.22.token_ref), channel_id=1, source_target_pairs={{0,32},{16,48},{32,0},{48,16},{64,96},{80,112},{96,64},{112,80},{1... | collective-permute-start | bytes 86024 | tf_op jit(solution)/shard_map/ppermute | solution.py:670
  39.1 0.6 %update_encoder.1 = (bf16[192,256]{1,0:T(8,128)(2,1)S(1)}, bf16[256,256]{1,0:T(8,128)(2,1)S(1)}, f32[16,128]{1,0:T(8,128)S(1)}) custom-call(f32[112,128]{1,0:T(8,128)S(1)} %get-tuple-element.72.grad_ref.enc_ref, f32[3,112,128]{2,1,0:T(8,128)S(1)} %get-tuple-element.73.state_ref, bf16[8,64,1408]{2,1,0:T(8,128)(2,1)S(1)} %copy-done.4), custom_call_target="tpu_custom_call" | custom-call | flops 690000000 | bytes 2160000 | tf_op jit(solution)/shard_map/update_encoder/pallas_call | solution.py:437
  39.7 1.2 %first_layer.1.first = bf16[6,130,16,128]{3,2,1,0:T(8,128)(2,1)S(1)} custom-call(bf16[256,256]{1,0:T(8,128)(2,1)S(1)} %get-tuple-element.74.one_ref, bf16[2,3,8,8,16,128]{5,4,3,2,1,0:T(8,128)(2,1)S(1)} %volume_windows.1.cells_ref, f32[56,128]{1,0:T(8,128)S(1)} %slice.22.token_ref), custom_call_target="tpu_custom_call" | custom-call | flops 1724999936 | bytes 5400000 | tf_op jit(solution)/shard_map/first_layer/pallas_call | solution.py:640
  40.9 1.1 %collective-permute-done.11 = f32[56,128]{1,0:T(8,128)S(1)} collective-permute-done((f32[56,128]{1,0:T(8,128)S(1)}, f32[56,128]{1,0:T(8,128)S(1)}, u32[]{:S(2)}, u32[]{:S(2)}) %collective-permute-start.11) | collective-permute-done | bytes 28704 | tf_op jit(solution)/shard_map/ppermute | solution.py:670
  42.0 1.3 %collective-permute-start.12 = (f32[56,128]{1,0:T(8,128)S(1)}, f32[56,128]{1,0:T(8,128)S(1)}, u32[]{:S(2)}, u32[]{:S(2)}) collective-permute-start(f32[56,128]{1,0:T(8,128)S(1)} %slice_add_fusion.2.token_ref), channel_id=1, source_target_pairs={{0,64},{16,80},{32,96},{48,112},{64,0},{80,16},{96,32},{112,48},{1... | collective-permute-start | bytes 86024 | tf_op jit(solution)/shard_map/ppermute | solution.py:670
  43.3 3.7 %second_layer.1 = bf16[16,4,128,128]{3,2,1,0:T(8,128)(2,1)} custom-call(bf16[192,256]{1,0:T(8,128)(2,1)S(1)} %get-tuple-element.77.two_ref, f32[16,128]{1,0:T(8,128)S(1)} %get-tuple-element.78.bias_ref, bf16[6,130,16,128]{3,2,1,0:T(8,128)(2,1)S(1)} %first_layer.1.first, f32[56,128]{1,0:T(8,128)S(1)} %slice_add_fusion.2.token_ref), custom_call_target="tpu_custom_call" | custom-call | flops 4830000128 | bytes 15120000 | tf_op jit(solution)/shard_map/second_layer/pallas_call | solution.py:657
  46.9 0.4 collective-permute-done.12
  47.3 0.7 %finish.1 = (bf16[112,128]{1,0:T(8,128)(2,1)}, f32[1786]{0:T(1024)}, f32[1786]{0:T(1024)}, f32[1786]{0:T(1024)}) custom-call(f32[56,128]{1,0:T(8,128)S(1)} %add.43.dec_ref, f32[112,128]{1,0:T(8,128)S(1)} %get-tuple-element.72.grad_ref.enc_ref, f32[3,112,128]{2,1,0:T(8,128)S(1)} %get-tuple-element.73.state_ref, f32[48,128]{1,0:T(8,128)S(1)} %pad_maximum_fusion.3.own_ref), custom_call_target="tpu_custom_call" | custom-call | flops 1150000000 | bytes 3600000 | tf_op jit(solution)/shard_map/finish/pallas_call | solution.py:527
  (44 shorter events, 0.2 us)
Async XLA Ops:
  0.6 2.3 %copy-start.5 = (f32[1786]{0:T(1024)S(1)}, f32[1786]{0:T(1024)}, u32[]{:S(2)}) copy-start(f32[1786]{0:T(1024)} %param.14) | copy-start | bytes 21436
  0.6 2.3 %copy-start.6 = (f32[1786]{0:T(1024)S(1)}, f32[1786]{0:T(1024)}, u32[]{:S(2)}) copy-start(f32[1786]{0:T(1024)} %param.15) | copy-start | bytes 21436
  0.7 2.3 %copy-start.7 = (f32[1786]{0:T(1024)S(1)}, f32[1786]{0:T(1024)}, u32[]{:S(2)}) copy-start(f32[1786]{0:T(1024)} %param.16) | copy-start | bytes 21436
  0.7 2.3 %copy-start.8 = (f32[1,1,7376]{2,1,0:T(1,128)S(1)}, f32[1,1,7376]{2,1,0:T(1,128)}, u32[]{:S(2)}) copy-start(f32[1,1,7376]{2,1,0:T(1,128)} %param.13) | copy-start | bytes 88516
  0.7 6.4 %copy-start = (bf16[1,1,4,128,128]{4,3,2,1,0:T(8,128)(2,1)S(1)}, bf16[1,1,4,128,128]{4,3,2,1,0:T(8,128)(2,1)}, u32[]{:S(2)}) copy-start(bf16[1,1,4,128,128]{4,3,2,1,0:T(8,128)(2,1)} %param.11) | copy-start | bytes 393220
  0.7 6.4 %copy-start.1 = (bf16[1,16,4,128,128]{4,3,2,1,0:T(8,128)(2,1)S(1)}, bf16[1,16,4,128,128]{4,3,2,1,0:T(8,128)(2,1)}, u32[]{:S(2)}) copy-start(bf16[1,16,4,128,128]{4,3,2,1,0:T(8,128)(2,1)} %param.9) | copy-start | bytes 6291460
  0.7 6.4 %copy-start.2 = (bf16[1,16,4,128,128]{4,3,2,1,0:T(8,128)(2,1)S(1)}, bf16[1,16,4,128,128]{4,3,2,1,0:T(8,128)(2,1)}, u32[]{:S(2)}) copy-start(bf16[1,16,4,128,128]{4,3,2,1,0:T(8,128)(2,1)} %param.10) | copy-start | bytes 6291460
  2.1 13.5 %collective-permute-start.2 = (bf16[144,16,128]{2,1,0:T(8,128)(2,1)S(1)}, bf16[144,16,128]{2,1,0:T(8,128)(2,1)S(1)}, u32[]{:S(2)}, u32[]{:S(2)}) collective-permute-start(bf16[144,16,128]{2,1,0:T(8,128)(2,1)S(1)} %far_edge.1), channel_id=1, source_target_pairs={{1,2},{3,4},{5,6},{7,8},{9,10},{11,12},{13,14},{2,1},{4,3},{6,5},{... | collective-permute-start | bytes 1769480 | tf_op jit(solution)/shard_map/ppermute | solution.py:703
  3.0 11.4 %copy-start.3 = (bf16[27,16,16]{0,2,1:T(8,128)(2,1)S(1)}, bf16[27,16,16]{0,2,1:T(8,128)(2,1)}, u32[]{:S(2)}) copy-start(bf16[27,16,16]{0,2,1:T(8,128)(2,1)} %param.12) | copy-start | bytes 41476
  3.0 10.2 %collective-permute-start = (f32[112,128]{1,0:T(8,128)S(1)}, f32[112,128]{1,0:T(8,128)S(1)}, u32[]{:S(2)}, u32[]{:S(2)}) collective-permute-start(f32[112,128]{1,0:T(8,128)S(1)} %pad_maximum_fusion.1), channel_id=1, source_target_pairs={{0,64},{16,80},{32,96},{48,112},{64,0},{80,16},{96,32},{112,48},{1... | collective-permute-start | bytes 172040 | tf_op jit(solution)/shard_map/ppermute | solution.py:670
  10.6 4.2 %collective-permute-start.3 = (bf16[144,16,128]{2,1,0:T(8,128)(2,1)S(1)}, bf16[144,16,128]{2,1,0:T(8,128)(2,1)S(1)}, u32[]{:S(2)}, u32[]{:S(2)}) collective-permute-start(bf16[144,16,128]{2,1,0:T(8,128)(2,1)S(1)} %get-tuple-element.54), channel_id=1, source_target_pairs={{0,1},{1,0},{2,3},{3,2},{4,5},{5,4},{6,7},{7,6},{8,9},{9,8},{10,11... | collective-permute-start | bytes 1769480 | tf_op jit(solution)/shard_map/ppermute | solution.py:670
  13.3 4.5 %collective-permute-start.1 = (f32[160,128]{1,0:T(8,128)S(1)}, f32[160,128]{1,0:T(8,128)S(1)}, u32[]{:S(2)}, u32[]{:S(2)}) collective-permute-start(f32[160,128]{1,0:T(8,128)S(1)} %get-tuple-element.89), channel_id=1, source_target_pairs={{0,32},{16,48},{32,0},{48,16},{64,96},{80,112},{96,64},{112,80},{1... | collective-permute-start | bytes 245768 | tf_op jit(solution)/shard_map/ppermute | solution.py:670
  17.9 8.5 %collective-permute-start.5 = (f32[112,128]{1,0:T(8,128)S(1)}, f32[112,128]{1,0:T(8,128)S(1)}, u32[]{:S(2)}, u32[]{:S(2)}) collective-permute-start(f32[112,128]{1,0:T(8,128)S(1)} %get-tuple-element.61.token_ref), channel_id=1, source_target_pairs={{0,24},{1,7},{2,26},{3,5},{4,28},{5,3},{6,30},{7,1},{8,16},{9,15},... | collective-permute-start | bytes 172040 | tf_op jit(solution)/shard_map/ppermute | solution.py:678
  22.9 5.7 %collective-permute-start.4 = (f32[112,128]{1,0:T(8,128)S(1)}, f32[112,128]{1,0:T(8,128)S(1)}, u32[]{:S(2)}, u32[]{:S(2)}) collective-permute-start(f32[112,128]{1,0:T(8,128)S(1)} %get-tuple-element.61.token_ref), channel_id=1, source_target_pairs={{0,8},{1,5},{2,10},{3,7},{4,12},{5,1},{6,14},{7,3},{8,0},{9,13},{1... | collective-permute-start | bytes 172040 | tf_op jit(solution)/shard_map/ppermute | solution.py:678
  22.9 5.7 %collective-permute-start.6 = (f32[304,128]{1,0:T(8,128)S(1)}, f32[304,128]{1,0:T(8,128)S(1)}, u32[]{:S(2)}, u32[]{:S(2)}) collective-permute-start(f32[304,128]{1,0:T(8,128)S(1)} %get-tuple-element.62), channel_id=1, source_target_pairs={{0,16},{1,3},{2,18},{3,1},{4,20},{5,7},{6,22},{7,5},{8,24},{9,11},... | collective-permute-start | bytes 466952 | tf_op jit(solution)/shard_map/ppermute | solution.py:678
  28.6 6.6 %collective-permute-start.9 = (f32[112,128]{1,0:T(8,128)S(1)}, f32[112,128]{1,0:T(8,128)S(1)}, u32[]{:S(2)}, u32[]{:S(2)}) collective-permute-start(f32[112,128]{1,0:T(8,128)S(1)} %fusion.token_ref), channel_id=1, source_target_pairs={{0,2},{1,17},{2,0},{3,19},{4,6},{5,21},{6,4},{7,23},{8,10},{9,25},... | collective-permute-start | bytes 172040 | tf_op jit(solution)/shard_map/ppermute | solution.py:678
  28.7 6.5 %collective-permute-start.8 = (f32[112,128]{1,0:T(8,128)S(1)}, f32[112,128]{1,0:T(8,128)S(1)}, u32[]{:S(2)}, u32[]{:S(2)}) collective-permute-start(f32[112,128]{1,0:T(8,128)S(1)} %fusion.token_ref), channel_id=1, source_target_pairs={{0,6},{1,25},{2,4},{3,27},{4,2},{5,29},{6,0},{7,31},{8,14},{9,17},... | collective-permute-start | bytes 172040 | tf_op jit(solution)/shard_map/ppermute | solution.py:678
  30.5 5.7 %collective-permute-start.7 = (f32[112,128]{1,0:T(8,128)S(1)}, f32[112,128]{1,0:T(8,128)S(1)}, u32[]{:S(2)}, u32[]{:S(2)}) collective-permute-start(f32[112,128]{1,0:T(8,128)S(1)} %fusion.token_ref), channel_id=1, source_target_pairs={{0,4},{1,9},{2,6},{3,11},{4,0},{5,13},{6,2},{7,15},{8,12},{9,1},{1... | collective-permute-start | bytes 172040 | tf_op jit(solution)/shard_map/ppermute | solution.py:678
  36.2 1.5 %collective-permute-start.10 = (f32[304,128]{1,0:T(8,128)S(1)}, f32[304,128]{1,0:T(8,128)S(1)}, u32[]{:S(2)}, u32[]{:S(2)}) collective-permute-start(f32[304,128]{1,0:T(8,128)S(1)} %pad_maximum_fusion), channel_id=1, source_target_pairs={{0,1},{1,0},{2,3},{3,2},{4,5},{5,4},{6,7},{7,6},{8,9},{9,8},{10,11... | collective-permute-start | bytes 466952 | tf_op jit(solution)/shard_map/ppermute | solution.py:670
  36.3 2.8 %copy-start.4 = (bf16[8,64,1408]{2,1,0:T(8,128)(2,1)S(1)}, bf16[8,64,1408]{2,1,0:T(8,128)(2,1)}, u32[]{:S(2)}) copy-start(bf16[8,64,1408]{2,1,0:T(8,128)(2,1)} %constant.5.clone.table_ref) | copy-start | bytes 4325380
  37.8 4.1 %collective-permute-start.11 = (f32[56,128]{1,0:T(8,128)S(1)}, f32[56,128]{1,0:T(8,128)S(1)}, u32[]{:S(2)}, u32[]{:S(2)}) collective-permute-start(f32[56,128]{1,0:T(8,128)S(1)} %slice.22.token_ref), channel_id=1, source_target_pairs={{0,32},{16,48},{32,0},{48,16},{64,96},{80,112},{96,64},{112,80},{1... | collective-permute-start | bytes 86024 | tf_op jit(solution)/shard_map/ppermute | solution.py:670
  42.0 5.4 %collective-permute-start.12 = (f32[56,128]{1,0:T(8,128)S(1)}, f32[56,128]{1,0:T(8,128)S(1)}, u32[]{:S(2)}, u32[]{:S(2)}) collective-permute-start(f32[56,128]{1,0:T(8,128)S(1)} %slice_add_fusion.2.token_ref), channel_id=1, source_target_pairs={{0,64},{16,80},{32,96},{48,112},{64,0},{80,16},{96,32},{112,48},{1... | collective-permute-start | bytes 86024 | tf_op jit(solution)/shard_map/ppermute | solution.py:670
